TPU v7x, 256 devices: a whole 4x4x8 slice. The times are simulated.
256 devices in a mesh: ctx: 32 (over z, x), dp: 8 (over y, core).
Axes of the slice: x: 4, y: 4, z: 8, core: 2. Of those that a mesh axis runs over, the one named last changes fastest.
Arguments:
- queries: bfloat16 [8, 16384, 1024], P('dp', 'ctx'), may hold values from -256 to 256
- keys: bfloat16 [8, 16384, 1024], P('dp', 'ctx'), may hold values from -4 to 4
- values: bfloat16 [8, 16384, 1024], P('dp', 'ctx'), may hold values from -6 to 6
- grad_out: bfloat16 [8, 16384, 1024], P('dp', 'ctx'), may hold values from -6 to 6
- out_weight: bfloat16 [1024, 1024], replicated, may hold values from -0.5 to 0.5
Outputs:
- mixed: bfloat16 [8, 16384, 1024], P('dp', 'ctx')
- grad_queries: bfloat16 [8, 16384, 1024], P('dp', 'ctx')
- grad_keys: bfloat16 [8, 16384, 1024], P('dp', 'ctx')
- grad_values: bfloat16 [8, 16384, 1024], P('dp', 'ctx')
- grad_weight: float32 [1024, 1024], P('ctx')
All inputs are finite; a program needn't handle non-finite values.
Results may differ from a plain program's by a relative error of at most 0.025.
Values may be sent and summed in bfloat16 or wider, within the bound.
No kernel may reach another device: no remote copies, remote signals or barrier semaphores. Data moves between devices by JAX's collectives and lax.ppermute only.
A program may use at most 128 MiB of HBM per device.

v0:
```python
import math

import jax
import jax.numpy as jnp
from jax import lax
from jax.sharding import PartitionSpec as P

HEAD = 128
BLOCK = 256
POOL = 16
GROUP = 8


def extended(x, sides, width):
    for axis, dim in sides:
        size, length = (lax.axis_size(axis), x.shape[dim])
        up = [(i, (i + 1) % size) for i in range(size - 1)]
        down = [(j, i) for i, j in up]
        last = lax.slice_in_dim(x, length - width, length, axis=dim)
        leading = lax.slice_in_dim(x, 0, width, axis=dim)
        before = lax.ppermute(last, axis, up)
        after = lax.ppermute(leading, axis, down)
        x = jnp.concatenate([before, x, after], axis=dim)
    return x


def from_behind(value, axis, steps):
    count = lax.axis_size(axis)
    leading, last = (max(0, -steps), min(count, count - steps))
    return lax.ppermute(value, axis, [(source, source + steps) for source in range(leading, last)])


def pooled(rows):
    shape = rows.shape
    grouped = rows.astype(jnp.float32).reshape(shape[:-2] + (shape[-2] // POOL, POOL, shape[-1]))
    return (jnp.sum(grouped, axis=-2) * (1.0 / math.sqrt(POOL))).astype(jnp.bfloat16)


def allowed_keys(device, tokens, devices):
    seq_len = tokens * devices
    blocks = seq_len // BLOCK
    group_rows = GROUP * tokens // POOL
    group = device // GROUP
    qblock = ((device * tokens + jnp.arange(tokens, dtype=jnp.int32)) // BLOCK)[:, None]
    fine_tok = device * tokens - BLOCK + jnp.arange(tokens + 2 * BLOCK, dtype=jnp.int32)
    fine_block = fine_tok // BLOCK
    fine_ok = (
        (fine_tok >= 0)[None, :]
        & (fine_tok < seq_len)[None, :]
        & (jnp.abs(fine_block[None, :] - qblock) <= 1)
    )
    one_index = group * group_rows + jnp.arange(group_rows, dtype=jnp.int32)
    one_block = one_index * POOL // BLOCK
    one_ok = jnp.abs(one_block[None, :] - qblock) > 1
    two_block = jnp.arange(blocks, dtype=jnp.int32)
    two_ok = (two_block // (GROUP * tokens // BLOCK) != group)[None, :] & (
        jnp.abs(two_block[None, :] - qblock) > 1
    )
    return jnp.concatenate([fine_ok, one_ok, two_ok], axis=1)


def heads_pass(query_rows, key_rows, value_rows, grad_rows, allowed):
    tokens = query_rows.shape[0]
    width = query_rows.shape[1]
    count = key_rows.shape[0]
    factor = 1.0 / math.sqrt(HEAD)

    def one_head(head, carry):
        attn, grad_q, grad_k, grad_v = carry
        begin = head * HEAD
        qhead = lax.dynamic_slice_in_dim(query_rows, begin, HEAD, 1)
        khead = lax.dynamic_slice_in_dim(key_rows, begin, HEAD, 1)
        vhead = lax.dynamic_slice_in_dim(value_rows, begin, HEAD, 1)
        ghead = lax.dynamic_slice_in_dim(grad_rows, begin, HEAD, 1)
        scores = (
            lax.dot_general(
                qhead, khead, (((1,), (1,)), ((), ())), preferred_element_type=jnp.float32
            )
            * factor
        )
        scores = jnp.where(allowed, scores, -jnp.inf)
        top = jnp.max(scores, axis=1, keepdims=True)
        weights = jnp.where(allowed, jnp.exp(scores - top), 0.0)
        probs = weights / jnp.sum(weights, axis=1, keepdims=True)
        probs_low = probs.astype(jnp.bfloat16)
        ohead = jnp.dot(probs_low, vhead, preferred_element_type=jnp.float32).astype(jnp.bfloat16)
        dprob = lax.dot_general(
            ghead, vhead, (((1,), (1,)), ((), ())), preferred_element_type=jnp.float32
        )
        delta = jnp.sum(
            ghead.astype(jnp.float32) * ohead.astype(jnp.float32), axis=1, keepdims=True
        )
        dscore = (probs * (dprob - delta)).astype(jnp.bfloat16)
        dqhead = (jnp.dot(dscore, khead, preferred_element_type=jnp.float32) * factor).astype(
            jnp.bfloat16
        )
        dkhead = (
            lax.dot_general(
                dscore, qhead, (((0,), (0,)), ((), ())), preferred_element_type=jnp.float32
            )
            * factor
        )
        dvhead = lax.dot_general(
            probs_low, ghead, (((0,), (0,)), ((), ())), preferred_element_type=jnp.float32
        )
        attn = lax.dynamic_update_slice_in_dim(attn, ohead, begin, 1)
        grad_q = lax.dynamic_update_slice_in_dim(grad_q, dqhead, begin, 1)
        grad_k = lax.dynamic_update_slice_in_dim(grad_k, dkhead, begin, 1)
        grad_v = lax.dynamic_update_slice_in_dim(grad_v, dvhead, begin, 1)
        return (attn, grad_q, grad_k, grad_v)

    start_state = (
        jnp.zeros((tokens, width), jnp.bfloat16),
        jnp.zeros((tokens, width), jnp.bfloat16),
        jnp.zeros((count, width), jnp.float32),
        jnp.zeros((count, width), jnp.float32),
    )
    return lax.fori_loop(0, width // HEAD, one_head, start_state)


def on_device(queries, keys, values, grad_out, out_weight):
    query_rows = queries[0]
    upstream = grad_out[0]
    tokens = query_rows.shape[0]
    devices = lax.axis_size("ctx")
    device = lax.axis_index("ctx")
    group_rows = GROUP * tokens // POOL
    scale = 1.0 / math.sqrt(POOL)
    stacked = jnp.stack([keys[0], values[0]])
    rimmed = extended(stacked, (("ctx", 1),), BLOCK)
    local_one = pooled(stacked)
    every_one = lax.all_gather(local_one, "ctx", axis=1, tiled=True)
    group_one = lax.dynamic_slice_in_dim(every_one, device // GROUP * group_rows, group_rows, 1)
    every_two = pooled(every_one)
    candidates = jnp.concatenate([rimmed, group_one, every_two], 1)
    allowed = allowed_keys(device, tokens, devices)
    backward = lax.dot_general(
        upstream, out_weight, (((1,), (1,)), ((), ())), preferred_element_type=jnp.float32
    ).astype(jnp.bfloat16)
    attn, grad_q, grad_k, grad_v = heads_pass(
        query_rows, candidates[0], candidates[1], backward, allowed
    )
    mixed = jnp.dot(attn, out_weight, preferred_element_type=jnp.float32).astype(jnp.bfloat16)
    partial_rows = lax.psum_scatter(
        lax.dot_general(
            attn, upstream, (((0,), (0,)), ((), ())), preferred_element_type=jnp.float32
        ).astype(jnp.bfloat16),
        "ctx",
        scatter_dimension=0,
        tiled=True,
    )
    grad_weight = lax.psum(partial_rows, "dp").astype(jnp.float32)
    grad_pair = jnp.stack([grad_k, grad_v])
    span = tokens + 2 * BLOCK
    own = grad_pair[:, BLOCK : BLOCK + tokens]
    from_after = from_behind(grad_pair[:, :BLOCK].astype(jnp.bfloat16), "ctx", -1).astype(
        jnp.float32
    )
    from_before = from_behind(
        grad_pair[:, tokens + BLOCK : span].astype(jnp.bfloat16), "ctx", 1
    ).astype(jnp.float32)
    own = own.at[:, tokens - BLOCK :].add(from_after)
    own = own.at[:, :BLOCK].add(from_before)
    grad_one = grad_pair[:, span : span + group_rows]
    grad_two = grad_pair[:, span + group_rows :]
    spread_two = jnp.repeat(grad_two * scale, POOL, axis=1)
    begin = device // GROUP * group_rows
    placed = lax.dynamic_slice_in_dim(spread_two, begin, group_rows, 1) + grad_one
    full_one = lax.dynamic_update_slice_in_dim(spread_two, placed, begin, 1)
    mine_one = lax.psum_scatter(full_one, "ctx", scatter_dimension=1, tiled=True)
    total = own + jnp.repeat(mine_one * scale, POOL, axis=1)
    grad_keys = total[0].astype(jnp.bfloat16)
    grad_values = total[1].astype(jnp.bfloat16)
    return (mixed[None], grad_q[None], grad_keys[None], grad_values[None], grad_weight)


def solution(mesh):
    placed = (
        P("dp", "ctx", None),
        P("dp", "ctx", None),
        P("dp", "ctx", None),
        P("dp", "ctx", None),
        P(),
    )
    return jax.shard_map(
        on_device,
        mesh=mesh,
        in_specs=placed,
        out_specs=(
            P("dp", "ctx", None),
            P("dp", "ctx", None),
            P("dp", "ctx", None),
            P("dp", "ctx", None),
            P("ctx", None),
        ),
        check_vma=False,
    )
```

profile of v0, /device:TPU:73, one launch (start us, length us, event | category | flops | bytes accessed | tf_op | source)
XLA Modules:
  0.0 768.4 jit_solution(13276324979005013194)
XLA Ops:
  7.2 2.6 convert_reduce_fusion.1
  13.4 3.1 collective-permute-start
  16.5 4.3 collective-permute-start.1
  22.2 3.5 convolution_convert_fusion.3
  25.7 19.2 %collective-permute-done = bf16[2,256,1024]{2,1,0:T(8,128)(2,1)} collective-permute-done((bf16[2,256,1024]{2,1,0:T(8,128)(2,1)}, bf16[2,256,1024]{2,1,0:T(8,128)(2,1)}, u32[]{:S(2)}, u32[]{:S(2)}) %collective-permute-start) | collective-permute-done | bytes 1048608 | tf_op jit(solution)/shard_map/ppermute | solution.py:21
  44.9 2.3 constant_dynamic-update-slice_fusion.6
  49.3 2.3 constant_dynamic-update-slice_fusion.3
  51.6 40.3 %all-gather.2.cloned.1.call-done = bf16[2,1024,1024]{2,1,0:T(8,128)(2,1)} async-done(((bf16[2,32,1024]{2,1,0:T(8,128)(2,1)}), bf16[2,1024,1024]{2,1,0:T(8,128)(2,1)}) %all-gather.2.cloned.1.call-update) | async-done | bytes 4194320 | tf_op jit(solution)/shard_map/all_gather | solution.py:132
  91.9 4.3 convert_reduce_fusion
  96.1 2.3 dynamic-slice_dynamic-update-slice_fusion
  99.2 5.6 slice_bitcast_fusion
  104.8 3.2 broadcast.238
  108.0 3.1 broadcast.238.clone
  113.2 130.4 %while.21 = (s32[]{:T(128)}, bf16[512,1024]{0,1:T(8,128)(2,1)}, bf16[512,1024]{1,0:T(8,128)(2,1)}, f32[1344,1024]{1,0:T(8,128)}, f32[1344,1024]{1,0:T(8,128)}, /...) while((s32[]{:T(128)}, bf16[512,1024]{0,1:T(8,128)(2,1)}, ...), condition=%wide.region_6.7_spmd, body=%wide.region_2.6_spmd.sunk | while | flops 1071356416 | bytes 36827344 | solution.py:118
  115.5 2.8 convolution_dynamic-update-slice_fusion.2
  118.3 2.5 constant_dynamic-update-slice_fusion.8
  122.0 2.9 fusion.80
  124.9 2.3 fusion.82
  127.2 2.2 fusion.81
  131.8 2.8 convolution_dynamic-update-slice_fusion.2
  134.7 2.5 constant_dynamic-update-slice_fusion.8
  138.3 2.9 fusion.80
  141.2 2.3 fusion.82
  143.5 2.2 fusion.81
  148.1 2.8 convolution_dynamic-update-slice_fusion.2
  151.0 2.5 constant_dynamic-update-slice_fusion.8
  154.6 2.9 fusion.80
  157.5 2.3 fusion.82
  159.8 2.2 fusion.81
  164.4 2.8 convolution_dynamic-update-slice_fusion.2
  167.3 2.5 constant_dynamic-update-slice_fusion.8
  170.9 2.9 fusion.80
  173.8 2.3 fusion.82
  180.8 2.8 convolution_dynamic-update-slice_fusion.2
  183.6 2.5 constant_dynamic-update-slice_fusion.8
  187.2 2.9 fusion.80
  190.2 2.3 fusion.82
  197.1 2.8 convolution_dynamic-update-slice_fusion.2
  199.9 2.5 constant_dynamic-update-slice_fusion.8
  203.5 2.9 fusion.80
  206.5 2.3 fusion.82
  208.8 2.2 fusion.81
  213.4 2.8 convolution_dynamic-update-slice_fusion.2
  216.2 2.5 constant_dynamic-update-slice_fusion.8
  219.8 2.9 fusion.80
  222.7 2.3 fusion.82
  225.1 2.2 fusion.81
  229.7 2.8 convolution_dynamic-update-slice_fusion.2
  232.5 2.5 constant_dynamic-update-slice_fusion.8
  236.1 2.9 fusion.80
  239.1 2.3 fusion.82
  243.6 4.1 convolution_convert_fusion.1
  248.0 7.6 fusion.23
  255.6 3.0 fusion.52
  261.8 4.2 fusion.24
  266.0 193.7 %reduce-scatter.5.cloned.1.call-done = bf16[32,1024]{1,0:T(8,128)(2,1)} async-done(((bf16[1024,1024]{1,0:T(8,128)(2,1)}), bf16[32,1024]{1,0:T(8,128)(2,1)}) %reduce-scatter.5.cloned.1.call-update) | async-done | bytes 65552 | tf_op jit(solution)/shard_map/reduce_scatter | solution.py:144
  459.7 4.3 broadcast_in_dim.47
  464.0 6.3 fusion.31
  472.6 2.2 fusion.34
  474.8 18.6 %collective-permute-done.3 = bf16[2,256,1024]{2,1,0:T(8,128)(2,1)S(1)} collective-permute-done((bf16[2,256,1024]{2,1,0:T(8,128)(2,1)}, bf16[2,256,1024]{2,1,0:T(8,128)(2,1)S(1)}, u32[]{:S(2)}, u32[]{:S(2)}) %collective-permute-start.3) | collective-permute-done | bytes 1048608 | tf_op jit(solution)/shard_map/ppermute | solution.py:30
  493.4 3.4 fusion.32
  496.8 28.9 %all-reduce.2.cloned.1.call-done = bf16[32,1024]{1,0:T(8,128)(2,1)} async-done(((bf16[32,1024]{1,0:T(8,128)(2,1)}), bf16[32,1024]{1,0:T(8,128)(2,1)}) %all-reduce.2.cloned.1.call-update) | async-done | bytes 65552 | tf_op jit(solution)/shard_map/psum | solution.py:152
  527.2 229.3 %reduce-scatter.3.cloned.1.call-done = f32[2,32,1024]{2,1,0:T(8,128)} async-done(((f32[2,1024,1024]{2,1,0:T(8,128)}), f32[2,32,1024]{2,1,0:T(8,128)}) %reduce-scatter.3.cloned.1.call-update) | async-done | bytes 262160 | tf_op jit(solution)/shard_map/reduce_scatter | solution.py:170
  757.5 2.9 fusion.25
  (110 shorter events, 53.7 us)
Async XLA Ops:
  7.2 15.1 %copy-start = (bf16[1024,1024]{1,0:T(8,128)(2,1)S(1)}, bf16[1024,1024]{1,0:T(8,128)(2,1)}, u32[]{:S(2)}) copy-start(bf16[1024,1024]{1,0:T(8,128)(2,1)} %param.15) | copy-start | bytes 6291460
  7.2 3.4 copy-start.2
  7.2 84.7 %all-gather.2.cloned.1.call-start = ((), (), s32[]{:S(2)}) async-start(), calls=%async_computation.2 | async-start | bytes 4325376 | tf_op jit(solution)/shard_map/all_gather | solution.py:132
  10.6 449.1 %reduce-scatter.5.cloned.1.call-start = ((), (), s32[]{:S(2)}) async-start(), calls=%async_computation.4 | async-start | bytes 2162688 | tf_op jit(solution)/shard_map/reduce_scatter | solution.py:144
  10.6 1.2 copy-start.4
  13.4 31.5 %collective-permute-start = (bf16[2,256,1024]{2,1,0:T(8,128)(2,1)}, bf16[2,256,1024]{2,1,0:T(8,128)(2,1)}, u32[]{:S(2)}, u32[]{:S(2)}) collective-permute-start(bf16[2,256,1024]{2,1,0:T(8,128)(2,1)} %get-tuple-element.248), channel_id=1, source_target_pairs={{0,8},{8,16},{16,24},{24,32},{32,40},{40,48},{48,56},{56,64},{64,7... | collective-permute-start | bytes 3145736 | tf_op jit(solution)/shard_map/ppermute | solution.py:21
  16.5 32.8 %collective-permute-start.1 = (bf16[2,256,1024]{2,1,0:T(8,128)(2,1)}, bf16[2,256,1024]{2,1,0:T(8,128)(2,1)}, u32[]{:S(2)}, u32[]{:S(2)}) collective-permute-start(bf16[2,256,1024]{2,1,0:T(8,128)(2,1)} %get-tuple-element.247), channel_id=1, source_target_pairs={{8,0},{16,8},{24,16},{32,24},{40,32},{48,40},{56,48},{64,56},{72,6... | collective-permute-start | bytes 3145736 | tf_op jit(solution)/shard_map/ppermute | solution.py:22
  25.7 21.5 %copy-start.3 = (bf16[1,512,1024]{2,1,0:T(8,128)(2,1)S(1)}, bf16[1,512,1024]{2,1,0:T(8,128)(2,1)}, u32[]{:S(2)}) copy-start(bf16[1,512,1024]{2,1,0:T(8,128)(2,1)} %param.12) | copy-start | bytes 3145732
  25.7 22.5 %copy-start.5 = (bf16[1,512,1024]{2,1,0:T(8,128)(2,1)S(1)}, bf16[1,512,1024]{2,1,0:T(8,128)(2,1)}, u32[]{:S(2)}) copy-start(bf16[1,512,1024]{2,1,0:T(8,128)(2,1)} %param.13) | copy-start | bytes 3145732
  114.8 3.5 copy-start.1
  131.1 3.5 copy-start.1
  147.4 3.5 copy-start.1
  163.7 3.5 copy-start.1
  180.1 3.5 copy-start.1
  196.4 3.5 copy-start.1
  212.7 3.5 copy-start.1
  229.0 3.5 copy-start.1
  247.7 278.0 %all-reduce.2.cloned.1.call-start = ((), (), s32[]{:S(2)}) async-start(), calls=%async_computation.5 | async-start | bytes 131072 | tf_op jit(solution)/shard_map/psum | solution.py:152
  248.0 12.8 %slice-start = ((s8[5505024]{0:T(1024)(128)(4,1)}), s8[4194304]{0:T(1024)(128)(4,1)S(1)}, s32[]{:S(2)}) async-start(s8[5505024]{0:T(1024)(128)(4,1)} %bitcast.37), calls=%async_computation.6 | async-start | bytes 8388608
  248.0 12.8 %slice-start.1 = ((s8[5505024]{0:T(1024)(128)(4,1)}), s8[1310720]{0:T(1024)(128)(4,1)S(1)}, s32[]{:S(2)}) async-start(s8[5505024]{0:T(1024)(128)(4,1)} %bitcast.37), calls=%async_computation.7 | async-start | bytes 2621440
  258.6 201.1 %collective-permute-start.2 = (bf16[2,256,1024]{2,1,0:T(8,128)(2,1)}, bf16[2,256,1024]{2,1,0:T(8,128)(2,1)}, u32[]{:S(2)}, u32[]{:S(2)}) collective-permute-start(bf16[2,256,1024]{2,1,0:T(8,128)(2,1)} %get-tuple-element.242), channel_id=1, source_target_pairs={{8,0},{16,8},{24,16},{32,24},{40,32},{48,40},{56,48},{64,56},{72,6... | collective-permute-start | bytes 3145736 | tf_op jit(solution)/shard_map/ppermute | solution.py:30
  459.7 296.8 %reduce-scatter.3.cloned.1.call-start = ((), (), s32[]{:S(2)}) async-start(), calls=%async_computation.3 | async-start | bytes 8650752 | tf_op jit(solution)/shard_map/reduce_scatter | solution.py:170
  470.3 2.3 copy-start.6
  470.4 23.0 %collective-permute-start.3 = (bf16[2,256,1024]{2,1,0:T(8,128)(2,1)}, bf16[2,256,1024]{2,1,0:T(8,128)(2,1)S(1)}, u32[]{:S(2)}, u32[]{:S(2)}) collective-permute-start(bf16[2,256,1024]{2,1,0:T(8,128)(2,1)} %get-tuple-element.241), channel_id=1, source_target_pairs={{0,8},{8,16},{16,24},{24,32},{32,40},{40,48},{48,56},{56,64},{64,7... | collective-permute-start | bytes 3145736 | tf_op jit(solution)/shard_map/ppermute | solution.py:30
Sparse Core Ops, SparseCore 0:
  11.2 80.6 all-gather.1
  247.9 211.7 reduce-scatter.4
  462.1 63.5 all-reduce.1
  529.6 226.9 reduce-scatter.2
where the time goes:
time: 776 us; the launch traced here: 768 us
  waiting for transfers between devices  530 us (68%)
  matrix products  126 us (16%)
  other arithmetic  43.5 us (6%)
  local copies, waits for them, and re-layouts  42.8 us (6%)
  between operations  14 us (2%)
  starting transfers between devices  12 us (2%)
    reduce_scatter x1, waiting for transfers between devices, on_device(): lax.psum_scatter(full_one, 'ctx', scatter_dimension=1, tiled=True)  229 us
    reduce_scatter x1, waiting for transfers between devices, on_device(): lax.psum_scatter(lax.dot_general(attn, upstream, (((0,), (0,)), ((), ()))...  194 us
    all_gather x1, waiting for transfers between devices, on_device(): every_one = lax.all_gather(local_one, 'ctx', axis=1, tiled=True)  40.3 us
    psum x1, waiting for transfers between devices, on_device(): grad_weight = lax.psum(partial_rows, 'dp').astype(jnp.float32)  28.9 us
    dot_general x8, matrix products, one_head(): lax.dot_general(ghead, vhead, (((1,), (1,)), ((), ())), preferred_element...  23.4 us
    dot_general x8, matrix products, one_head(): lax.dot_general(probs_low, ghead, (((0,), (0,)), ((), ())), preferred_ele...  22.6 us
    dot_general x8, matrix products, one_head(): jnp.dot(probs_low, vhead, preferred_element_type=jnp.float32)  20.3 us
    ppermute x1, waiting for transfers between devices, extended(): before = lax.ppermute(last, axis, up)  19.2 us
  transfers between devices with their start and end apart: 8, of which 6 were waited for; matrix products, arithmetic and copies ran while one was open for 6% of the time, Pallas kernels for 0%

commit v1 on v0

v1 whole, which is shorter than its diff:
```python
import functools
import math

import jax
import jax.numpy as jnp
from jax import lax
from jax.experimental import pallas as pl
from jax.experimental.pallas import tpu as pltpu
from jax.sharding import PartitionSpec as P

HEAD = 128
BLOCK = 256
POOL = 16
GROUP = 8
SCALE = 1.0 / math.sqrt(POOL)
FACTOR = 1.0 / math.sqrt(HEAD)
LOG2E = math.log2(math.e)
MASKED = -1e30
F32 = jnp.float32
BF16 = jnp.bfloat16


def dot(a, b, da, db):
    return lax.dot_general(a, b, (((da,), (db,)), ((), ())), preferred_element_type=F32)


def parts_of(side, mem, which):
    own, before, after, one, two = mem
    near = (before, after)[side]
    ones = one[:, which].reshape(-1, HEAD)
    twos = two[:, which].reshape(-1, HEAD)
    return own[...], near[which], ones, twos


def scores_of(side, q, keys, edge_ref, bias_ref):
    own, near, ones, twos = keys
    n1 = ones.shape[0]
    s_own = dot(own, q, 1, 1) * (FACTOR * LOG2E)
    s_near = dot(near, q, 1, 1) * (FACTOR * LOG2E) + edge_ref[side]
    s_one = dot(ones, q, 1, 1) * (FACTOR * LOG2E) + bias_ref[side, :n1]
    s_two = dot(twos, q, 1, 1) * (FACTOR * LOG2E) + bias_ref[side, n1:]
    return s_own, s_near, s_one, s_two


def forward_kernel(edge_ref, bias_ref, q_ref, k_ref, v_ref, g_ref, before, after, one, two, attn_ref, stat_ref):
    for side in range(2):
        rows = pl.ds(side * BLOCK, BLOCK)
        q = q_ref[rows, :]
        keys = parts_of(side, (k_ref, before, after, one, two), 0)
        values = parts_of(side, (v_ref, before, after, one, two), 1)
        scores = scores_of(side, q, keys, edge_ref, bias_ref)
        top = functools.reduce(jnp.maximum, [jnp.max(s, axis=0, keepdims=True) for s in scores])
        total = 0.0
        out = 0.0
        for s, v in zip(scores, values):
            p = jnp.exp2(s - top)
            total = total + jnp.sum(p, axis=0, keepdims=True)
            out = out + dot(v, p.astype(BF16), 0, 0)
        out = jnp.transpose(out / total).astype(BF16)
        attn_ref[rows, :] = out
        stat_ref[0, 0:1, rows] = top + jnp.log2(total)
        g = g_ref[rows, :].astype(F32)
        stat_ref[0, 1:2, rows] = jnp.sum(jnp.transpose(g * out.astype(F32)), axis=0, keepdims=True)


def backward_kernel(
    edge_ref, bias_ref, q_ref, k_ref, v_ref, g_ref, before, after, one, two, stat_ref,
    dq_ref, down_ref, dbefore_ref, dafter_ref, done_ref, dtwo_ref,
):
    n1 = one.shape[0] * one.shape[2]
    for side in range(2):
        rows = pl.ds(side * BLOCK, BLOCK)
        q = q_ref[rows, :]
        g = g_ref[rows, :]
        keys = parts_of(side, (k_ref, before, after, one, two), 0)
        values = parts_of(side, (v_ref, before, after, one, two), 1)
        scores = scores_of(side, q, keys, edge_ref, bias_ref)
        lse = stat_ref[0, 0:1, rows]
        delta = stat_ref[0, 1:2, rows]
        dq = 0.0
        grads = []
        for s, k, v in zip(scores, keys, values):
            p = jnp.exp2(s - lse)
            dp = dot(v, g, 1, 1)
            ds = (p * (dp - delta)).astype(BF16)
            dq = dq + dot(k, ds, 0, 0)
            grads.append((dot(ds, q, 1, 0) * FACTOR, dot(p.astype(BF16), g, 1, 0)))
        dq_ref[rows, :] = jnp.transpose(dq * FACTOR).astype(BF16)
        near_ref = (dbefore_ref, dafter_ref)[side]
        for which in range(2):
            d_own, d_near, d_one, d_two = (pair[which] for pair in grads)
            near_ref[which] = d_near.astype(BF16)
            if side == 0:
                down_ref[which] = d_own
                done_ref[which] = d_one
                dtwo_ref[which] = d_two
            else:
                down_ref[which] += d_own
                done_ref[which] += d_one
                dtwo_ref[which] += d_two


def head_specs(tokens, one, two):
    col = lambda *lead: pl.BlockSpec(lead + (HEAD,), lambda h: (0,) * len(lead) + (h,))
    rows = col(tokens)
    near = col(2, BLOCK)
    return rows, near, col(one.shape[0], 2, one.shape[2]), col(two.shape[0], 2, two.shape[2]), col


PARAMS = pltpu.CompilerParams(vmem_limit_bytes=40 * 1024 * 1024)


def forward_heads(edge, bias, q, k, v, g, before, after, one, two):
    tokens, width = q.shape
    heads = width // HEAD
    rows, near, ones, twos, col = head_specs(tokens, one, two)
    stat = pl.BlockSpec((1, 2, tokens), lambda h: (h, 0, 0))
    return pl.pallas_call(
        forward_kernel,
        grid=(heads,),
        in_specs=[
            pl.BlockSpec(memory_space=pltpu.SMEM),
            pl.BlockSpec(bias.shape, lambda h: (0, 0, 0)),
            rows, rows, rows, rows, near, near, ones, twos,
        ],
        out_specs=[rows, stat],
        out_shape=[
            jax.ShapeDtypeStruct((tokens, width), BF16),
            jax.ShapeDtypeStruct((heads, 2, tokens), F32),
        ],
        compiler_params=PARAMS,
        name="forward_heads",
    )(edge, bias, q, k, v, g, before, after, one, two)


def backward_heads(edge, bias, q, k, v, g, before, after, one, two, stats):
    tokens, width = q.shape
    heads = width // HEAD
    rows, near, ones, twos, col = head_specs(tokens, one, two)
    stat = pl.BlockSpec((1, 2, tokens), lambda h: (h, 0, 0))
    n1, n2 = one.shape[0] * one.shape[2], two.shape[0] * two.shape[2]
    return pl.pallas_call(
        backward_kernel,
        grid=(heads,),
        in_specs=[
            pl.BlockSpec(memory_space=pltpu.SMEM),
            pl.BlockSpec(bias.shape, lambda h: (0, 0, 0)),
            rows, rows, rows, rows, near, near, ones, twos, stat,
        ],
        out_specs=[rows, col(2, tokens), near, near, col(2, n1), col(2, n2)],
        out_shape=[
            jax.ShapeDtypeStruct((tokens, width), BF16),
            jax.ShapeDtypeStruct((2, tokens, width), F32),
            jax.ShapeDtypeStruct((2, BLOCK, width), BF16),
            jax.ShapeDtypeStruct((2, BLOCK, width), BF16),
            jax.ShapeDtypeStruct((2, n1, width), F32),
            jax.ShapeDtypeStruct((2, n2, width), F32),
        ],
        compiler_params=PARAMS,
        name="backward_heads",
    )(edge, bias, q, k, v, g, before, after, one, two, stats)


def exchange(x, axis, groups=None):
    return lax.all_to_all(x, axis, 0, 0, axis_index_groups=groups, tiled=True)


def pooled(rows):
    shape = rows.shape
    grouped = rows.astype(F32).reshape(shape[:-2] + (shape[-2] // POOL, POOL, shape[-1]))
    return (jnp.sum(grouped, axis=-2) * SCALE).astype(BF16)


def masks(device, devices, tokens):
    group = device // GROUP
    per_group = GROUP * tokens // BLOCK
    block = device * (tokens // BLOCK) + jnp.arange(2, dtype=jnp.int32)[:, None]
    one = group * per_group + jnp.arange(GROUP * tokens // POOL, dtype=jnp.int32) * POOL // BLOCK
    two = jnp.arange(devices * tokens // BLOCK, dtype=jnp.int32)
    one_ok = jnp.abs(one[None] - block) > 1
    two_ok = (jnp.abs(two[None] - block) > 1) & (two // per_group != group)[None]
    ok = jnp.concatenate([one_ok, two_ok], axis=1)
    bias = jnp.where(ok, 0.0, MASKED).astype(F32)
    bias = jnp.broadcast_to(bias[:, :, None], bias.shape + (BLOCK,))
    edge = jnp.stack([device == 0, device == devices - 1]).astype(F32) * MASKED
    return edge, bias


def on_device(queries, keys, values, grad_out, out_weight):
    q, k, v, upstream = queries[0], keys[0], values[0], grad_out[0]
    tokens, width = q.shape
    devices = lax.axis_size("ctx")
    dp = lax.axis_size("dp")
    device = lax.axis_index("ctx")
    groups = devices // GROUP
    near = [[g * GROUP + i for i in range(GROUP)] for g in range(groups)]
    far = [[g * GROUP + i for g in range(groups)] for i in range(GROUP)]
    up = [(i, i + 1) for i in range(devices - 1)]
    down = [(i + 1, i) for i in range(devices - 1)]
    rows_one = tokens // POOL
    rows_two = tokens // BLOCK

    before = lax.ppermute(jnp.stack([k[tokens - BLOCK :], v[tokens - BLOCK :]]), "ctx", up)
    after = lax.ppermute(jnp.stack([k[:BLOCK], v[:BLOCK]]), "ctx", down)
    local_one = jnp.stack([pooled(k), pooled(v)])
    one = exchange(jnp.broadcast_to(local_one[None], (GROUP,) + local_one.shape), "ctx", near)
    group_two = jnp.swapaxes(pooled(one), 0, 1).reshape(2, GROUP * rows_two, width)
    two = exchange(jnp.broadcast_to(group_two[None], (groups,) + group_two.shape), "ctx", far)

    edge, bias = masks(device, devices, tokens)
    g = dot(upstream, out_weight, 1, 1).astype(BF16)
    attn, stats = forward_heads(edge, bias, q, k, v, g, before, after, one, two)

    partial = dot(attn, upstream, 0, 0).astype(BF16)
    share = width // (devices * dp)
    partial = partial.reshape(groups, GROUP, dp, share, width).transpose(2, 0, 1, 3, 4)
    summed = lax.psum_scatter(partial, "dp", scatter_dimension=0, tiled=False)
    mixed = jnp.dot(attn, out_weight, preferred_element_type=F32).astype(BF16)

    dq, d_own, d_before, d_after, d_one, d_two = backward_heads(
        edge, bias, q, k, v, g, before, after, one, two, stats
    )
    from_after = lax.ppermute(d_before, "ctx", down)
    from_before = lax.ppermute(d_after, "ctx", up)

    d_two = d_two.astype(BF16).reshape(2, groups, GROUP * rows_two, width).transpose(1, 0, 2, 3)
    weight_far = summed.astype(BF16).reshape(groups, GROUP * share, width)
    packed = jnp.concatenate([d_two.reshape(groups, -1, width), weight_far], axis=1)
    packed = jnp.sum(exchange(packed, "ctx", far).astype(F32), axis=0)
    n2 = 2 * GROUP * rows_two
    mine_two = packed[:n2].reshape(2, GROUP * rows_two, 1, width)
    d_one = d_one.reshape(2, GROUP * rows_two, POOL, width) + mine_two * SCALE
    d_one = d_one.astype(BF16).reshape(2, GROUP, rows_one, width).transpose(1, 0, 2, 3)
    weight_near = packed[n2:].astype(BF16).reshape(GROUP, share, width)
    packed = jnp.concatenate([d_one.reshape(GROUP, -1, width), weight_near], axis=1)
    packed = jnp.sum(exchange(packed, "ctx", near).astype(F32), axis=0)
    mine_one = packed[: 2 * rows_one].reshape(2, rows_one, 1, width)
    mine_weight = packed[2 * rows_one :].astype(BF16)
    grad_weight = exchange(jnp.broadcast_to(mine_weight[None], (dp, share, width)), "dp")
    grad_weight = grad_weight.reshape(dp * share, width).astype(F32)

    total = d_own.reshape(2, rows_one, POOL, width) + mine_one * SCALE
    total = total.reshape(2, tokens, width)
    head = total[:, :BLOCK] + from_before.astype(F32)
    tail = total[:, tokens - BLOCK :] + from_after.astype(F32)
    total = jnp.concatenate([head, tail], axis=1).astype(BF16)
    return mixed[None], dq[None], total[0][None], total[1][None], grad_weight


def solution(mesh):
    rows = P("dp", "ctx", None)
    return jax.shard_map(
        on_device,
        mesh=mesh,
        in_specs=(rows, rows, rows, rows, P()),
        out_specs=(rows, rows, rows, rows, P("ctx", None)),
        check_vma=False,
    )
```

time: 776 us -> 229 us (0.30)
  waiting for transfers between devices: 530 us -> 62.2 us
  matrix products: 126 us -> 9.53 us
  Pallas kernels: 0 us -> 36.4 us
  other arithmetic: 43.5 us -> 17.7 us
  blocking collectives: 0 us -> 22.3 us
  starting transfers between devices: 12 us -> 33 us
  local copies, waits for them, and re-layouts: 42.8 us -> 32 us
    reduce_scatter x2 -> x1, waiting for transfers between devices: 423 us -> 6.07 us  [on_device(): summed = lax.psum_scatter(partial, 'dp', scatter_dimension=0, tiled=False)]
    dot_general x51 -> x3, matrix products: 126 us -> 9.53 us  [the longest x2 6.08 us: dot(): lax.dot_general(a, b, (((da,), (db,)), ((), ())), preferred_element_type=...]
    all_to_all x0 -> x4, waiting for transfers between devices: none -> 56.1 us  [exchange(): return lax.all_to_all(x, axis, 0, 0, axis_index_groups=groups, tiled=True)]
    all_gather x1 -> x0, waiting for transfers between devices: 40.3 us -> none  [on_device(): every_one = lax.all_gather(local_one, 'ctx', axis=1, tiled=True)]
    ppermute x4, waiting for transfers between devices: 37.8 us -> 0.01 us  [the longest x1 0.01 us: on_device(): after = lax.ppermute(jnp.stack([k[:BLOCK], v[:BLOCK]]), 'ctx', down)]
    pallas_call x0 -> x2, Pallas kernels: none -> 36.4 us  [the longest x1 21.2 us: backward_heads(): pl.pallas_call(backward_kernel, grid=(heads,), in_specs=[pl.BlockSpec(mem...]
    psum x1 -> x0, waiting for transfers between devices: 28.9 us -> none  [on_device(): grad_weight = lax.psum(partial_rows, 'dp').astype(jnp.float32)]
    all_to_all x0 -> x1, blocking collectives: none -> 22.3 us  [exchange(): return lax.all_to_all(x, axis, 0, 0, axis_index_groups=groups, tiled=True)]
  transfers between devices with their start and end apart: 8 -> 9, of which waited for: 6 -> 4; matrix products, arithmetic and copies ran while one was open for 6% -> 9% of each run, Pallas kernels for 0% -> 9%
where the time goes in v1:
time: 229 us; the launch traced here: 228 us
  waiting for transfers between devices  62.2 us (27%)
  Pallas kernels  36.4 us (16%)
  starting transfers between devices  33 us (14%)
  local copies, waits for them, and re-layouts  32 us (14%)
  blocking collectives  22.3 us (10%)
  other arithmetic  17.7 us (8%)
  between operations  14.4 us (6%)
  matrix products  9.53 us (4%)
    all_to_all x4, waiting for transfers between devices, exchange(): return lax.all_to_all(x, axis, 0, 0, axis_index_groups=groups, tiled=True)  56.1 us
    all_to_all x1, blocking collectives, exchange(): return lax.all_to_all(x, axis, 0, 0, axis_index_groups=groups, tiled=True)  22.3 us
    pallas_call x1, Pallas kernels, backward_heads(): pl.pallas_call(backward_kernel, grid=(heads,), in_specs=[pl.BlockSpec(mem...  21.2 us
    all_to_all x4, starting transfers between devices, exchange(): return lax.all_to_all(x, axis, 0, 0, axis_index_groups=groups, tiled=True)  20.1 us
    unnamed x36, local copies, waits for them, and re-layouts  15.5 us
    pallas_call x1, Pallas kernels, forward_heads(): pl.pallas_call(forward_kernel, grid=(heads,), in_specs=[pl.BlockSpec(memo...  15.2 us
    reshape x2, local copies, waits for them, and re-layouts, on_device(): partial.reshape(groups, GROUP, dp, share, width).transpose(2, 0, 1, 3, 4)  8.79 us
    dot_general x2, matrix products, dot(): lax.dot_general(a, b, (((da,), (db,)), ((), ())), preferred_element_type=...  6.08 us
  transfers between devices with their start and end apart: 9, of which 4 were waited for; matrix products, arithmetic and copies ran while one was open for 9% of the time, Pallas kernels for 9%

profile of v1, /device:TPU:73, one launch (start us, length us, event | category | flops | bytes accessed | tf_op | source)
XLA Modules:
  0.0 227.6 jit_solution(2064236052955291553)
XLA Ops:
  7.2 0.0 copy-start
  7.2 1.8 convert_reduce_fusion.2
  9.0 1.6 convert_reduce_fusion.3
  10.7 1.1 broadcast_in_dim.46
  11.8 5.4 %all-to-all-start = ((bf16[8,2,32,1024]{3,2,1,0:T(8,128)(2,1)}), bf16[8,2,32,1024]{3,2,1,0:T(8,128)(2,1)S(1)}, u32[]{:S(2)}, u32[]{:S(2)}) async-start(bf16[8,2,32,1024]{3,2,1,0:T(8,128)(2,1)} %broadcast_in_dim.46), calls=%async_computation | async-start | bytes 2097152 | tf_op jit(solution)/shard_map/all_to_all | solution.py:165
  17.1 1.7 fusion.13
  18.9 1.1 pad_maximum_fusion.3
  19.9 3.7 %collective-permute-start.1 = (bf16[2,256,1024]{2,1,0:T(8,128)(2,1)}, bf16[2,256,1024]{2,1,0:T(8,128)(2,1)}, u32[]{:S(2)}, u32[]{:S(2)}) collective-permute-start(bf16[2,256,1024]{2,1,0:T(8,128)(2,1)} %pad_maximum_fusion.3), channel_id=1, source_target_pairs={{8,0},{16,8},{24,16},{32,24},{40,32},{48,40},{56,48},{64,56},{72,6... | collective-permute-start | bytes 3145736 | tf_op jit(solution)/shard_map/ppermute | solution.py:204
  23.6 1.1 pad_maximum_fusion.2
  24.7 1.9 collective-permute-start
  26.7 0.1 abs_compare_fusion
  26.7 0.1 compare_and_fusion
  26.8 25.9 %all-to-all-done.one = bf16[8,2,32,1024]{3,2,1,0:T(8,128)(2,1)S(1)} async-done(((bf16[8,2,32,1024]{3,2,1,0:T(8,128)(2,1)}), bf16[8,2,32,1024]{3,2,1,0:T(8,128)(2,1)S(1)}, u32[]{:S(2)}, u32[]{:S(2)}) %all-to-all-start) | async-done | bytes 1048608 | tf_op jit(solution)/shard_map/all_to_all | solution.py:165
  52.8 0.4 convert_reduce_fusion.1
  53.2 0.1 fusion.10
  53.3 0.1 copy.18
  53.4 0.7 broadcast_in_dim.48
  54.1 3.6 %all-to-all-start.1 = ((bf16[4,2,16,1024]{3,2,1,0:T(8,128)(2,1)}), bf16[4,2,16,1024]{3,2,1,0:T(8,128)(2,1)S(1)}, u32[]{:S(2)}, u32[]{:S(2)}) async-start(bf16[4,2,16,1024]{3,2,1,0:T(8,128)(2,1)} %broadcast_in_dim.48), calls=%async_computation.1 | async-start | bytes 524288 | tf_op jit(solution)/shard_map/all_to_all | solution.py:165
  57.7 0.1 add_select_fusion.1.edge_ref
  57.8 3.5 %convolution_convert_fusion.2.g_ref = bf16[512,1024]{1,0:T(8,128)(2,1)} fusion(bf16[1024,1024]{1,0:T(8,128)(2,1)S(1)} %copy-done, bf16[1,512,1024]{2,1,0:T(8,128)(2,1)} %param.8), kind=kOutput, calls=%fused_computation.16 | convolution fusion | flops 1074266112 | bytes 4194304 | tf_op jit(solution)/shard_map/dot_general | solution.py:24
  61.3 2.3 %all-to-all-done.1.two = bf16[4,2,16,1024]{3,2,1,0:T(8,128)(2,1)S(1)} async-done(((bf16[4,2,16,1024]{3,2,1,0:T(8,128)(2,1)}), bf16[4,2,16,1024]{3,2,1,0:T(8,128)(2,1)S(1)}, u32[]{:S(2)}, u32[]{:S(2)}) %all-to-all-start.1) | async-done | bytes 262176 | tf_op jit(solution)/shard_map/all_to_all | solution.py:165
  63.6 0.1 broadcast_in_dim.24.bias_ref
  63.7 0.0 copy-start.5
  63.8 0.0 copy-start.1
  63.8 1.5 copy-done.1
  65.2 1.2 copy-done.3
  66.4 1.2 copy-done.7
  67.7 1.2 copy-done.9
  68.9 15.2 %forward_heads.1 = (bf16[512,1024]{1,0:T(8,128)(2,1)S(1)}, f32[8,2,512]{2,1,0:T(2,128)S(1)}) custom-call(f32[2]{0:T(128)S(1)} %add_select_fusion.1.edge_ref, f32[2,320,256]{2,1,0:T(8,128)S(1)} %broadcast_in_dim.24.bias_ref, bf16[512,1024]{1,0:T(8,128)(2,1)S(1)} %bitcast.59, bf16[512,1024]{1,0:T(8,128)(2,1)S(1)} %bitcast.54, bf16[512,1024]{1,0:T(8,128)(2,1)S(1)} %bitcast.57, ...), custom_call_target="tpu_custom_call" | custom-call | tf_op jit(solution)/shard_map/forward_heads/pallas_call | solution.py:118
  84.1 1.0 copy-done.16
  85.1 2.6 %convolution_convert_fusion = bf16[1024,1024]{1,0:T(8,128)(2,1)} fusion(bf16[512,1024]{1,0:T(8,128)(2,1)S(1)} %get-tuple-element.13, bf16[1,512,1024]{2,1,0:T(8,128)(2,1)S(1)} %copy-done.17), kind=kOutput, calls=%fused_computation.14 | convolution fusion | flops 1074790400 | bytes 4194304 | tf_op jit(solution)/shard_map/dot_general | solution.py:24
  87.7 4.1 %reshape.190 = bf16[4,8,8,4,1024]{4,3,2,1,0:T(4,128)(2,1)} reshape(bf16[1024,1024]{1,0:T(8,128)(2,1)} %convolution_convert_fusion) | data formatting | bytes 4194304 | tf_op jit(solution)/shard_map/reshape | solution.py:216
  91.8 4.7 %copy.25 = bf16[4,8,8,4,1024]{4,1,3,0,2:T(8,128)(2,1)} copy(bf16[4,8,8,4,1024]{4,3,2,1,0:T(4,128)(2,1)} %reshape.190) | data formatting | bytes 4194304 | tf_op jit(solution)/shard_map/reshape | solution.py:216
  96.5 0.0 reduce-scatter.2.cloned.1.call-update
  96.5 1.2 copy-done.2
  97.8 1.2 copy-done.4
  99.0 1.1 copy-done.6
  100.1 1.2 copy-done.8
  101.3 1.2 copy-done.10
  102.5 21.2 %backward_heads.1 = (bf16[512,1024]{1,0:T(8,128)(2,1)}, f32[2,512,1024]{2,1,0:T(8,128)}, bf16[2,256,1024]{2,1,0:T(8,128)(2,1)S(1)}, bf16[2,256,1024]{2,1,0:T(8,1...) custom-call(f32[2]{0:T(128)S(1)} %add_select_fusion.1.edge_ref, f32[2,320,256]{2,1,0:T(8,128)S(1)} %copy-done.6, ...), custom_call_target="tpu_custom_call" | custom-call | tf_op jit(solution)/shard_map/backward_heads/pallas_call | solution.py:142
  123.7 1.4 copy-done.11
  125.1 1.0 copy-done.13
  126.0 1.1 copy-done.15
  127.2 6.1 %reduce-scatter.2.cloned.1.call-done = bf16[1,4,8,4,1024]{4,2,3,1,0:T(8,128)(2,1)} async-done(((bf16[8,4,8,4,1024]{4,2,3,1,0:T(8,128)(2,1)}), bf16[1,4,8,4,1024]{4,2,3,1,0:T(8,128)(2,1)}) %reduce-scatter.2.cloned.1.call-update) | async-done | bytes 262160 | tf_op jit(solution)/shard_map/reduce_scatter | solution.py:217
  133.2 1.2 copy.22
  134.4 0.1 reshape_reduce_scatter.3
  134.5 22.3 %all_to_all.25 = bf16[4,64,1024]{2,1,0:T(8,128)(2,1)S(1)} all-to-all(bf16[4,64,1024]{2,1,0:T(8,128)(2,1)S(1)} %pad_maximum_fusion.4), channel_id=1, replica_groups={{0,64,128,192},{8,72,136,200},{16,80,144,208},{24,88,152,216},{32,96,16..., dimensions={0} | all-to-all | bytes 1048576 | tf_op jit(solution)/shard_map/all_to_all | solution.py:165
  156.8 0.1 convert_reduce_fusion.4
  156.9 0.3 add.66
  157.2 0.5 fusion.4
  157.7 1.1 copy.23
  158.8 2.5 %pad_maximum_fusion = bf16[8,68,1024]{2,1,0:T(8,128)(2,1)} fusion(bf16[8,4,1024]{2,1,0:T(4,128)(2,1)S(1)} %reshape.192, bf16[8,64,1024]{2,1,0:T(8,128)(2,1)} %bitcast.64), kind=kLoop, calls=%fused_computation.18 | loop fusion | flops 2228224 | bytes 2228224 | tf_op jit(solution)/shard_map/concatenate | solution.py:235
  161.3 4.3 %all-to-all-start.3 = ((bf16[8,68,1024]{2,1,0:T(8,128)(2,1)}), bf16[8,68,1024]{2,1,0:T(8,128)(2,1)}, u32[]{:S(2)}, u32[]{:S(2)}) async-start(bf16[8,68,1024]{2,1,0:T(8,128)(2,1)} %pad_maximum_fusion), calls=%async_computation.4 | async-start | bytes 2359296 | tf_op jit(solution)/shard_map/all_to_all | solution.py:165
  165.6 3.2 %collective-permute-start.2 = (bf16[2,256,1024]{2,1,0:T(8,128)(2,1)}, bf16[2,256,1024]{2,1,0:T(8,128)(2,1)}, u32[]{:S(2)}, u32[]{:S(2)}) collective-permute-start(bf16[2,256,1024]{2,1,0:T(8,128)(2,1)} %copy-done.15), channel_id=1, source_target_pairs={{0,8},{8,16},{16,24},{24,32},{32,40},{40,48},{48,56},{56,64},{64,7... | collective-permute-start | bytes 3145736 | tf_op jit(solution)/shard_map/ppermute | solution.py:224
  168.8 4.2 %collective-permute-start.3 = (bf16[2,256,1024]{2,1,0:T(8,128)(2,1)S(1)}, bf16[2,256,1024]{2,1,0:T(8,128)(2,1)}, u32[]{:S(2)}, u32[]{:S(2)}) collective-permute-start(bf16[2,256,1024]{2,1,0:T(8,128)(2,1)S(1)} %copy-done.14), channel_id=1, source_target_pairs={{8,0},{16,8},{24,16},{32,24},{40,32},{48,40},{56,48},{64,56},{72,6... | collective-permute-start | bytes 3145736 | tf_op jit(solution)/shard_map/ppermute | solution.py:223
  173.0 3.5 %fusion.3 = bf16[1,512,1024]{2,1,0:T(8,128)(2,1)} fusion(bf16[512,1024]{1,0:T(8,128)(2,1)} %copy-done.16, bf16[1024,1024]{1,0:T(8,128)(2,1)S(1)} %copy-done), kind=kOutput, calls=%fused_computation.17 | convolution fusion | flops 1074266112 | bytes 4194304 | tf_op jit(solution)/shard_map/dot_general | solution.py:218
  176.5 27.9 %all-to-all-done.3 = bf16[8,68,1024]{2,1,0:T(8,128)(2,1)} async-done(((bf16[8,68,1024]{2,1,0:T(8,128)(2,1)}), bf16[8,68,1024]{2,1,0:T(8,128)(2,1)}, u32[]{:S(2)}, u32[]{:S(2)}) %all-to-all-start.3) | async-done | bytes 1114144 | tf_op jit(solution)/shard_map/all_to_all | solution.py:165
  204.4 1.5 convert_reduce_fusion
  205.9 0.6 broadcast_in_dim.51
  206.5 6.8 %all-to-all-start.4 = ((bf16[8,4,1024]{2,1,0:T(4,128)(2,1)}), bf16[8,4,1024]{2,1,0:T(4,128)(2,1)S(1)}, u32[]{:S(2)}, u32[]{:S(2)}) async-start(bf16[8,4,1024]{2,1,0:T(4,128)(2,1)} %broadcast_in_dim.51), calls=%async_computation.5 | async-start | bytes 131072 | tf_op jit(solution)/shard_map/all_to_all | solution.py:165
  213.3 2.8 %bitcast_add_fusion = f32[2,512,1024]{2,1,0:T(8,128)S(1)} fusion(f32[2,512,1024]{2,1,0:T(8,128)} %get-tuple-element.16, f32[2,32,1024]{2,1,0:T(8,128)S(1)} %bitcast.65), kind=kLoop, calls=%fused_computation | loop fusion | flops 1048576 | bytes 8650752 | tf_op jit(solution)/shard_map/add | solution.py:242
  216.2 2.4 %fusion = (bf16[2,256,1024]{2,1,0:T(8,128)(2,1)S(1)}, bf16[2,256,1024]{2,1,0:T(8,128)(2,1)S(1)}) fusion(f32[2,512,1024]{2,1,0:T(8,128)S(1)} %bitcast_add_fusion, bf16[2,256,1024]{2,1,0:T(8,128)(2,1)} %collective-permute-done.3, bf16[2,256,1024]{2,1,0:T(8,128)(2,1)} %collective-permute-done.2), kind=kLoop, calls=%fused_computation.3 | loop fusion | flops 3145728 | bytes 8388608 | tf_op jit(solution)/shard_map/convert.6
  218.6 1.5 pad_maximum_fusion.1
  220.1 0.7 reshape.197
  (41 shorter events, 0.3 us)
Async XLA Ops:
  7.2 50.7 %copy-start = (bf16[1024,1024]{1,0:T(8,128)(2,1)S(1)}, bf16[1024,1024]{1,0:T(8,128)(2,1)}, u32[]{:S(2)}) copy-start(bf16[1024,1024]{1,0:T(8,128)(2,1)} %param.9) | copy-start | bytes 6291460
  11.8 41.0 %all-to-all-start = ((bf16[8,2,32,1024]{3,2,1,0:T(8,128)(2,1)}), bf16[8,2,32,1024]{3,2,1,0:T(8,128)(2,1)S(1)}, u32[]{:S(2)}, u32[]{:S(2)}) async-start(bf16[8,2,32,1024]{3,2,1,0:T(8,128)(2,1)} %broadcast_in_dim.46), calls=%async_computation | async-start | bytes 2097152 | tf_op jit(solution)/shard_map/all_to_all | solution.py:165
  19.9 41.4 %collective-permute-start.1 = (bf16[2,256,1024]{2,1,0:T(8,128)(2,1)}, bf16[2,256,1024]{2,1,0:T(8,128)(2,1)}, u32[]{:S(2)}, u32[]{:S(2)}) collective-permute-start(bf16[2,256,1024]{2,1,0:T(8,128)(2,1)} %pad_maximum_fusion.3), channel_id=1, source_target_pairs={{8,0},{16,8},{24,16},{32,24},{40,32},{48,40},{56,48},{64,56},{72,6... | collective-permute-start | bytes 3145736 | tf_op jit(solution)/shard_map/ppermute | solution.py:204
  24.7 36.6 %collective-permute-start = (bf16[2,256,1024]{2,1,0:T(8,128)(2,1)}, bf16[2,256,1024]{2,1,0:T(8,128)(2,1)}, u32[]{:S(2)}, u32[]{:S(2)}) collective-permute-start(bf16[2,256,1024]{2,1,0:T(8,128)(2,1)} %pad_maximum_fusion.2), channel_id=1, source_target_pairs={{0,8},{8,16},{16,24},{24,32},{32,40},{40,48},{48,56},{56,64},{64,7... | collective-permute-start | bytes 3145736 | tf_op jit(solution)/shard_map/ppermute | solution.py:203
  54.1 9.5 %all-to-all-start.1 = ((bf16[4,2,16,1024]{3,2,1,0:T(8,128)(2,1)}), bf16[4,2,16,1024]{3,2,1,0:T(8,128)(2,1)S(1)}, u32[]{:S(2)}, u32[]{:S(2)}) async-start(bf16[4,2,16,1024]{3,2,1,0:T(8,128)(2,1)} %broadcast_in_dim.48), calls=%async_computation.1 | async-start | bytes 524288 | tf_op jit(solution)/shard_map/all_to_all | solution.py:165
  57.7 75.5 %reduce-scatter.2.cloned.1.call-start = ((), (), s32[]{:S(2)}) async-start(), calls=%async_computation.6 | async-start | bytes 2359296 | tf_op jit(solution)/shard_map/reduce_scatter | solution.py:217
  63.7 20.4 %copy-start.5 = (f32[2,320,256]{2,1,0:T(8,128)}, f32[2,320,256]{2,1,0:T(8,128)S(1)}, u32[]{:S(2)}) copy-start(f32[2,320,256]{2,1,0:T(8,128)S(1)} %broadcast_in_dim.24.bias_ref) | copy-start | bytes 1966084
  63.8 1.5 copy-start.1
  65.2 1.2 copy-start.3
  66.4 1.2 copy-start.7
  67.7 1.2 copy-start.9
  68.9 16.2 %copy-start.17 = (bf16[1,512,1024]{2,1,0:T(8,128)(2,1)S(1)}, bf16[1,512,1024]{2,1,0:T(8,128)(2,1)}, u32[]{:S(2)}) copy-start(bf16[1,512,1024]{2,1,0:T(8,128)(2,1)} %param.8) | copy-start | bytes 3145732
  84.1 1.0 copy-start.16
  96.5 1.2 copy-start.2
  97.8 1.2 copy-start.4
  99.0 1.1 copy-start.6
  100.1 1.2 copy-start.8
  101.3 1.2 copy-start.10
  123.7 1.4 copy-start.11
  125.1 1.0 copy-start.13
  126.0 1.1 copy-start.15
  134.5 22.7 %copy-start.12 = (f32[2,256,1024]{2,1,0:T(8,128)S(1)}, f32[2,256,1024]{2,1,0:T(8,128)}, u32[]{:S(2)}) copy-start(f32[2,256,1024]{2,1,0:T(8,128)} %copy-done.11) | copy-start | bytes 6291460
  158.8 10.0 %copy-start.14 = (bf16[2,256,1024]{2,1,0:T(8,128)(2,1)S(1)}, bf16[2,256,1024]{2,1,0:T(8,128)(2,1)}, u32[]{:S(2)}) copy-start(bf16[2,256,1024]{2,1,0:T(8,128)(2,1)} %copy-done.13) | copy-start | bytes 3145732
  161.3 43.1 %all-to-all-start.3 = ((bf16[8,68,1024]{2,1,0:T(8,128)(2,1)}), bf16[8,68,1024]{2,1,0:T(8,128)(2,1)}, u32[]{:S(2)}, u32[]{:S(2)}) async-start(bf16[8,68,1024]{2,1,0:T(8,128)(2,1)} %pad_maximum_fusion), calls=%async_computation.4 | async-start | bytes 2359296 | tf_op jit(solution)/shard_map/all_to_all | solution.py:165
  165.6 50.6 %collective-permute-start.2 = (bf16[2,256,1024]{2,1,0:T(8,128)(2,1)}, bf16[2,256,1024]{2,1,0:T(8,128)(2,1)}, u32[]{:S(2)}, u32[]{:S(2)}) collective-permute-start(bf16[2,256,1024]{2,1,0:T(8,128)(2,1)} %copy-done.15), channel_id=1, source_target_pairs={{0,8},{8,16},{16,24},{24,32},{32,40},{40,48},{48,56},{56,64},{64,7... | collective-permute-start | bytes 3145736 | tf_op jit(solution)/shard_map/ppermute | solution.py:224
  168.8 47.3 %collective-permute-start.3 = (bf16[2,256,1024]{2,1,0:T(8,128)(2,1)S(1)}, bf16[2,256,1024]{2,1,0:T(8,128)(2,1)}, u32[]{:S(2)}, u32[]{:S(2)}) collective-permute-start(bf16[2,256,1024]{2,1,0:T(8,128)(2,1)S(1)} %copy-done.14), channel_id=1, source_target_pairs={{8,0},{16,8},{24,16},{32,24},{40,32},{48,40},{56,48},{64,56},{72,6... | collective-permute-start | bytes 3145736 | tf_op jit(solution)/shard_map/ppermute | solution.py:223
  206.5 13.5 %all-to-all-start.4 = ((bf16[8,4,1024]{2,1,0:T(4,128)(2,1)}), bf16[8,4,1024]{2,1,0:T(4,128)(2,1)S(1)}, u32[]{:S(2)}, u32[]{:S(2)}) async-start(bf16[8,4,1024]{2,1,0:T(4,128)(2,1)} %broadcast_in_dim.51), calls=%async_computation.5 | async-start | bytes 131072 | tf_op jit(solution)/shard_map/all_to_all | solution.py:165
Sparse Core Ops, SparseCore 0:
  96.6 36.5 reduce-scatter.1

commit v2 on v1

v2 whole, which is shorter than its diff:
```python
import math

import jax
import jax.numpy as jnp
from jax import lax
from jax.experimental import pallas as pl
from jax.experimental.pallas import tpu as pltpu
from jax.sharding import PartitionSpec as P

HEAD = 128
BLOCK = 256
POOL = 16
GROUP = 8
SCALE = 1.0 / math.sqrt(POOL)
FACTOR = 1.0 / math.sqrt(HEAD)
LOG2 = FACTOR * math.log2(math.e)
MASKED = -1e30
F32 = jnp.float32
BF16 = jnp.bfloat16
PER = (2, 2, 2, 2, 2, 2, 4, 2)
PARAMS = pltpu.CompilerParams(vmem_limit_bytes=56 * 1024 * 1024)


def dot(a, b, da, db):
    return lax.dot_general(a, b, (((da,), (db,)), ((), ())), preferred_element_type=F32)


def shape(dims, kind):
    return jax.ShapeDtypeStruct(dims, kind)


def cols(*lead, width=HEAD):
    def spec(per):
        return pl.BlockSpec(lead + (width * per,), lambda h: (0,) * len(lead) + (h,))

    return spec, lambda ref, i: ref.at[(slice(None),) * len(lead) + (pl.ds(i * width, width),)]


def heads_of(*dims):
    def spec(per):
        return pl.BlockSpec((per,) + dims, lambda h: (h,) + (0,) * len(dims))

    return spec, lambda ref, i: ref.at[pl.ds(i, 1)]


def second(lead, rows, *rest):
    def spec(per):
        return pl.BlockSpec((lead, rows * per) + rest, lambda h: (0, h) + (0,) * len(rest))

    return spec, lambda ref, i: ref.at[:, pl.ds(i * rows, rows)]


def leading(rows, *rest):
    def spec(per):
        return pl.BlockSpec((rows * per,) + rest, lambda h: (h,) + (0,) * len(rest))

    return spec, lambda ref, i: ref.at[pl.ds(i * rows, rows)]


def fixed(*dims):
    return lambda per: pl.BlockSpec(dims, lambda h: (0,) * len(dims)), lambda ref, i: ref


SMEM = lambda per: pl.BlockSpec(memory_space=pltpu.SMEM), lambda ref, i: ref


def over_heads(kernel, steps, per, ins, outs, out_shape, name, flops=1):
    def body(*refs):
        for i in range(per):
            kernel(*(view(ref, i) for ref, (_, view) in zip(refs, ins + outs)))

    return pl.pallas_call(
        body,
        grid=(steps // per,),
        in_specs=[spec(per) for spec, _ in ins],
        out_specs=[spec(per) for spec, _ in outs],
        out_shape=out_shape,
        compiler_params=PARAMS,
        cost_estimate=pl.CostEstimate(flops=flops, bytes_accessed=1, transcendentals=0),
        name=name,
    )


def prepare_kernel(k_ref, v_ref, last_ref, first_ref, one_ref):
    tokens = k_ref.shape[0]
    count = tokens // POOL
    row = lax.broadcasted_iota(jnp.int32, (count, tokens), 0)
    at = lax.broadcasted_iota(jnp.int32, (count, tokens), 1)
    member = (at // POOL == row).astype(BF16)
    for which, ref in enumerate((k_ref, v_ref)):
        rows = ref[...]
        last_ref[which] = rows[tokens - BLOCK :]
        first_ref[which] = rows[:BLOCK]
        one = (dot(member, rows, 1, 0) * SCALE).astype(BF16)
        for slot in range(GROUP):
            one_ref[slot, which * count : (which + 1) * count] = one


def prepare(k, v):
    tokens, width = k.shape
    step = 2 * HEAD
    rows = cols(tokens, width=step)
    edge = cols(2, BLOCK, width=step)
    return over_heads(
        prepare_kernel,
        width // step,
        PER[0],
        [rows, rows],
        [edge, edge, cols(GROUP, 2 * tokens // POOL, width=step)],
        [
            shape((2, BLOCK, width), BF16),
            shape((2, BLOCK, width), BF16),
            shape((GROUP, 2 * tokens // POOL, width), BF16),
        ],
        "prepare",
    )(k, v)


def both(left, right):
    return jnp.concatenate([left, right], axis=1)


def near_scores(edge_ref, before, after, q):
    first = dot(before[0], q[:BLOCK], 1, 1) * LOG2 + edge_ref[0]
    return both(first, dot(after[0], q[BLOCK:], 1, 1) * LOG2 + edge_ref[1])


def join(stat_ref, acc_ref, s):
    own_top = stat_ref[0, 0:1]
    top = jnp.maximum(own_top, jnp.max(s, axis=0, keepdims=True))
    shrink = jnp.exp2(own_top - top)
    p = jnp.exp2(s - top)
    total = stat_ref[0, 1:2] * shrink + jnp.sum(p, axis=0, keepdims=True)
    return top, total, acc_ref[0] * shrink, p.astype(BF16)


def own_kernel(q_ref, k_ref, v_ref, acc_ref, stat_ref):
    s = dot(k_ref[...], q_ref[...], 1, 1) * LOG2
    top = jnp.max(s, axis=0, keepdims=True)
    p = jnp.exp2(s - top)
    stat_ref[0, 0:1] = top
    stat_ref[0, 1:2] = jnp.sum(p, axis=0, keepdims=True)
    acc_ref[0] = dot(v_ref[...], p.astype(BF16), 0, 0)


def forward_own(q, k, v):
    tokens, width = q.shape
    heads = width // HEAD
    rows = cols(tokens)
    return over_heads(
        own_kernel,
        heads,
        PER[1],
        [rows, rows, rows],
        [heads_of(HEAD, tokens), heads_of(2, tokens)],
        [shape((heads, HEAD, tokens), F32), shape((heads, 2, tokens), F32)],
        "forward_own",
    )(q, k, v)


def coarse_rows(one, two):
    half = one.shape[1] // 2
    middle = [one[:, which * half : (which + 1) * half].reshape(-1, HEAD) for which in range(2)]
    groups, per_group, _ = two.shape
    count = groups * per_group
    pairs = per_group // (2 * GROUP)
    to = lax.broadcasted_iota(jnp.int32, (count, count), 0)
    at = lax.broadcasted_iota(jnp.int32, (count, count), 1)
    member = to // (pairs * groups) % GROUP
    source = to // pairs % groups * per_group + member * 2 * pairs + to // (count // 2) * pairs + to % pairs
    top = dot((at == source).astype(BF16), two[...].reshape(count, HEAD), 1, 0).astype(BF16)
    keys = jnp.concatenate([middle[0], top[: count // 2]], axis=0)
    values = jnp.concatenate([middle[1], top[count // 2 :]], axis=0)
    return keys, values


def forward_coarse_kernel(bias_ref, q_ref, one, two, acc_ref, stat_ref, out_ref, new_ref):
    keys, values = coarse_rows(one, two)
    s = dot(keys, q_ref[...], 1, 1) * LOG2 + bias_ref[...]
    top, total, out, p = join(stat_ref, acc_ref, s)
    new_ref[0, 0:1] = top
    new_ref[0, 1:2] = total
    out_ref[0] = out + dot(values, p, 0, 0)


def forward_coarse(bias, q, one, two, acc, stat):
    tokens, width = q.shape
    heads = width // HEAD
    state = [heads_of(HEAD, tokens), heads_of(2, tokens)]
    return over_heads(
        forward_coarse_kernel,
        heads,
        PER[3],
        [fixed(*bias.shape), cols(tokens), cols(*one.shape[:2]), cols(*two.shape[:2])] + state,
        state,
        [shape((heads, HEAD, tokens), F32), shape((heads, 2, tokens), F32)],
        "forward_coarse",
    )(bias, q, one, two, acc, stat)


def forward_near_kernel(
    edge_ref, q_ref, g_ref, before, after, acc_ref, own_ref, attn_ref, across_ref, stat_ref
):
    s = near_scores(edge_ref, before, after, q_ref[...])
    top, total, out, p = join(own_ref, acc_ref, s)
    out = out + both(dot(before[1], p[:, :BLOCK], 0, 0), dot(after[1], p[:, BLOCK:], 0, 0))
    across = (out / total).astype(BF16)
    across_ref[...] = across
    attn_ref[...] = jnp.transpose(across.astype(F32)).astype(BF16)
    stat_ref[0, 0:1] = top + jnp.log2(total)
    stat_ref[0, 1:2] = jnp.sum(jnp.transpose(g_ref[...].astype(F32)) * across.astype(F32), axis=0, keepdims=True)


def forward_near(edge, q, g, before, after, acc, stat):
    tokens, width = q.shape
    heads = width // HEAD
    rows = cols(tokens)
    near = cols(2, BLOCK)
    return over_heads(
        forward_near_kernel,
        heads,
        PER[2],
        [SMEM, rows, rows, near, near, heads_of(HEAD, tokens), heads_of(2, tokens)],
        [rows, leading(HEAD, tokens), heads_of(2, tokens)],
        [
            shape((tokens, width), BF16),
            shape((width, tokens), BF16),
            shape((heads, 2, tokens), F32),
        ],
        "forward_near",
    )(edge, q, g, before, after, acc, stat)


def weight_kernel(core_ref, across_ref, up_ref, keep_ref, send_ref):
    weight = dot(across_ref[...], up_ref[...], 1, 0).astype(BF16)
    first = core_ref[0] == 0
    keep_ref[0] = jnp.where(first, weight[:, :HEAD], weight[:, HEAD:])
    send_ref[0] = jnp.where(first, weight[:, HEAD:], weight[:, :HEAD])


def weight_terms(core, across, upstream):
    width, tokens = across.shape
    model = upstream.shape[1]
    pairs = model // (2 * HEAD)
    return over_heads(
        weight_kernel,
        pairs,
        PER[7],
        [SMEM, fixed(width, tokens), cols(tokens, width=2 * HEAD)],
        [leading(1, width, HEAD)] * 2,
        [shape((pairs, width, HEAD), BF16)] * 2,
        "weight_terms",
    )(core, across, upstream)


def gradients(s, dprob, stat_ref):
    p = jnp.exp2(s - stat_ref[0, 0:1])
    return p.astype(BF16), (p * (dprob - stat_ref[0, 1:2])).astype(BF16)


def backward_coarse_kernel(bias_ref, q_ref, g_ref, one, two, stat_ref, part_ref, dq_ref, one_ref, two_ref):
    keys, values = coarse_rows(one, two)
    q, g = q_ref[...], g_ref[...]
    s = dot(keys, q, 1, 1) * LOG2 + bias_ref[...]
    p, ds = gradients(s, dot(values, g, 1, 1), stat_ref)
    dk = dot(ds, q, 1, 0) * FACTOR
    dv = dot(p, g, 1, 0)
    dq_ref[...] = jnp.transpose((part_ref[0] + dot(keys, ds, 0, 0)) * FACTOR).astype(BF16)
    slots = one_ref.shape[0]
    count = slots * (one_ref.shape[2] // 2)
    for ref, begin, end in ((one_ref, 0, count), (two_ref, count, dk.shape[0])):
        pieces = [d[begin:end].reshape(slots, -1, HEAD) for d in (dk, dv)]
        ref[:, 0] = jnp.concatenate(pieces, axis=1).astype(BF16)


def backward_coarse(bias, q, g, one, two, stat, part):
    tokens, width = q.shape
    heads = width // HEAD
    rows = cols(tokens)
    slots = one.shape[0]
    for_one, for_two = one.shape[1], two.shape[0] * two.shape[1] // slots
    return over_heads(
        backward_coarse_kernel,
        heads,
        PER[5],
        [
            fixed(*bias.shape), rows, rows, cols(*one.shape[:2]), cols(*two.shape[:2]), heads_of(2, tokens),
            heads_of(HEAD, tokens),
        ],
        [rows, second(slots, 1, for_one, HEAD), second(slots, 1, for_two, HEAD)],
        [
            shape((tokens, width), BF16),
            shape((slots, heads, for_one, HEAD), BF16),
            shape((slots, heads, for_two, HEAD), BF16),
        ],
        "backward_coarse",
    )(bias, q, g, one, two, stat, part)


def fine_kernel(
    edge_ref, q_ref, k_ref, v_ref, g_ref, before, after, stat_ref, part_ref, down_ref, dbefore_ref, dafter_ref
):
    q, k, v, g = q_ref[...], k_ref[...], v_ref[...], g_ref[...]
    s_near = near_scores(edge_ref, before, after, q)
    dp_near = both(dot(before[1], g[:BLOCK], 1, 1), dot(after[1], g[BLOCK:], 1, 1))
    p_near, ds_near = gradients(s_near, dp_near, stat_ref)
    p, ds = gradients(dot(k, q, 1, 1) * LOG2, dot(v, g, 1, 1), stat_ref)
    down_ref[0] = dot(ds, q, 1, 0) * FACTOR
    down_ref[1] = dot(p, g, 1, 0)
    near = both(dot(before[0], ds_near[:, :BLOCK], 0, 0), dot(after[0], ds_near[:, BLOCK:], 0, 0))
    part_ref[0] = near + dot(k, ds, 0, 0)
    for side, ref in enumerate((dbefore_ref, dafter_ref)):
        rows = slice(side * BLOCK, (side + 1) * BLOCK)
        ref[0] = (dot(ds_near[:, rows], q[rows], 1, 0) * FACTOR).astype(BF16)
        ref[1] = dot(p_near[:, rows], g[rows], 1, 0).astype(BF16)


def backward_fine(edge, q, k, v, g, before, after, stat):
    tokens, width = q.shape
    heads = width // HEAD
    rows = cols(tokens)
    near = cols(2, BLOCK)
    return over_heads(
        fine_kernel,
        heads,
        PER[4],
        [SMEM, rows, rows, rows, rows, near, near, heads_of(2, tokens)],
        [heads_of(HEAD, tokens), cols(2, tokens), near, near],
        [
            shape((heads, HEAD, tokens), F32),
            shape((2, tokens, width), F32),
            shape((2, BLOCK, width), BF16),
            shape((2, BLOCK, width), BF16),
        ],
        "backward_fine",
    )(edge, q, k, v, g, before, after, stat)


def project_kernel(attn_ref, weight_ref, out_ref):
    out_ref[...] = dot(attn_ref[...], weight_ref[...], 1, 0).astype(BF16)


def project(attn, weight):
    tokens, width = attn.shape
    model = weight.shape[1]
    step = 2 * HEAD
    return over_heads(
        project_kernel,
        model // step,
        1,
        [fixed(tokens, width), cols(width, width=step)],
        [cols(tokens, width=step)],
        [shape((tokens, model), BF16)],
        "project",
    )(attn, weight)[0]


def finish_kernel(own, first, last, one_ref, two_ref, dk_ref, dv_ref):
    tokens = own.shape[1]
    size = tokens // POOL
    one = jnp.sum(one_ref[...].astype(F32), axis=0)
    for which, out_ref in enumerate((dk_ref, dv_ref)):
        term = one[which * size : (which + 1) * size] * SCALE
        term = jnp.broadcast_to(term[:, None], (size, POOL, HEAD)).reshape(tokens, HEAD)
        for side, edge in enumerate((first, last)):
            rows = pl.ds(side * BLOCK, BLOCK)
            at = 2 * which + side
            top = two_ref[0, at : at + 1] * (SCALE * SCALE)
            total = own[which, rows] + term[side * BLOCK : (side + 1) * BLOCK] + top + edge[which].astype(F32)
            out_ref[rows, :] = total.astype(BF16)


def finish(own, first, last, one, two):
    tokens, width = own.shape[1:]
    rows = 2 * tokens // POOL
    return over_heads(
        finish_kernel,
        width // HEAD,
        PER[6],
        [
            cols(2, tokens), cols(2, BLOCK), cols(2, BLOCK),
            second(one.shape[0], rows, HEAD), heads_of(*two.shape[1:]),
        ],
        [cols(tokens)] * 2,
        [shape((tokens, width), BF16)] * 2,
        "finish",
    )(own, first, last, one, two)


def exchange(x, axis, groups=None):
    return lax.all_to_all(x, axis, 0, 0, axis_index_groups=groups, tiled=True)


def masks(device, devices, tokens):
    group = device // GROUP
    per_group = GROUP * tokens // BLOCK
    block = device * (tokens // BLOCK) + jnp.arange(2, dtype=jnp.int32)[:, None]
    one = group * per_group + jnp.arange(GROUP * tokens // POOL, dtype=jnp.int32) * POOL // BLOCK
    pairs = tokens // BLOCK
    groups = devices // GROUP
    at = jnp.arange(devices * pairs, dtype=jnp.int32)
    from_group = (group - at // pairs) % groups
    two = from_group * per_group + at // (pairs * groups) * pairs + at % pairs
    one_ok = jnp.abs(one[None] - block) > 1
    two_ok = (jnp.abs(two[None] - block) > 1) & (two // per_group != group)[None]
    ok = jnp.concatenate([one_ok, two_ok], axis=1)
    bias = jnp.where(ok, 0.0, MASKED).astype(F32)
    bias = jnp.repeat(bias.T, BLOCK, axis=1)
    edge = jnp.stack([device == 0, device == devices - 1]).astype(F32) * MASKED
    return edge, bias


def after_all(x, *others):
    return lax.optimization_barrier((x,) + others)[0]


def on_device(queries, keys, values, grad_out, out_weight):
    q, k, v, upstream = queries[0], keys[0], values[0], grad_out[0]
    tokens, width = q.shape
    model = upstream.shape[1]
    devices = lax.axis_size("ctx")
    dp = lax.axis_size("dp")
    device = lax.axis_index("ctx")
    groups = devices // GROUP
    near = [[g * GROUP + i for i in range(GROUP)] for g in range(groups)]
    up = [(i, i + 1) for i in range(devices - 1)]
    down = [(i + 1, i) for i in range(devices - 1)]
    rows_one = tokens // POOL

    pairs = tokens // BLOCK

    far = [[(i, (i + step * GROUP) % devices) for i in range(devices)] for step in range(groups)]
    back = [[(j, i) for i, j in moves] for moves in far]

    last, first, one = prepare(k, v)
    one = exchange(one, "ctx", near)
    edge, bias = masks(device, devices, tokens)
    acc, stat = forward_own(q, k, v)
    one = after_all(one, acc)
    two = one.astype(F32).reshape(GROUP * 2 * pairs, POOL, width)
    two = (jnp.sum(two, axis=1) * SCALE).astype(BF16)
    two = [two] + [lax.ppermute(two, "ctx", moves) for moves in far[1:]]
    g = dot(after_all(upstream, two[0]), out_weight, 1, 1).astype(BF16)
    last, first, two = lax.optimization_barrier((last, first, two, g))[:3]
    before = lax.ppermute(last, "ctx", up)
    after = lax.ppermute(first, "ctx", down)
    two = jnp.stack(two)
    acc, stat = forward_coarse(bias, after_all(q, last), one, two, acc, stat)
    before, after = lax.optimization_barrier((before, after, acc))[:2]
    attn, across, stat = forward_near(edge, q, g, before, after, acc, stat)

    place = lax.axis_index("dp")
    keep, send = weight_terms((place % 2).reshape(1).astype(jnp.int32), across, upstream)
    other = lax.ppermute(send, "dp", [(i, i ^ 1) for i in range(dp)])
    part, d_own, d_before, d_after = backward_fine(
        edge, q, k, v, g, before, after, after_all(stat, send)
    )
    other = after_all(other, d_own)
    shares = []
    for step in range(dp // 2):
        at = (place // 2 + step) % (dp // 2)
        share = lax.dynamic_index_in_dim(keep, at, 0, False).astype(F32)
        share = share + lax.dynamic_index_in_dim(other, at, 0, False).astype(F32)
        shares.append(share.astype(BF16))
    sent = [
        lax.ppermute(share, "dp", [(i, (i + 2 * step) % dp) for i in range(dp)])
        for step, share in enumerate(shares)
        if step
    ]
    from_after = lax.ppermute(d_before, "ctx", down)
    from_before = lax.ppermute(d_after, "ctx", up)
    dq, d_one, d_two = backward_coarse(
        bias, q, lax.optimization_barrier((g, *shares))[0], one, two, stat, part
    )
    sent = lax.optimization_barrier((dq, *sent))[1:]
    weight = sum((share.astype(F32) for share in sent), shares[0].astype(F32)).astype(BF16)
    weight = weight.reshape(groups, GROUP, -1, HEAD).transpose(1, 0, 2, 3).reshape(GROUP, -1, HEAD)

    heads = width // HEAD
    d_one, d_two = d_one.reshape(GROUP, -1, HEAD), d_two.reshape(GROUP, -1, HEAD)
    start, count = d_one.shape[1], d_two.shape[1]
    mixed = project(after_all(attn, dq), out_weight)
    packed = jnp.concatenate([d_one, d_two, weight], axis=1)
    packed = exchange(after_all(packed, from_after, from_before, mixed), "ctx", near)
    small = jnp.sum(packed[:, start:].astype(F32), axis=0).astype(BF16)
    weight = small[count:].reshape(groups, -1, HEAD)
    d_two = small[:count]
    d_two = d_two.reshape(heads, 2, groups, pairs, HEAD).transpose(2, 0, 1, 3, 4).reshape(groups, -1, HEAD)
    count = d_two.shape[1]
    small = []
    for step, moves in enumerate(back):
        at = (device // GROUP - step) % groups
        piece = jnp.concatenate([d_two[step], lax.dynamic_index_in_dim(weight, at, 0, False)], axis=0)
        small.append(lax.ppermute(piece, "ctx", moves) if step else piece)
    small = sum(piece.astype(F32) for piece in small)
    mine_two = small[:count].reshape(heads, 2 * pairs, HEAD)
    weight = small[count:].astype(BF16)
    weight = exchange(jnp.broadcast_to(weight[None], (dp,) + weight.shape), "dp")
    grad_weight = jnp.swapaxes(weight, 0, 1).reshape(-1, model).astype(F32)

    grad_keys, grad_values = finish(d_own, from_before, from_after, packed, mine_two)
    return mixed[None], dq[None], grad_keys[None], grad_values[None], grad_weight


def solution(mesh):
    rows = P("dp", "ctx", None)
    return jax.shard_map(
        on_device,
        mesh=mesh,
        in_specs=(rows, rows, rows, rows, P()),
        out_specs=(rows, rows, rows, rows, P("ctx", None)),
        check_vma=False,
    )
```

time: 229 us -> 174 us (0.76)
  local copies, waits for them, and re-layouts: 32 us -> 4.79 us
  blocking collectives: 22.3 us -> 0 us
  starting transfers between devices: 33 us -> 53.5 us
  Pallas kernels: 36.4 us -> 55.8 us
  waiting for transfers between devices: 62.2 us -> 47.9 us
  between operations: 14.4 us -> 0.97 us
  other arithmetic: 17.7 us -> 5.61 us
  matrix products: 9.53 us -> 3.48 us
    all_to_all x4 -> x3, waiting for transfers between devices: 56.1 us -> 28.5 us  [exchange(): return lax.all_to_all(x, axis, 0, 0, axis_index_groups=groups, tiled=True)]
    all_to_all x1 -> x0, blocking collectives: 22.3 us -> none  [exchange(): return lax.all_to_all(x, axis, 0, 0, axis_index_groups=groups, tiled=True)]
    ppermute x2 -> x12, starting transfers between devices: 5.57 us -> 26.9 us  [the longest x3 6.65 us: on_device(): two = [two] + [lax.ppermute(two, 'ctx', moves) for moves in far[1:]]]
    pallas_call x2 -> x9, Pallas kernels: 36.4 us -> 55.8 us  [the longest x1 10.8 us: backward_fine(): over_heads(fine_kernel, heads, PER[4], [SMEM, rows, rows, rows, rows, nea...]
    ppermute x2 -> x12, waiting for transfers between devices: 0.01 us -> 16.7 us  [the longest x1 9 us: on_device(): before = lax.ppermute(last, 'ctx', up)]
    unnamed x36 -> x21, local copies, waits for them, and re-layouts: 15.5 us -> 2.94 us
    reshape x4 -> x1, local copies, waits for them, and re-layouts: 8.85 us -> 0.02 us  [on_device(): weight.reshape(groups, GROUP, -1, HEAD).transpose(1, 0, 2, 3)]
    reduce_scatter x1 -> x0, waiting for transfers between devices: 6.07 us -> none  [on_device(): summed = lax.psum_scatter(partial, 'dp', scatter_dimension=0, tiled=False)]
  transfers between devices with their start and end apart: 9 -> 17, of which waited for: 4 -> 8; matrix products, arithmetic and copies ran while one was open for 9% -> 6% of each run, Pallas kernels for 9% -> 25%
where the time goes in v2:
time: 174 us; the launch traced here: 172 us
  Pallas kernels  55.8 us (32%)
  starting transfers between devices  53.5 us (31%)
  waiting for transfers between devices  47.9 us (28%)
  other arithmetic  5.61 us (3%)
  local copies, waits for them, and re-layouts  4.79 us (3%)
  matrix products  3.48 us (2%)
    all_to_all x3, waiting for transfers between devices, exchange(): return lax.all_to_all(x, axis, 0, 0, axis_index_groups=groups, tiled=True)  28.5 us
    all_to_all x3, starting transfers between devices, exchange(): return lax.all_to_all(x, axis, 0, 0, axis_index_groups=groups, tiled=True)  18.6 us
    pallas_call x1, Pallas kernels, backward_fine(): over_heads(fine_kernel, heads, PER[4], [SMEM, rows, rows, rows, rows, nea...  10.8 us
    ppermute x1, waiting for transfers between devices, on_device(): before = lax.ppermute(last, 'ctx', up)  9 us
    pallas_call x1, Pallas kernels, backward_coarse(): over_heads(backward_coarse_kernel, heads, PER[5], [fixed(*bias.shape), ro...  8.09 us
    pallas_call x1, Pallas kernels, forward_coarse(): over_heads(forward_coarse_kernel, heads, PER[3], [fixed(*bias.shape), col...  7.14 us
    pallas_call x1, Pallas kernels, forward_own(): over_heads(own_kernel, heads, PER[1], [rows, rows, rows], [heads_of(HEAD,...  6.87 us
    pallas_call x1, Pallas kernels, forward_near(): over_heads(forward_near_kernel, heads, PER[2], [SMEM, rows, rows, near, n...  6.7 us
  transfers between devices with their start and end apart: 17, of which 8 were waited for; matrix products, arithmetic and copies ran while one was open for 6% of the time, Pallas kernels for 25%

profile of v2, /device:TPU:73, one launch (start us, length us, event | category | flops | bytes accessed | tf_op | source)
XLA Modules:
  0.0 172.0 jit_solution(11708051277435452060)
XLA Ops:
  0.6 3.0 %prepare.1 = (bf16[2,256,1024]{2,1,0:T(8,128)(2,1)}, bf16[2,256,1024]{2,1,0:T(8,128)(2,1)}, bf16[8,64,1024]{2,1,0:T(8,128)(2,1)}) custom-call(bf16[512,1024]{1,0:T(8,128)(2,1)} %bitcast.66, bf16[512,1024]{1,0:T(8,128)(2,1)} %bitcast.69), custom_call_target="tpu_custom_call" | custom-call | flops 1 | bytes 1 | tf_op jit(solution)/shard_map/prepare/pallas_call | solution.py:104
  3.6 5.4 %all-to-all-start = ((bf16[8,64,1024]{2,1,0:T(8,128)(2,1)}), bf16[8,64,1024]{2,1,0:T(8,128)(2,1)S(1)}, u32[]{:S(2)}, u32[]{:S(2)}) async-start(bf16[8,64,1024]{2,1,0:T(8,128)(2,1)} %get-tuple-element.45), calls=%async_computation | async-start | bytes 2097152 | tf_op jit(solution)/shard_map/all_to_all | solution.py:391
  9.0 6.9 %forward_own.1 = (f32[8,128,512]{2,1,0:T(8,128)}, f32[8,2,512]{2,1,0:T(2,128)}) custom-call(bf16[512,1024]{1,0:T(8,128)(2,1)} %bitcast.60, bf16[512,1024]{1,0:T(8,128)(2,1)} %bitcast.67, bf16[512,1024]{1,0:T(8,128)(2,1)} %bitcast.70), custom_call_target="tpu_custom_call" | custom-call | flops 1 | bytes 1 | tf_op jit(solution)/shard_map/forward_own/pallas_call | solution.py:150
  15.9 8.0 %all-to-all-done.refs_2_.refs_3_ = bf16[8,64,1024]{2,1,0:T(8,128)(2,1)S(1)} async-done(((bf16[8,64,1024]{2,1,0:T(8,128)(2,1)}), bf16[8,64,1024]{2,1,0:T(8,128)(2,1)S(1)}, u32[]{:S(2)}, u32[]{:S(2)}) %all-to-all-start) | async-done | bytes 1048608 | tf_op jit(solution)/shard_map/all_to_all | solution.py:391
  23.9 0.4 convert_reduce_fusion
  24.3 3.4 %collective-permute-start = (bf16[32,1024]{1,0:T(8,128)(2,1)S(1)}, bf16[32,1024]{1,0:T(8,128)(2,1)S(1)}, u32[]{:S(2)}, u32[]{:S(2)}) collective-permute-start(bf16[32,1024]{1,0:T(8,128)(2,1)S(1)} %multiply_convert_fusion), channel_id=1, source_target_pairs={{0,64},{8,72},{16,80},{24,88},{32,96},{40,104},{48,112},{56,120},{... | collective-permute-start | bytes 196616 | tf_op jit(solution)/shard_map/ppermute | solution.py:442
  27.7 1.0 collective-permute-start.1
  28.7 2.3 %collective-permute-start.2 = (bf16[32,1024]{1,0:T(8,128)(2,1)S(1)}, bf16[32,1024]{1,0:T(8,128)(2,1)S(1)}, u32[]{:S(2)}, u32[]{:S(2)}) collective-permute-start(bf16[32,1024]{1,0:T(8,128)(2,1)S(1)} %multiply_convert_fusion), channel_id=1, source_target_pairs={{0,192},{8,200},{16,208},{24,216},{32,224},{40,232},{48,240},{56,2... | collective-permute-start | bytes 196616 | tf_op jit(solution)/shard_map/ppermute | solution.py:442
  31.0 0.0 copy-done.4
  31.0 3.5 %convolution_convert_fusion.refs_2_.refs_4_ = bf16[512,1024]{1,0:T(8,128)(2,1)} fusion(bf16[512,1024]{1,0:T(8,128)(2,1)} %bitcast.76, bf16[1024,1024]{1,0:T(8,128)(2,1)S(1)} %copy-done.4), kind=kOutput, calls=%fused_computation.2 | convolution fusion | flops 1074266112 | bytes 4194304 | tf_op jit(solution)/shard_map/dot_general | solution.py:25
  34.5 0.0 copy-done
  34.5 0.0 collective-permute-done
  34.5 2.4 %collective-permute-done.1 = bf16[32,1024]{1,0:T(8,128)(2,1)S(1)} collective-permute-done((bf16[32,1024]{1,0:T(8,128)(2,1)S(1)}, bf16[32,1024]{1,0:T(8,128)(2,1)S(1)}, u32[]{:S(2)}, u32[]{:S(2)}) %collective-permute-start.1) | collective-permute-done | bytes 65568 | tf_op jit(solution)/shard_map/ppermute | solution.py:442
  36.8 0.0 collective-permute-done.2
  36.9 1.9 %collective-permute-start.3 = (bf16[2,256,1024]{2,1,0:T(8,128)(2,1)}, bf16[2,256,1024]{2,1,0:T(8,128)(2,1)S(1)}, u32[]{:S(2)}, u32[]{:S(2)}) collective-permute-start(bf16[2,256,1024]{2,1,0:T(8,128)(2,1)} %get-tuple-element.51), channel_id=1, source_target_pairs={{0,8},{8,16},{16,24},{24,32},{32,40},{40,48},{48,56},{56,64},{64,7... | collective-permute-start | bytes 3145736 | tf_op jit(solution)/shard_map/ppermute | solution.py:445
  38.8 5.5 %collective-permute-start.4 = (bf16[2,256,1024]{2,1,0:T(8,128)(2,1)}, bf16[2,256,1024]{2,1,0:T(8,128)(2,1)S(1)}, u32[]{:S(2)}, u32[]{:S(2)}) collective-permute-start(bf16[2,256,1024]{2,1,0:T(8,128)(2,1)} %get-tuple-element.52), channel_id=1, source_target_pairs={{8,0},{16,8},{24,16},{32,24},{40,32},{48,40},{56,48},{64,56},{72,6... | collective-permute-start | bytes 3145736 | tf_op jit(solution)/shard_map/ppermute | solution.py:446
  44.3 0.1 compare_and_fusion
  44.4 0.1 abs_compare_fusion
  44.5 0.1 copy.14
  44.6 0.4 broadcast_in_dim.35
  45.0 0.9 copy.18
  46.0 0.6 add_select_fusion.1.refs_0_
  46.6 0.7 pad_maximum_fusion.1.refs_3_.refs_4_
  47.3 7.1 %forward_coarse.1 = (f32[8,128,512]{2,1,0:T(8,128)}, f32[8,2,512]{2,1,0:T(2,128)}) custom-call(f32[320,512]{1,0:T(8,128)} %bitcast.72, bf16[512,1024]{1,0:T(8,128)(2,1)} %bitcast.61, bf16[8,64,1024]{2,1,0:T(8,128)(2,1)} %copy-done, bf16[4,32,1024]{2,1,0:T(8,128)(2,1)} %pad_maximum_fusion.1.refs_3_.refs_4_, f32[8,128,512]{2,1,0:T(8,128)} %get-tuple-element.46.refs_4_, ...), custom_call_target="tpu_custom_call" | custom-call | flops 1 | bytes 1 | tf_op jit(solution)/shard_map/forward_coarse/pallas_call | solution.py:190
  54.5 9.0 %collective-permute-done.3.refs_3_.refs_5_ = bf16[2,256,1024]{2,1,0:T(8,128)(2,1)S(1)} collective-permute-done((bf16[2,256,1024]{2,1,0:T(8,128)(2,1)}, bf16[2,256,1024]{2,1,0:T(8,128)(2,1)S(1)}, u32[]{:S(2)}, u32[]{:S(2)}) %collective-permute-start.3) | collective-permute-done | bytes 1048608 | tf_op jit(solution)/shard_map/ppermute | solution.py:445
  63.5 1.0 collective-permute-done.4.refs_4_.refs_6_
  64.5 1.0 copy-done.3
  65.4 6.7 %forward_near.1 = (bf16[512,1024]{1,0:T(8,128)(2,1)}, bf16[1024,512]{1,0:T(8,128)(2,1)}, f32[8,2,512]{2,1,0:T(2,128)}) custom-call(f32[2]{0:T(128)} %add_select_fusion.1.refs_0_, bf16[512,1024]{1,0:T(8,128)(2,1)} %bitcast.62, bf16[512,1024]{1,0:T(8,128)(2,1)} %convolution_convert_fusion.refs_2_.refs_4_, bf16[2,256,1024]{2,1,0:T(8,128)(2,1)} %copy-done.2, ...), custom_call_target="tpu_custom_call" | custom-call | flops 1 | bytes 1 | tf_op jit(solution)/shard_map/forward_near/pallas_call | solution.py:219
  72.1 3.8 %weight_terms.1 = (bf16[4,1024,128]{2,1,0:T(8,128)(2,1)}, bf16[4,1024,128]{2,1,0:T(8,128)(2,1)}) custom-call(s32[1]{0:T(128)} %bitcast.12.refs_0_, bf16[1024,512]{1,0:T(8,128)(2,1)} %get-tuple-element.64.refs_1_, bf16[512,1024]{1,0:T(8,128)(2,1)} %bitcast.77), custom_call_target="tpu_custom_call" | custom-call | flops 1 | bytes 1 | tf_op jit(solution)/shard_map/weight_terms/pallas_call | solution.py:245
  76.0 3.5 %collective-permute-start.5 = (bf16[4,1024,128]{2,1,0:T(8,128)(2,1)}, bf16[4,1024,128]{2,1,0:T(8,128)(2,1)}, u32[]{:S(2)}, u32[]{:S(2)}) collective-permute-start(bf16[4,1024,128]{2,1,0:T(8,128)(2,1)} %get-tuple-element.66), channel_id=1, source_target_pairs={{0,1},{1,0},{2,3},{3,2},{4,5},{5,4},{6,7},{7,6},{8,9},{9,8},{10,11... | collective-permute-start | bytes 3145736 | tf_op jit(solution)/shard_map/ppermute | solution.py:454
  79.4 10.8 %backward_fine.1 = (f32[8,128,512]{2,1,0:T(8,128)}, f32[2,512,1024]{2,1,0:T(8,128)}, bf16[2,256,1024]{2,1,0:T(8,128)(2,1)}, bf16[2,256,1024]{2,1,0:T(8,128)(2,1)}) custom-call(f32[2]{0:T(128)} %add_select_fusion.1.refs_0_, bf16[512,1024]{1,0:T(8,128)(2,1)} %bitcast.63, bf16[512,1024]{1,0:T(8,128)(2,1)} %bitcast.68, bf16[512,1024]{1,0:T(8,128)(2,1)} %bitcast.71, ...), custom_call_target="tpu_custom_call" | custom-call | flops 1 | bytes 1 | tf_op jit(solution)/shard_map/backward_fine/pallas_call | solution.py:323
  90.2 1.9 %collective-permute-start.6 = (bf16[2,256,1024]{2,1,0:T(8,128)(2,1)}, bf16[2,256,1024]{2,1,0:T(8,128)(2,1)S(1)}, u32[]{:S(2)}, u32[]{:S(2)}) collective-permute-start(bf16[2,256,1024]{2,1,0:T(8,128)(2,1)} %get-tuple-element.75), channel_id=1, source_target_pairs={{0,8},{8,16},{16,24},{24,32},{32,40},{40,48},{48,56},{56,64},{64,7... | collective-permute-start | bytes 3145736 | tf_op jit(solution)/shard_map/ppermute | solution.py:471
  92.1 6.1 %collective-permute-start.7 = (bf16[2,256,1024]{2,1,0:T(8,128)(2,1)}, bf16[2,256,1024]{2,1,0:T(8,128)(2,1)S(1)}, u32[]{:S(2)}, u32[]{:S(2)}) collective-permute-start(bf16[2,256,1024]{2,1,0:T(8,128)(2,1)} %get-tuple-element.76), channel_id=1, source_target_pairs={{8,0},{16,8},{24,16},{32,24},{40,32},{48,40},{56,48},{64,56},{72,6... | collective-permute-start | bytes 3145736 | tf_op jit(solution)/shard_map/ppermute | solution.py:470
  98.3 0.0 collective-permute-done.5
  98.3 1.5 fusion.3
  99.8 1.4 collective-permute-start.8
  101.2 1.0 collective-permute-start.9
  102.2 1.8 %collective-permute-start.10 = (bf16[1024,128]{1,0:T(8,128)(2,1)S(1)}, bf16[1024,128]{1,0:T(8,128)(2,1)S(1)}, u32[]{:S(2)}, u32[]{:S(2)}) collective-permute-start(bf16[1024,128]{1,0:T(8,128)(2,1)S(1)} %get-tuple-element.85), channel_id=1, source_target_pairs={{0,6},{1,7},{2,0},{3,1},{4,2},{5,3},{6,4},{7,5},{8,14},{9,15},{10,... | collective-permute-start | bytes 786440 | tf_op jit(solution)/shard_map/ppermute | solution.py:466
  104.0 8.1 %backward_coarse.1 = (bf16[512,1024]{1,0:T(8,128)(2,1)}, bf16[8,8,64,128]{3,2,1,0:T(8,128)(2,1)}, bf16[8,8,16,128]{3,2,1,0:T(8,128)(2,1)}) custom-call(f32[320,512]{1,0:T(8,128)} %bitcast.73, bf16[512,1024]{1,0:T(8,128)(2,1)} %bitcast.64, bf16[512,1024]{1,0:T(8,128)(2,1)} %convolution_convert_fusion.refs_2_.refs_4_, bf16[8,64,1024]{2,1,0:T(8,128)(2,1)} %copy-done, ...), custom_call_target="tpu_custom_call" | custom-call | flops 1 | bytes 1 | tf_op jit(solution)/shard_map/backward_coarse/pallas_call | solution.py:282
  112.1 0.0 copy-start.9
  112.1 4.9 %project.1 = bf16[512,1024]{1,0:T(8,128)(2,1)} custom-call(bf16[512,1024]{1,0:T(8,128)(2,1)} %get-tuple-element.74.refs_0_, bf16[1024,1024]{1,0:T(8,128)(2,1)} %refs_1_.1), custom_call_target="tpu_custom_call" | custom-call | flops 1 | bytes 1 | tf_op jit(solution)/shard_map/project/pallas_call | solution.py:347
  117.0 0.0 collective-permute-done.8
  117.0 0.0 collective-permute-done.9
  117.0 0.0 collective-permute-done.10
  117.0 0.1 add_convert_fusion
  117.2 1.3 pad_maximum_fusion
  118.4 1.6 collective-permute-done.6.refs_1_
  120.0 1.1 collective-permute-done.7.refs_2_
  121.1 1.0 copy-done.6
  122.1 6.4 %all-to-all-start.1 = ((bf16[8,768,128]{2,1,0:T(8,128)(2,1)}), bf16[8,768,128]{2,1,0:T(8,128)(2,1)S(1)}, u32[]{:S(2)}, u32[]{:S(2)}) async-start(bf16[8,768,128]{2,1,0:T(8,128)(2,1)} %pad_maximum_fusion), calls=%async_computation.1 | async-start | bytes 3145728 | tf_op jit(solution)/shard_map/all_to_all | solution.py:391
  128.5 20.5 %all-to-all-done.1.refs_3_ = bf16[8,768,128]{2,1,0:T(8,128)(2,1)S(1)} async-done(((bf16[8,768,128]{2,1,0:T(8,128)(2,1)}), bf16[8,768,128]{2,1,0:T(8,128)(2,1)S(1)}, u32[]{:S(2)}, u32[]{:S(2)}) %all-to-all-start.1) | async-done | bytes 1572896 | tf_op jit(solution)/shard_map/all_to_all | solution.py:391
  149.0 0.1 slice_reduce_fusion
  149.1 3.1 %collective-permute-start.13 = (bf16[64,128]{1,0:T(8,128)(2,1)S(1)}, bf16[64,128]{1,0:T(8,128)(2,1)S(1)}, u32[]{:S(2)}, u32[]{:S(2)}) collective-permute-start(bf16[64,128]{1,0:T(8,128)(2,1)S(1)} %pad_maximum_fusion.4), channel_id=1, source_target_pairs={{192,0},{200,8},{208,16},{216,24},{224,32},{232,40},{240,48},{248,... | collective-permute-start | bytes 49160 | tf_op jit(solution)/shard_map/ppermute | solution.py:494
  152.2 0.6 collective-permute-start.12
  152.8 1.6 collective-permute-start.11
  154.4 0.0 collective-permute-done.13
  154.4 4.3 %collective-permute-done.12 = bf16[64,128]{1,0:T(8,128)(2,1)S(1)} collective-permute-done((bf16[64,128]{1,0:T(8,128)(2,1)S(1)}, bf16[64,128]{1,0:T(8,128)(2,1)S(1)}, u32[]{:S(2)}, u32[]{:S(2)}) %collective-permute-start.12) | collective-permute-done | bytes 16416 | tf_op jit(solution)/shard_map/ppermute | solution.py:494
  158.7 0.0 collective-permute-done.11
  158.7 0.6 broadcast_in_dim.40
  159.4 6.8 %all-to-all-start.2 = ((bf16[8,32,128]{2,1,0:T(8,128)(2,1)}), bf16[8,32,128]{2,1,0:T(8,128)(2,1)S(1)}, u32[]{:S(2)}, u32[]{:S(2)}) async-start(bf16[8,32,128]{2,1,0:T(8,128)(2,1)} %broadcast_in_dim.40), calls=%async_computation.2 | async-start | bytes 131072 | tf_op jit(solution)/shard_map/all_to_all | solution.py:391
  166.2 0.6 slice.48
  166.8 4.5 %finish.1 = (bf16[512,1024]{1,0:T(8,128)(2,1)}, bf16[512,1024]{1,0:T(8,128)(2,1)}) custom-call(f32[2,512,1024]{2,1,0:T(8,128)} %get-tuple-element.69.refs_0_, bf16[2,256,1024]{2,1,0:T(8,128)(2,1)} %copy-done.5, bf16[2,256,1024]{2,1,0:T(8,128)(2,1)} %copy-done.6, bf16[8,768,128]{2,1,0:T(8,128)(2,1)} %copy-done.1, f32[8,4,128]{2,1,0:T(4,128)} %bitcast.85), custom_call_target="tpu_custom_call" | custom-call | flops 1 | bytes 1 | tf_op jit(solution)/shard_map/finish/pallas_call | solution.py:376
  171.3 0.0 all-to-all-done.2
  171.3 0.7 copy_bitcast_fusion
  (30 shorter events, 0.2 us)
Async XLA Ops:
  3.6 20.3 %all-to-all-start = ((bf16[8,64,1024]{2,1,0:T(8,128)(2,1)}), bf16[8,64,1024]{2,1,0:T(8,128)(2,1)S(1)}, u32[]{:S(2)}, u32[]{:S(2)}) async-start(bf16[8,64,1024]{2,1,0:T(8,128)(2,1)} %get-tuple-element.45), calls=%async_computation | async-start | bytes 2097152 | tf_op jit(solution)/shard_map/all_to_all | solution.py:391
  9.0 22.0 %copy-start.4 = (bf16[1024,1024]{1,0:T(8,128)(2,1)S(1)}, bf16[1024,1024]{1,0:T(8,128)(2,1)}, u32[]{:S(2)}) copy-start(bf16[1024,1024]{1,0:T(8,128)(2,1)} %refs_1_.1) | copy-start | bytes 6291460
  23.9 10.6 %copy-start = (bf16[8,64,1024]{2,1,0:T(8,128)(2,1)}, bf16[8,64,1024]{2,1,0:T(8,128)(2,1)S(1)}, u32[]{:S(2)}) copy-start(bf16[8,64,1024]{2,1,0:T(8,128)(2,1)S(1)} %all-to-all-done.refs_2_.refs_3_) | copy-start | bytes 3145732
  24.3 10.1 %collective-permute-start = (bf16[32,1024]{1,0:T(8,128)(2,1)S(1)}, bf16[32,1024]{1,0:T(8,128)(2,1)S(1)}, u32[]{:S(2)}, u32[]{:S(2)}) collective-permute-start(bf16[32,1024]{1,0:T(8,128)(2,1)S(1)} %multiply_convert_fusion), channel_id=1, source_target_pairs={{0,64},{8,72},{16,80},{24,88},{32,96},{40,104},{48,112},{56,120},{... | collective-permute-start | bytes 196616 | tf_op jit(solution)/shard_map/ppermute | solution.py:442
  27.7 9.1 %collective-permute-start.1 = (bf16[32,1024]{1,0:T(8,128)(2,1)S(1)}, bf16[32,1024]{1,0:T(8,128)(2,1)S(1)}, u32[]{:S(2)}, u32[]{:S(2)}) collective-permute-start(bf16[32,1024]{1,0:T(8,128)(2,1)S(1)} %multiply_convert_fusion), channel_id=1, source_target_pairs={{0,128},{8,136},{16,144},{24,152},{32,160},{40,168},{48,176},{56,1... | collective-permute-start | bytes 196616 | tf_op jit(solution)/shard_map/ppermute | solution.py:442
  28.7 8.1 %collective-permute-start.2 = (bf16[32,1024]{1,0:T(8,128)(2,1)S(1)}, bf16[32,1024]{1,0:T(8,128)(2,1)S(1)}, u32[]{:S(2)}, u32[]{:S(2)}) collective-permute-start(bf16[32,1024]{1,0:T(8,128)(2,1)S(1)} %multiply_convert_fusion), channel_id=1, source_target_pairs={{0,192},{8,200},{16,208},{24,216},{32,224},{40,232},{48,240},{56,2... | collective-permute-start | bytes 196616 | tf_op jit(solution)/shard_map/ppermute | solution.py:442
  36.9 26.6 %collective-permute-start.3 = (bf16[2,256,1024]{2,1,0:T(8,128)(2,1)}, bf16[2,256,1024]{2,1,0:T(8,128)(2,1)S(1)}, u32[]{:S(2)}, u32[]{:S(2)}) collective-permute-start(bf16[2,256,1024]{2,1,0:T(8,128)(2,1)} %get-tuple-element.51), channel_id=1, source_target_pairs={{0,8},{8,16},{16,24},{24,32},{32,40},{40,48},{48,56},{56,64},{64,7... | collective-permute-start | bytes 3145736 | tf_op jit(solution)/shard_map/ppermute | solution.py:445
  38.8 25.7 %collective-permute-start.4 = (bf16[2,256,1024]{2,1,0:T(8,128)(2,1)}, bf16[2,256,1024]{2,1,0:T(8,128)(2,1)S(1)}, u32[]{:S(2)}, u32[]{:S(2)}) collective-permute-start(bf16[2,256,1024]{2,1,0:T(8,128)(2,1)} %get-tuple-element.52), channel_id=1, source_target_pairs={{8,0},{16,8},{24,16},{32,24},{40,32},{48,40},{56,48},{64,56},{72,6... | collective-permute-start | bytes 3145736 | tf_op jit(solution)/shard_map/ppermute | solution.py:446
  63.5 1.0 copy-start.2
  64.5 1.0 copy-start.3
  76.0 22.4 %collective-permute-start.5 = (bf16[4,1024,128]{2,1,0:T(8,128)(2,1)}, bf16[4,1024,128]{2,1,0:T(8,128)(2,1)}, u32[]{:S(2)}, u32[]{:S(2)}) collective-permute-start(bf16[4,1024,128]{2,1,0:T(8,128)(2,1)} %get-tuple-element.66), channel_id=1, source_target_pairs={{0,1},{1,0},{2,3},{3,2},{4,5},{5,4},{6,7},{7,6},{8,9},{9,8},{10,11... | collective-permute-start | bytes 3145736 | tf_op jit(solution)/shard_map/ppermute | solution.py:454
  79.4 18.9 %copy-start.8 = (bf16[4,1024,128]{2,1,0:T(8,128)(2,1)S(1)}, bf16[4,1024,128]{2,1,0:T(8,128)(2,1)}, u32[]{:S(2)}) copy-start(bf16[4,1024,128]{2,1,0:T(8,128)(2,1)} %get-tuple-element.65) | copy-start | bytes 3145732
  90.2 29.8 %collective-permute-start.6 = (bf16[2,256,1024]{2,1,0:T(8,128)(2,1)}, bf16[2,256,1024]{2,1,0:T(8,128)(2,1)S(1)}, u32[]{:S(2)}, u32[]{:S(2)}) collective-permute-start(bf16[2,256,1024]{2,1,0:T(8,128)(2,1)} %get-tuple-element.75), channel_id=1, source_target_pairs={{0,8},{8,16},{16,24},{24,32},{32,40},{40,48},{48,56},{56,64},{64,7... | collective-permute-start | bytes 3145736 | tf_op jit(solution)/shard_map/ppermute | solution.py:471
  92.1 29.0 %collective-permute-start.7 = (bf16[2,256,1024]{2,1,0:T(8,128)(2,1)}, bf16[2,256,1024]{2,1,0:T(8,128)(2,1)S(1)}, u32[]{:S(2)}, u32[]{:S(2)}) collective-permute-start(bf16[2,256,1024]{2,1,0:T(8,128)(2,1)} %get-tuple-element.76), channel_id=1, source_target_pairs={{8,0},{16,8},{24,16},{32,24},{40,32},{48,40},{56,48},{64,56},{72,6... | collective-permute-start | bytes 3145736 | tf_op jit(solution)/shard_map/ppermute | solution.py:470
  99.8 17.1 %collective-permute-start.8 = (bf16[1024,128]{1,0:T(8,128)(2,1)S(1)}, bf16[1024,128]{1,0:T(8,128)(2,1)S(1)}, u32[]{:S(2)}, u32[]{:S(2)}) collective-permute-start(bf16[1024,128]{1,0:T(8,128)(2,1)S(1)} %get-tuple-element.87), channel_id=1, source_target_pairs={{0,2},{1,3},{2,4},{3,5},{4,6},{5,7},{6,0},{7,1},{8,10},{9,11},{10,... | collective-permute-start | bytes 786440 | tf_op jit(solution)/shard_map/ppermute | solution.py:466
  101.2 15.8 %collective-permute-start.9 = (bf16[1024,128]{1,0:T(8,128)(2,1)S(1)}, bf16[1024,128]{1,0:T(8,128)(2,1)S(1)}, u32[]{:S(2)}, u32[]{:S(2)}) collective-permute-start(bf16[1024,128]{1,0:T(8,128)(2,1)S(1)} %get-tuple-element.86), channel_id=1, source_target_pairs={{0,4},{1,5},{2,6},{3,7},{4,0},{5,1},{6,2},{7,3},{8,12},{9,13},{10,... | collective-permute-start | bytes 786440 | tf_op jit(solution)/shard_map/ppermute | solution.py:466
  102.2 14.8 %collective-permute-start.10 = (bf16[1024,128]{1,0:T(8,128)(2,1)S(1)}, bf16[1024,128]{1,0:T(8,128)(2,1)S(1)}, u32[]{:S(2)}, u32[]{:S(2)}) collective-permute-start(bf16[1024,128]{1,0:T(8,128)(2,1)S(1)} %get-tuple-element.85), channel_id=1, source_target_pairs={{0,6},{1,7},{2,0},{3,1},{4,2},{5,3},{6,4},{7,5},{8,14},{9,15},{10,... | collective-permute-start | bytes 786440 | tf_op jit(solution)/shard_map/ppermute | solution.py:466
  112.1 5.1 %copy-start.7 = (bf16[8,8,64,128]{3,2,1,0:T(8,128)(2,1)S(1)}, bf16[8,8,64,128]{3,2,1,0:T(8,128)(2,1)}, u32[]{:S(2)}) copy-start(bf16[8,8,64,128]{3,2,1,0:T(8,128)(2,1)} %get-tuple-element.77) | copy-start | bytes 3145732
  112.1 5.1 %copy-start.9 = (bf16[8,8,16,128]{3,2,1,0:T(8,128)(2,1)S(1)}, bf16[8,8,16,128]{3,2,1,0:T(8,128)(2,1)}, u32[]{:S(2)}) copy-start(bf16[8,8,16,128]{3,2,1,0:T(8,128)(2,1)} %get-tuple-element.78) | copy-start | bytes 786436
  120.0 32.2 %copy-start.5 = (bf16[2,256,1024]{2,1,0:T(8,128)(2,1)}, bf16[2,256,1024]{2,1,0:T(8,128)(2,1)S(1)}, u32[]{:S(2)}) copy-start(bf16[2,256,1024]{2,1,0:T(8,128)(2,1)S(1)} %collective-permute-done.6.refs_1_) | copy-start | bytes 3145732
  121.1 1.0 copy-start.6
  122.1 26.9 %all-to-all-start.1 = ((bf16[8,768,128]{2,1,0:T(8,128)(2,1)}), bf16[8,768,128]{2,1,0:T(8,128)(2,1)S(1)}, u32[]{:S(2)}, u32[]{:S(2)}) async-start(bf16[8,768,128]{2,1,0:T(8,128)(2,1)} %pad_maximum_fusion), calls=%async_computation.1 | async-start | bytes 3145728 | tf_op jit(solution)/shard_map/all_to_all | solution.py:391
  149.0 17.8 %copy-start.1 = (bf16[8,768,128]{2,1,0:T(8,128)(2,1)}, bf16[8,768,128]{2,1,0:T(8,128)(2,1)S(1)}, u32[]{:S(2)}) copy-start(bf16[8,768,128]{2,1,0:T(8,128)(2,1)S(1)} %all-to-all-done.1.refs_3_) | copy-start | bytes 4718596
  149.1 5.3 %collective-permute-start.13 = (bf16[64,128]{1,0:T(8,128)(2,1)S(1)}, bf16[64,128]{1,0:T(8,128)(2,1)S(1)}, u32[]{:S(2)}, u32[]{:S(2)}) collective-permute-start(bf16[64,128]{1,0:T(8,128)(2,1)S(1)} %pad_maximum_fusion.4), channel_id=1, source_target_pairs={{192,0},{200,8},{208,16},{216,24},{224,32},{232,40},{240,48},{248,... | collective-permute-start | bytes 49160 | tf_op jit(solution)/shard_map/ppermute | solution.py:494
  152.2 6.5 %collective-permute-start.12 = (bf16[64,128]{1,0:T(8,128)(2,1)S(1)}, bf16[64,128]{1,0:T(8,128)(2,1)S(1)}, u32[]{:S(2)}, u32[]{:S(2)}) collective-permute-start(bf16[64,128]{1,0:T(8,128)(2,1)S(1)} %pad_maximum_fusion.3), channel_id=1, source_target_pairs={{128,0},{136,8},{144,16},{152,24},{160,32},{168,40},{176,48},{184,... | collective-permute-start | bytes 49160 | tf_op jit(solution)/shard_map/ppermute | solution.py:494
  152.8 5.9 %collective-permute-start.11 = (bf16[64,128]{1,0:T(8,128)(2,1)S(1)}, bf16[64,128]{1,0:T(8,128)(2,1)S(1)}, u32[]{:S(2)}, u32[]{:S(2)}) collective-permute-start(bf16[64,128]{1,0:T(8,128)(2,1)S(1)} %pad_maximum_fusion.2), channel_id=1, source_target_pairs={{64,0},{72,8},{80,16},{88,24},{96,32},{104,40},{112,48},{120,56},{... | collective-permute-start | bytes 49160 | tf_op jit(solution)/shard_map/ppermute | solution.py:494
  159.4 12.0 %all-to-all-start.2 = ((bf16[8,32,128]{2,1,0:T(8,128)(2,1)}), bf16[8,32,128]{2,1,0:T(8,128)(2,1)S(1)}, u32[]{:S(2)}, u32[]{:S(2)}) async-start(bf16[8,32,128]{2,1,0:T(8,128)(2,1)} %broadcast_in_dim.40), calls=%async_computation.2 | async-start | bytes 131072 | tf_op jit(solution)/shard_map/all_to_all | solution.py:391

commit v3 on v2

--- a/solution.py
+++ b/solution.py
@@ -81,19 +81,25 @@
     )
 
 
-def prepare_kernel(k_ref, v_ref, last_ref, first_ref, one_ref):
+def pooling(count, rows):
+    row = lax.broadcasted_iota(jnp.int32, (count, rows), 0)
+    at = lax.broadcasted_iota(jnp.int32, (count, rows), 1)
+    return (at // POOL == row).astype(BF16)
+
+
+def prepare_kernel(k_ref, v_ref, last_ref, first_ref, one_ref, two_ref):
     tokens = k_ref.shape[0]
     count = tokens // POOL
-    row = lax.broadcasted_iota(jnp.int32, (count, tokens), 0)
-    at = lax.broadcasted_iota(jnp.int32, (count, tokens), 1)
-    member = (at // POOL == row).astype(BF16)
+    tops = []
     for which, ref in enumerate((k_ref, v_ref)):
         rows = ref[...]
         last_ref[which] = rows[tokens - BLOCK :]
         first_ref[which] = rows[:BLOCK]
-        one = (dot(member, rows, 1, 0) * SCALE).astype(BF16)
+        one = (dot(pooling(count, tokens), rows, 1, 0) * SCALE).astype(BF16)
         for slot in range(GROUP):
             one_ref[slot, which * count : (which + 1) * count] = one
+        tops.append(dot(pooling(8, count), one, 1, 0) * SCALE)
+    two_ref[...] = jnp.concatenate(tops, axis=0).astype(BF16)
 
 
 def prepare(k, v):
@@ -106,11 +112,12 @@
         width // step,
         PER[0],
         [rows, rows],
-        [edge, edge, cols(GROUP, 2 * tokens // POOL, width=step)],
+        [edge, edge, cols(GROUP, 2 * tokens // POOL, width=step), cols(16, width=step)],
         [
             shape((2, BLOCK, width), BF16),
             shape((2, BLOCK, width), BF16),
             shape((GROUP, 2 * tokens // POOL, width), BF16),
+            shape((16, width), BF16),
         ],
         "prepare",
     )(k, v)
@@ -161,13 +168,14 @@
 def coarse_rows(one, two):
     half = one.shape[1] // 2
     middle = [one[:, which * half : (which + 1) * half].reshape(-1, HEAD) for which in range(2)]
-    groups, per_group, _ = two.shape
-    count = groups * per_group
-    pairs = per_group // (2 * GROUP)
+    per_member = two.shape[1]
+    count = GROUP * per_member
+    pairs = one.shape[1] // (2 * POOL)
+    groups = per_member // (2 * pairs)
     to = lax.broadcasted_iota(jnp.int32, (count, count), 0)
     at = lax.broadcasted_iota(jnp.int32, (count, count), 1)
-    member = to // (pairs * groups) % GROUP
-    source = to // pairs % groups * per_group + member * 2 * pairs + to // (count // 2) * pairs + to % pairs
+    member = to // (groups * pairs) % GROUP
+    source = member * per_member + to // pairs % groups * 2 * pairs + to // (count // 2) * pairs + to % pairs
     top = dot((at == source).astype(BF16), two[...].reshape(count, HEAD), 1, 0).astype(BF16)
     keys = jnp.concatenate([middle[0], top[: count // 2]], axis=0)
     values = jnp.concatenate([middle[1], top[count // 2 :]], axis=0)
@@ -258,82 +266,92 @@
     return p.astype(BF16), (p * (dprob - stat_ref[0, 1:2])).astype(BF16)
 
 
-def backward_coarse_kernel(bias_ref, q_ref, g_ref, one, two, stat_ref, part_ref, dq_ref, one_ref, two_ref):
+def backward_near_kernel(
+    edge_ref, q_ref, g_ref, before, after, stat_ref, part_ref, sum_ref, dbefore_ref, dafter_ref
+):
+    q, g = q_ref[...], g_ref[...]
+    s = near_scores(edge_ref, before, after, q)
+    dprob = both(dot(before[1], g[:BLOCK], 1, 1), dot(after[1], g[BLOCK:], 1, 1))
+    p, ds = gradients(s, dprob, stat_ref)
+    for side, ref in enumerate((dbefore_ref, dafter_ref)):
+        rows = slice(side * BLOCK, (side + 1) * BLOCK)
+        ref[0] = (dot(ds[:, rows], q[rows], 1, 0) * FACTOR).astype(BF16)
+        ref[1] = dot(p[:, rows], g[rows], 1, 0).astype(BF16)
+    dq = both(dot(before[0], ds[:, :BLOCK], 0, 0), dot(after[0], ds[:, BLOCK:], 0, 0))
+    sum_ref[0] = part_ref[0] + dq
+
+
+def backward_near(edge, q, g, before, after, stat, part):
+    tokens, width = q.shape
+    heads = width // HEAD
+    rows = cols(tokens)
+    near = cols(2, BLOCK)
+    return over_heads(
+        backward_near_kernel,
+        heads,
+        PER[4],
+        [SMEM, rows, rows, near, near, heads_of(2, tokens), heads_of(HEAD, tokens)],
+        [heads_of(HEAD, tokens), near, near],
+        [shape((heads, HEAD, tokens), F32), shape((2, BLOCK, width), BF16), shape((2, BLOCK, width), BF16)],
+        "backward_near",
+    )(edge, q, g, before, after, stat, part)
+
+
+def backward_coarse_kernel(bias_ref, q_ref, g_ref, one, two, stat_ref, sum_ref, out_ref):
+    q, g = q_ref[...], g_ref[...]
     keys, values = coarse_rows(one, two)
-    q, g = q_ref[...], g_ref[...]
     s = dot(keys, q, 1, 1) * LOG2 + bias_ref[...]
     p, ds = gradients(s, dot(values, g, 1, 1), stat_ref)
     dk = dot(ds, q, 1, 0) * FACTOR
     dv = dot(p, g, 1, 0)
-    dq_ref[...] = jnp.transpose((part_ref[0] + dot(keys, ds, 0, 0)) * FACTOR).astype(BF16)
-    slots = one_ref.shape[0]
-    count = slots * (one_ref.shape[2] // 2)
-    for ref, begin, end in ((one_ref, 0, count), (two_ref, count, dk.shape[0])):
-        pieces = [d[begin:end].reshape(slots, -1, HEAD) for d in (dk, dv)]
-        ref[:, 0] = jnp.concatenate(pieces, axis=1).astype(BF16)
-
-
-def backward_coarse(bias, q, g, one, two, stat, part):
+    sum_ref[0] = dot(keys, ds, 0, 0)
+    count = one.shape[0] * (one.shape[1] // 2)
+    pieces = [d.reshape(out_ref.shape[0], -1, HEAD) for d in (dk[:count], dv[:count], dk[count:], dv[count:])]
+    out_ref[:, 0] = jnp.concatenate(pieces, axis=1).astype(BF16)
+
+
+def backward_coarse(bias, q, g, one, two, stat):
     tokens, width = q.shape
     heads = width // HEAD
     rows = cols(tokens)
-    slots = one.shape[0]
-    for_one, for_two = one.shape[1], two.shape[0] * two.shape[1] // slots
+    slots, per_slot = one.shape[0], one.shape[1] + two.shape[1]
     return over_heads(
         backward_coarse_kernel,
         heads,
         PER[5],
         [
             fixed(*bias.shape), rows, rows, cols(*one.shape[:2]), cols(*two.shape[:2]), heads_of(2, tokens),
-            heads_of(HEAD, tokens),
         ],
-        [rows, second(slots, 1, for_one, HEAD), second(slots, 1, for_two, HEAD)],
+        [heads_of(HEAD, tokens), second(slots, 1, per_slot, HEAD)],
         [
-            shape((tokens, width), BF16),
-            shape((slots, heads, for_one, HEAD), BF16),
-            shape((slots, heads, for_two, HEAD), BF16),
+            shape((heads, HEAD, tokens), F32),
+            shape((slots, heads, per_slot, HEAD), BF16),
         ],
         "backward_coarse",
-    )(bias, q, g, one, two, stat, part)
-
-
-def fine_kernel(
-    edge_ref, q_ref, k_ref, v_ref, g_ref, before, after, stat_ref, part_ref, down_ref, dbefore_ref, dafter_ref
-):
+    )(bias, q, g, one, two, stat)
+
+
+def backward_own_kernel(q_ref, k_ref, v_ref, g_ref, stat_ref, part_ref, dq_ref, down_ref):
     q, k, v, g = q_ref[...], k_ref[...], v_ref[...], g_ref[...]
-    s_near = near_scores(edge_ref, before, after, q)
-    dp_near = both(dot(before[1], g[:BLOCK], 1, 1), dot(after[1], g[BLOCK:], 1, 1))
-    p_near, ds_near = gradients(s_near, dp_near, stat_ref)
     p, ds = gradients(dot(k, q, 1, 1) * LOG2, dot(v, g, 1, 1), stat_ref)
     down_ref[0] = dot(ds, q, 1, 0) * FACTOR
     down_ref[1] = dot(p, g, 1, 0)
-    near = both(dot(before[0], ds_near[:, :BLOCK], 0, 0), dot(after[0], ds_near[:, BLOCK:], 0, 0))
-    part_ref[0] = near + dot(k, ds, 0, 0)
-    for side, ref in enumerate((dbefore_ref, dafter_ref)):
-        rows = slice(side * BLOCK, (side + 1) * BLOCK)
-        ref[0] = (dot(ds_near[:, rows], q[rows], 1, 0) * FACTOR).astype(BF16)
-        ref[1] = dot(p_near[:, rows], g[rows], 1, 0).astype(BF16)
-
-
-def backward_fine(edge, q, k, v, g, before, after, stat):
+    dq_ref[...] = jnp.transpose((part_ref[0] + dot(k, ds, 0, 0)) * FACTOR).astype(BF16)
+
+
+def backward_own(q, k, v, g, stat, part):
     tokens, width = q.shape
     heads = width // HEAD
     rows = cols(tokens)
-    near = cols(2, BLOCK)
-    return over_heads(
-        fine_kernel,
+    return over_heads(
+        backward_own_kernel,
         heads,
         PER[4],
-        [SMEM, rows, rows, rows, rows, near, near, heads_of(2, tokens)],
-        [heads_of(HEAD, tokens), cols(2, tokens), near, near],
-        [
-            shape((heads, HEAD, tokens), F32),
-            shape((2, tokens, width), F32),
-            shape((2, BLOCK, width), BF16),
-            shape((2, BLOCK, width), BF16),
-        ],
-        "backward_fine",
-    )(edge, q, k, v, g, before, after, stat)
+        [rows, rows, rows, rows, heads_of(2, tokens), heads_of(HEAD, tokens)],
+        [rows, cols(2, tokens)],
+        [shape((tokens, width), BF16), shape((2, tokens, width), F32)],
+        "backward_own",
+    )(q, k, v, g, stat, part)
 
 
 def project_kernel(attn_ref, weight_ref, out_ref):
@@ -355,36 +373,35 @@
     )(attn, weight)[0]
 
 
-def finish_kernel(own, first, last, one_ref, two_ref, dk_ref, dv_ref):
+def finish_kernel(own, first, last, coarse, two_ref, dk_ref, dv_ref):
     tokens = own.shape[1]
     size = tokens // POOL
-    one = jnp.sum(one_ref[...].astype(F32), axis=0)
+    one = jnp.sum(coarse[:, : 2 * size].astype(F32), axis=0)
     for which, out_ref in enumerate((dk_ref, dv_ref)):
         term = one[which * size : (which + 1) * size] * SCALE
         term = jnp.broadcast_to(term[:, None], (size, POOL, HEAD)).reshape(tokens, HEAD)
         for side, edge in enumerate((first, last)):
-            rows = pl.ds(side * BLOCK, BLOCK)
+            rows = slice(side * BLOCK, (side + 1) * BLOCK)
             at = 2 * which + side
             top = two_ref[0, at : at + 1] * (SCALE * SCALE)
-            total = own[which, rows] + term[side * BLOCK : (side + 1) * BLOCK] + top + edge[which].astype(F32)
-            out_ref[rows, :] = total.astype(BF16)
-
-
-def finish(own, first, last, one, two):
+            out_ref[rows, :] = (own[which, rows] + term[rows] + top + edge[which].astype(F32)).astype(BF16)
+
+
+def finish(own, first, last, coarse, rows, two):
     tokens, width = own.shape[1:]
-    rows = 2 * tokens // POOL
+    heads = width // HEAD
     return over_heads(
         finish_kernel,
-        width // HEAD,
+        heads,
         PER[6],
         [
             cols(2, tokens), cols(2, BLOCK), cols(2, BLOCK),
-            second(one.shape[0], rows, HEAD), heads_of(*two.shape[1:]),
+            second(coarse.shape[0], rows, HEAD), heads_of(*two.shape[1:]),
         ],
         [cols(tokens)] * 2,
         [shape((tokens, width), BF16)] * 2,
         "finish",
-    )(own, first, last, one, two)
+    )(own, first, last, coarse, two)
 
 
 def exchange(x, axis, groups=None):
@@ -399,8 +416,7 @@
     pairs = tokens // BLOCK
     groups = devices // GROUP
     at = jnp.arange(devices * pairs, dtype=jnp.int32)
-    from_group = (group - at // pairs) % groups
-    two = from_group * per_group + at // (pairs * groups) * pairs + at % pairs
+    two = (group - at // pairs) % groups * per_group + at // (pairs * groups) * pairs + at % pairs
     one_ok = jnp.abs(one[None] - block) > 1
     two_ok = (jnp.abs(two[None] - block) > 1) & (two // per_group != group)[None]
     ok = jnp.concatenate([one_ok, two_ok], axis=1)
@@ -432,30 +448,36 @@
     far = [[(i, (i + step * GROUP) % devices) for i in range(devices)] for step in range(groups)]
     back = [[(j, i) for i, j in moves] for moves in far]
 
-    last, first, one = prepare(k, v)
+    last, first, one, two = prepare(k, v)
     one = exchange(one, "ctx", near)
+    two = [two] + [lax.ppermute(two, "ctx", moves) for moves in far[1:]]
+    two = jnp.stack(two).reshape(groups, 2, -1, width)[:, :, :pairs].reshape(-1, width)
+    two = jnp.broadcast_to(two[None], (GROUP,) + two.shape)
     edge, bias = masks(device, devices, tokens)
     acc, stat = forward_own(q, k, v)
     one = after_all(one, acc)
-    two = one.astype(F32).reshape(GROUP * 2 * pairs, POOL, width)
-    two = (jnp.sum(two, axis=1) * SCALE).astype(BF16)
-    two = [two] + [lax.ppermute(two, "ctx", moves) for moves in far[1:]]
-    g = dot(after_all(upstream, two[0]), out_weight, 1, 1).astype(BF16)
-    last, first, two = lax.optimization_barrier((last, first, two, g))[:3]
+    two = after_all(two, one)
+    two = exchange(two, "ctx", near)
+    last, first = lax.optimization_barrier((last, first, two))[:2]
+    g = dot(after_all(upstream, last), out_weight, 1, 1).astype(BF16)
     before = lax.ppermute(last, "ctx", up)
     after = lax.ppermute(first, "ctx", down)
-    two = jnp.stack(two)
-    acc, stat = forward_coarse(bias, after_all(q, last), one, two, acc, stat)
+    acc, stat = forward_coarse(bias, after_all(q, last, g), one, two, acc, stat)
     before, after = lax.optimization_barrier((before, after, acc))[:2]
     attn, across, stat = forward_near(edge, q, g, before, after, acc, stat)
 
+    heads = width // HEAD
+    part, packed = backward_coarse(bias, q, g, one, two, stat)
+    packed = packed.reshape(GROUP, -1, HEAD)
+    g, stat = lax.optimization_barrier((g, stat, packed))[:2]
+    across = after_all(across, packed)
+    packed = exchange(packed, "ctx", near)
     place = lax.axis_index("dp")
-    keep, send = weight_terms((place % 2).reshape(1).astype(jnp.int32), across, upstream)
+    core = (place % 2).reshape(1).astype(jnp.int32)
+    keep, send = weight_terms(core, across, upstream)
     other = lax.ppermute(send, "dp", [(i, i ^ 1) for i in range(dp)])
-    part, d_own, d_before, d_after = backward_fine(
-        edge, q, k, v, g, before, after, after_all(stat, send)
-    )
-    other = after_all(other, d_own)
+    part, d_before, d_after = backward_near(edge, q, g, before, after, after_all(stat, send), part)
+    other, packed = lax.optimization_barrier((other, packed, part))[:2]
     shares = []
     for step in range(dp // 2):
         at = (place // 2 + step) % (dp // 2)
@@ -467,38 +489,33 @@
         for step, share in enumerate(shares)
         if step
     ]
+    d_before, d_after = lax.optimization_barrier((d_before, d_after, packed, *shares))[:2]
     from_after = lax.ppermute(d_before, "ctx", down)
     from_before = lax.ppermute(d_after, "ctx", up)
-    dq, d_one, d_two = backward_coarse(
-        bias, q, lax.optimization_barrier((g, *shares))[0], one, two, stat, part
-    )
+    dq, d_own = backward_own(after_all(q, d_before), k, v, g, stat, part)
     sent = lax.optimization_barrier((dq, *sent))[1:]
     weight = sum((share.astype(F32) for share in sent), shares[0].astype(F32)).astype(BF16)
     weight = weight.reshape(groups, GROUP, -1, HEAD).transpose(1, 0, 2, 3).reshape(GROUP, -1, HEAD)
-
-    heads = width // HEAD
-    d_one, d_two = d_one.reshape(GROUP, -1, HEAD), d_two.reshape(GROUP, -1, HEAD)
-    start, count = d_one.shape[1], d_two.shape[1]
-    mixed = project(after_all(attn, dq), out_weight)
-    packed = jnp.concatenate([d_one, d_two, weight], axis=1)
-    packed = exchange(after_all(packed, from_after, from_before, mixed), "ctx", near)
-    small = jnp.sum(packed[:, start:].astype(F32), axis=0).astype(BF16)
-    weight = small[count:].reshape(groups, -1, HEAD)
-    d_two = small[:count]
-    d_two = d_two.reshape(heads, 2, groups, pairs, HEAD).transpose(2, 0, 1, 3, 4).reshape(groups, -1, HEAD)
+    mixed = project(after_all(attn, weight), out_weight)
+    weight = exchange(weight, "ctx", near)
+    weight = after_all(weight, from_after, from_before, mixed)
+    weight = jnp.sum(weight.astype(F32), axis=0).astype(BF16).reshape(groups, -1, HEAD)
+    d_two = packed.reshape(GROUP, heads, -1, HEAD)[:, :, 2 * rows_one :].astype(F32)
+    d_two = jnp.sum(d_two, axis=0).astype(BF16).reshape(heads, 2, groups, pairs, HEAD)
+    d_two = d_two.transpose(2, 0, 1, 3, 4).reshape(groups, -1, HEAD)
     count = d_two.shape[1]
-    small = []
+    sums = []
     for step, moves in enumerate(back):
         at = (device // GROUP - step) % groups
         piece = jnp.concatenate([d_two[step], lax.dynamic_index_in_dim(weight, at, 0, False)], axis=0)
-        small.append(lax.ppermute(piece, "ctx", moves) if step else piece)
-    small = sum(piece.astype(F32) for piece in small)
-    mine_two = small[:count].reshape(heads, 2 * pairs, HEAD)
-    weight = small[count:].astype(BF16)
+        sums.append(lax.ppermute(piece, "ctx", moves) if step else piece)
+    sums = sum(piece.astype(F32) for piece in sums)
+    mine_two = sums[:count].reshape(heads, 2 * pairs, HEAD)
+    weight = sums[count:].astype(BF16)
     weight = exchange(jnp.broadcast_to(weight[None], (dp,) + weight.shape), "dp")
     grad_weight = jnp.swapaxes(weight, 0, 1).reshape(-1, model).astype(F32)
 
-    grad_keys, grad_values = finish(d_own, from_before, from_after, packed, mine_two)
+    grad_keys, grad_values = finish(d_own, from_before, from_after, packed, packed.shape[1] // heads, mine_two)
     return mixed[None], dq[None], grad_keys[None], grad_values[None], grad_weight
 
 

time: 174 us -> 165 us (0.948)
  waiting for transfers between devices: 47.9 us -> 23.1 us
  starting transfers between devices: 53.5 us -> 66.8 us
  Pallas kernels: 55.8 us -> 60.4 us
  other arithmetic: 5.61 us -> 1.99 us
  local copies, waits for them, and re-layouts: 4.79 us -> 7.03 us
    all_to_all x3 -> x5, waiting for transfers between devices: 28.5 us -> 8.46 us  [exchange(): return lax.all_to_all(x, axis, 0, 0, axis_index_groups=groups, tiled=True)]
    all_to_all x3 -> x5, starting transfers between devices: 18.6 us -> 28.6 us  [exchange(): return lax.all_to_all(x, axis, 0, 0, axis_index_groups=groups, tiled=True)]
    ppermute x1, waiting for transfers between devices: 9 us -> 3.37 us  [on_device(): before = lax.ppermute(last, 'ctx', up)]
    pallas_call x2 -> x3, Pallas kernels: 15.3 us -> 20 us  [the longest x1 8.52 us: backward_own(): over_heads(backward_own_kernel, heads, PER[4], [rows, rows, rows, rows, h...]
    ppermute x3, waiting for transfers between devices: 0.01 us -> 3.06 us  [on_device(): lax.ppermute(share, 'dp', [(i, (i + 2 * step) % dp) for i in range(dp)])]
    ppermute x1, starting transfers between devices: 3.45 us -> 5.38 us  [on_device(): other = lax.ppermute(send, 'dp', [(i, i ^ 1) for i in range(dp)])]
  transfers between devices with their start and end apart: 17 -> 19, of which waited for: 8 -> 8; matrix products, arithmetic and copies ran while one was open for 6% -> 6% of each run, Pallas kernels for 25% -> 26%
where the time goes in v3:
time: 165 us; the launch traced here: 164 us
  starting transfers between devices  66.8 us (40%)
  Pallas kernels  60.4 us (37%)
  waiting for transfers between devices  23.1 us (14%)
  local copies, waits for them, and re-layouts  7.03 us (4%)
  matrix products  3.49 us (2%)
  other arithmetic  1.99 us (1%)
    all_to_all x5, starting transfers between devices, exchange(): return lax.all_to_all(x, axis, 0, 0, axis_index_groups=groups, tiled=True)  28.6 us
    pallas_call x1, Pallas kernels, backward_own(): over_heads(backward_own_kernel, heads, PER[4], [rows, rows, rows, rows, h...  8.52 us
    all_to_all x5, waiting for transfers between devices, exchange(): return lax.all_to_all(x, axis, 0, 0, axis_index_groups=groups, tiled=True)  8.46 us
    ppermute x3, starting transfers between devices, on_device(): two = [two] + [lax.ppermute(two, 'ctx', moves) for moves in far[1:]]  7.86 us
    pallas_call x1, Pallas kernels, backward_coarse(): over_heads(backward_coarse_kernel, heads, PER[5], [fixed(*bias.shape), ro...  7.65 us
    pallas_call x1, Pallas kernels, forward_coarse(): over_heads(forward_coarse_kernel, heads, PER[3], [fixed(*bias.shape), col...  7.13 us
    pallas_call x1, Pallas kernels, backward_near(): over_heads(backward_near_kernel, heads, PER[4], [SMEM, rows, rows, near,...  6.91 us
    pallas_call x1, Pallas kernels, forward_own(): over_heads(own_kernel, heads, PER[1], [rows, rows, rows], [heads_of(HEAD,...  6.72 us
  transfers between devices with their start and end apart: 19, of which 8 were waited for; matrix products, arithmetic and copies ran while one was open for 6% of the time, Pallas kernels for 26%

profile of v3, /device:TPU:73, one launch (start us, length us, event | category | flops | bytes accessed | tf_op | source)
XLA Modules:
  0.0 163.8 jit_solution(6757351794952583299)
XLA Ops:
  0.6 3.6 %prepare.1 = (bf16[2,256,1024]{2,1,0:T(8,128)(2,1)}, bf16[2,256,1024]{2,1,0:T(8,128)(2,1)}, bf16[8,64,1024]{2,1,0:T(8,128)(2,1)}, bf16[16,1024]{1,0:T(8,128)(2,1)}) custom-call(bf16[512,1024]{1,0:T(8,128)(2,1)} %bitcast.64, bf16[512,1024]{1,0:T(8,128)(2,1)} %bitcast.67), custom_call_target="tpu_custom_call" | custom-call | flops 1 | bytes 1 | tf_op jit(solution)/shard_map/prepare/pallas_call | solution.py:110
  4.2 5.5 %all-to-all-start = ((bf16[8,64,1024]{2,1,0:T(8,128)(2,1)}), bf16[8,64,1024]{2,1,0:T(8,128)(2,1)S(1)}, u32[]{:S(2)}, u32[]{:S(2)}) async-start(bf16[8,64,1024]{2,1,0:T(8,128)(2,1)} %get-tuple-element.52), calls=%async_computation | async-start | bytes 2097152 | tf_op jit(solution)/shard_map/all_to_all | solution.py:408
  9.7 0.1 collective-permute-start.2
  9.8 5.4 %collective-permute-start.1 = (bf16[16,1024]{1,0:T(8,128)(2,1)S(1)}, bf16[16,1024]{1,0:T(8,128)(2,1)S(1)}, u32[]{:S(2)}, u32[]{:S(2)}) collective-permute-start(bf16[16,1024]{1,0:T(8,128)(2,1)S(1)} %copy-done.8), channel_id=1, source_target_pairs={{0,128},{8,136},{16,144},{24,152},{32,160},{40,168},{48,176},{56,1... | collective-permute-start | bytes 98312 | tf_op jit(solution)/shard_map/ppermute | solution.py:453
  15.2 2.4 %collective-permute-start = (bf16[16,1024]{1,0:T(8,128)(2,1)S(1)}, bf16[16,1024]{1,0:T(8,128)(2,1)S(1)}, u32[]{:S(2)}, u32[]{:S(2)}) collective-permute-start(bf16[16,1024]{1,0:T(8,128)(2,1)S(1)} %copy-done.8), channel_id=1, source_target_pairs={{0,64},{8,72},{16,80},{24,88},{32,96},{40,104},{48,112},{56,120},{... | collective-permute-start | bytes 98312 | tf_op jit(solution)/shard_map/ppermute | solution.py:453
  17.6 6.7 %forward_own.1 = (f32[8,128,512]{2,1,0:T(8,128)}, f32[8,2,512]{2,1,0:T(2,128)}) custom-call(bf16[512,1024]{1,0:T(8,128)(2,1)} %bitcast.58, bf16[512,1024]{1,0:T(8,128)(2,1)} %bitcast.65, bf16[512,1024]{1,0:T(8,128)(2,1)} %bitcast.68), custom_call_target="tpu_custom_call" | custom-call | flops 1 | bytes 1 | tf_op jit(solution)/shard_map/forward_own/pallas_call | solution.py:157
  24.3 0.0 collective-permute-done.2
  24.3 2.3 %collective-permute-done.1 = bf16[16,1024]{1,0:T(8,128)(2,1)S(1)} collective-permute-done((bf16[16,1024]{1,0:T(8,128)(2,1)S(1)}, bf16[16,1024]{1,0:T(8,128)(2,1)S(1)}, u32[]{:S(2)}, u32[]{:S(2)}) %collective-permute-start.1) | collective-permute-done | bytes 32800 | tf_op jit(solution)/shard_map/ppermute | solution.py:453
  26.6 0.0 collective-permute-done
  26.7 0.0 all-to-all-done.refs_2_.refs_3_
  26.7 0.0 copy-start
  26.7 0.8 broadcast_in_dim.41
  27.5 6.3 %all-to-all-start.1 = ((bf16[8,16,1024]{2,1,0:T(8,128)(2,1)}), bf16[8,16,1024]{2,1,0:T(8,128)(2,1)S(1)}, u32[]{:S(2)}, u32[]{:S(2)}) async-start(bf16[8,16,1024]{2,1,0:T(8,128)(2,1)} %broadcast_in_dim.41), calls=%async_computation.1 | async-start | bytes 524288 | tf_op jit(solution)/shard_map/all_to_all | solution.py:408
  33.9 6.0 %all-to-all-done.1.refs_3_.refs_4_ = bf16[8,16,1024]{2,1,0:T(8,128)(2,1)S(1)} async-done(((bf16[8,16,1024]{2,1,0:T(8,128)(2,1)}), bf16[8,16,1024]{2,1,0:T(8,128)(2,1)S(1)}, u32[]{:S(2)}, u32[]{:S(2)}) %all-to-all-start.1) | async-done | bytes 262176 | tf_op jit(solution)/shard_map/all_to_all | solution.py:408
  39.9 1.9 %collective-permute-start.3 = (bf16[2,256,1024]{2,1,0:T(8,128)(2,1)}, bf16[2,256,1024]{2,1,0:T(8,128)(2,1)S(1)}, u32[]{:S(2)}, u32[]{:S(2)}) collective-permute-start(bf16[2,256,1024]{2,1,0:T(8,128)(2,1)} %get-tuple-element.56), channel_id=1, source_target_pairs={{0,8},{8,16},{16,24},{24,32},{32,40},{40,48},{48,56},{56,64},{64,7... | collective-permute-start | bytes 3145736 | tf_op jit(solution)/shard_map/ppermute | solution.py:463
  41.8 5.5 %collective-permute-start.4 = (bf16[2,256,1024]{2,1,0:T(8,128)(2,1)}, bf16[2,256,1024]{2,1,0:T(8,128)(2,1)S(1)}, u32[]{:S(2)}, u32[]{:S(2)}) collective-permute-start(bf16[2,256,1024]{2,1,0:T(8,128)(2,1)} %get-tuple-element.58), channel_id=1, source_target_pairs={{8,0},{16,8},{24,16},{32,24},{40,32},{48,40},{56,48},{64,56},{72,6... | collective-permute-start | bytes 3145736 | tf_op jit(solution)/shard_map/ppermute | solution.py:464
  47.3 0.1 compare_and_fusion
  47.4 0.1 abs_compare_fusion
  47.5 0.8 copy.23
  48.3 1.5 broadcast_in_dim.44
  49.7 0.9 copy.32
  50.6 0.6 add_select_fusion.1.refs_0_
  51.2 3.5 %convolution_convert_fusion.refs_2_.refs_3_ = bf16[512,1024]{1,0:T(8,128)(2,1)} fusion(bf16[512,1024]{1,0:T(8,128)(2,1)} %bitcast.75, bf16[1024,1024]{1,0:T(8,128)(2,1)S(1)} %copy-done.5), kind=kOutput, calls=%fused_computation | convolution fusion | flops 1074266112 | bytes 4194304 | tf_op jit(solution)/shard_map/dot_general | solution.py:25
  54.7 7.1 %forward_coarse.1 = (f32[8,128,512]{2,1,0:T(8,128)}, f32[8,2,512]{2,1,0:T(2,128)}) custom-call(f32[320,512]{1,0:T(8,128)} %bitcast.71, bf16[512,1024]{1,0:T(8,128)(2,1)} %bitcast.59, bf16[8,64,1024]{2,1,0:T(8,128)(2,1)} %copy-done, bf16[8,16,1024]{2,1,0:T(8,128)(2,1)} %copy-done.4, f32[8,128,512]{2,1,0:T(8,128)} %get-tuple-element.53.refs_4_, ...), custom_call_target="tpu_custom_call" | custom-call | flops 1 | bytes 1 | tf_op jit(solution)/shard_map/forward_coarse/pallas_call | solution.py:198
  61.8 3.4 %collective-permute-done.3.refs_3_ = bf16[2,256,1024]{2,1,0:T(8,128)(2,1)S(1)} collective-permute-done((bf16[2,256,1024]{2,1,0:T(8,128)(2,1)}, bf16[2,256,1024]{2,1,0:T(8,128)(2,1)S(1)}, u32[]{:S(2)}, u32[]{:S(2)}) %collective-permute-start.3) | collective-permute-done | bytes 1048608 | tf_op jit(solution)/shard_map/ppermute | solution.py:463
  65.2 1.0 collective-permute-done.4.refs_4_
  66.2 1.0 copy-done.3
  67.2 6.7 %forward_near.1 = (bf16[512,1024]{1,0:T(8,128)(2,1)}, bf16[1024,512]{1,0:T(8,128)(2,1)}, f32[8,2,512]{2,1,0:T(2,128)}) custom-call(f32[2]{0:T(128)} %add_select_fusion.1.refs_0_, bf16[512,1024]{1,0:T(8,128)(2,1)} %bitcast.60, bf16[512,1024]{1,0:T(8,128)(2,1)} %convolution_convert_fusion.refs_2_.refs_3_, bf16[2,256,1024]{2,1,0:T(8,128)(2,1)} %copy-done.2, ...), custom_call_target="tpu_custom_call" | custom-call | flops 1 | bytes 1 | tf_op jit(solution)/shard_map/forward_near/pallas_call | solution.py:227
  73.8 7.6 %backward_coarse.1 = (f32[8,128,512]{2,1,0:T(8,128)}, bf16[8,8,80,128]{3,2,1,0:T(8,128)(2,1)}) custom-call(f32[320,512]{1,0:T(8,128)} %bitcast.72, bf16[512,1024]{1,0:T(8,128)(2,1)} %bitcast.61, bf16[512,1024]{1,0:T(8,128)(2,1)} %convolution_convert_fusion.refs_2_.refs_3_, bf16[8,64,1024]{2,1,0:T(8,128)(2,1)} %copy-done, bf16[8,16,1024]{2,1,0:T(8,128)(2,1)} %copy-done.4, ...), custom_call_target="tpu_custom_call" | custom-call | flops 1 | bytes 1 | tf_op jit(solution)/shard_map/backward_coarse/pallas_call | solution.py:318
  81.5 4.7 %all-to-all-start.2 = ((bf16[8,640,128]{2,1,0:T(8,128)(2,1)}), bf16[8,640,128]{2,1,0:T(8,128)(2,1)S(1)}, u32[]{:S(2)}, u32[]{:S(2)}) async-start(bf16[8,640,128]{2,1,0:T(8,128)(2,1)} %bitcast.74), calls=%async_computation.2 | async-start | bytes 2621440 | tf_op jit(solution)/shard_map/all_to_all | solution.py:408
  86.2 3.8 %weight_terms.1 = (bf16[4,1024,128]{2,1,0:T(8,128)(2,1)}, bf16[4,1024,128]{2,1,0:T(8,128)(2,1)}) custom-call(s32[1]{0:T(128)} %bitcast.11.refs_0_, bf16[1024,512]{1,0:T(8,128)(2,1)} %get-tuple-element.69.refs_1_, bf16[512,1024]{1,0:T(8,128)(2,1)} %bitcast.76), custom_call_target="tpu_custom_call" | custom-call | flops 1 | bytes 1 | tf_op jit(solution)/shard_map/weight_terms/pallas_call | solution.py:253
  90.0 5.4 %collective-permute-start.5 = (bf16[4,1024,128]{2,1,0:T(8,128)(2,1)}, bf16[4,1024,128]{2,1,0:T(8,128)(2,1)S(1)}, u32[]{:S(2)}, u32[]{:S(2)}) collective-permute-start(bf16[4,1024,128]{2,1,0:T(8,128)(2,1)} %get-tuple-element.71), channel_id=1, source_target_pairs={{0,1},{1,0},{2,3},{3,2},{4,5},{5,4},{6,7},{7,6},{8,9},{9,8},{10,11... | collective-permute-start | bytes 3145736 | tf_op jit(solution)/shard_map/ppermute | solution.py:478
  95.4 6.9 %backward_near.1 = (f32[8,128,512]{2,1,0:T(8,128)}, bf16[2,256,1024]{2,1,0:T(8,128)(2,1)}, bf16[2,256,1024]{2,1,0:T(8,128)(2,1)}) custom-call(f32[2]{0:T(128)} %add_select_fusion.1.refs_0_, bf16[512,1024]{1,0:T(8,128)(2,1)} %bitcast.62, bf16[512,1024]{1,0:T(8,128)(2,1)} %convolution_convert_fusion.refs_2_.refs_3_, bf16[2,256,1024]{2,1,0:T(8,128)(2,1)} %copy-done.2, ...), custom_call_target="tpu_custom_call" | custom-call | flops 1 | bytes 1 | tf_op jit(solution)/shard_map/backward_near/pallas_call | solution.py:289
  102.3 0.0 collective-permute-done.5
  102.3 0.0 all-to-all-done.2.refs_3_
  102.4 0.3 fusion.3
  102.7 3.6 %collective-permute-start.9 = (bf16[2,256,1024]{2,1,0:T(8,128)(2,1)}, bf16[2,256,1024]{2,1,0:T(8,128)(2,1)S(1)}, u32[]{:S(2)}, u32[]{:S(2)}) collective-permute-start(bf16[2,256,1024]{2,1,0:T(8,128)(2,1)} %get-tuple-element.89), channel_id=1, source_target_pairs={{0,8},{8,16},{16,24},{24,32},{32,40},{40,48},{48,56},{56,64},{64,7... | collective-permute-start | bytes 3145736 | tf_op jit(solution)/shard_map/ppermute | solution.py:494
  106.3 4.4 %collective-permute-start.10 = (bf16[2,256,1024]{2,1,0:T(8,128)(2,1)}, bf16[2,256,1024]{2,1,0:T(8,128)(2,1)}, u32[]{:S(2)}, u32[]{:S(2)}) collective-permute-start(bf16[2,256,1024]{2,1,0:T(8,128)(2,1)} %get-tuple-element.81), channel_id=1, source_target_pairs={{8,0},{16,8},{24,16},{32,24},{40,32},{48,40},{56,48},{64,56},{72,6... | collective-permute-start | bytes 3145736 | tf_op jit(solution)/shard_map/ppermute | solution.py:493
  110.7 1.4 collective-permute-start.6
  112.1 1.0 collective-permute-start.7
  113.1 1.8 %collective-permute-start.8 = (bf16[1024,128]{1,0:T(8,128)(2,1)S(1)}, bf16[1024,128]{1,0:T(8,128)(2,1)S(1)}, u32[]{:S(2)}, u32[]{:S(2)}) collective-permute-start(bf16[1024,128]{1,0:T(8,128)(2,1)S(1)} %get-tuple-element.93), channel_id=1, source_target_pairs={{0,6},{1,7},{2,0},{3,1},{4,2},{5,3},{6,4},{7,5},{8,14},{9,15},{10,... | collective-permute-start | bytes 786440 | tf_op jit(solution)/shard_map/ppermute | solution.py:488
  114.9 8.5 %backward_own.1 = (bf16[512,1024]{1,0:T(8,128)(2,1)}, f32[2,512,1024]{2,1,0:T(8,128)}) custom-call(bf16[512,1024]{1,0:T(8,128)(2,1)} %bitcast.63, bf16[512,1024]{1,0:T(8,128)(2,1)} %bitcast.66, bf16[512,1024]{1,0:T(8,128)(2,1)} %bitcast.69, bf16[512,1024]{1,0:T(8,128)(2,1)} %convolution_convert_fusion.refs_2_.refs_3_, ...), custom_call_target="tpu_custom_call" | custom-call | flops 1 | bytes 1 | tf_op jit(solution)/shard_map/backward_own/pallas_call | solution.py:346
  123.4 0.0 collective-permute-done.6
  123.4 0.0 collective-permute-done.7
  123.4 3.1 %collective-permute-done.8 = bf16[1024,128]{1,0:T(8,128)(2,1)S(1)} collective-permute-done((bf16[1024,128]{1,0:T(8,128)(2,1)S(1)}, bf16[1024,128]{1,0:T(8,128)(2,1)S(1)}, u32[]{:S(2)}, u32[]{:S(2)}) %collective-permute-start.8) | collective-permute-done | bytes 262176 | tf_op jit(solution)/shard_map/ppermute | solution.py:488
  126.5 0.1 add_convert_fusion
  126.6 0.7 copy.24
  127.3 3.4 %all-to-all-start.3 = ((bf16[8,128,128]{2,1,0:T(8,128)(2,1)}), bf16[8,128,128]{2,1,0:T(8,128)(2,1)S(1)}, u32[]{:S(2)}, u32[]{:S(2)}) async-start(bf16[8,128,128]{2,1,0:T(8,128)(2,1)} %bitcast.19), calls=%async_computation.3 | async-start | bytes 524288 | tf_op jit(solution)/shard_map/all_to_all | solution.py:408
  131.0 4.8 %project.1 = bf16[512,1024]{1,0:T(8,128)(2,1)} custom-call(bf16[512,1024]{1,0:T(8,128)(2,1)} %get-tuple-element.87.refs_0_, bf16[1024,1024]{1,0:T(8,128)(2,1)} %refs_1_.1), custom_call_target="tpu_custom_call" | custom-call | flops 1 | bytes 1 | tf_op jit(solution)/shard_map/project/pallas_call | solution.py:365
  135.8 2.4 %all-to-all-done.3 = bf16[8,128,128]{2,1,0:T(8,128)(2,1)S(1)} async-done(((bf16[8,128,128]{2,1,0:T(8,128)(2,1)}), bf16[8,128,128]{2,1,0:T(8,128)(2,1)S(1)}, u32[]{:S(2)}, u32[]{:S(2)}) %all-to-all-start.3) | async-done | bytes 262176 | tf_op jit(solution)/shard_map/all_to_all | solution.py:408
  138.2 0.0 collective-permute-done.9.refs_1_
  138.2 0.0 collective-permute-done.10.refs_2_
  138.3 0.7 collective-permute-start.13
  139.0 4.7 %collective-permute-start.12 = (bf16[64,128]{1,0:T(8,128)(2,1)S(1)}, bf16[64,128]{1,0:T(8,128)(2,1)S(1)}, u32[]{:S(2)}, u32[]{:S(2)}) collective-permute-start(bf16[64,128]{1,0:T(8,128)(2,1)S(1)} %pad_maximum_fusion.4), channel_id=1, source_target_pairs={{128,0},{136,8},{144,16},{152,24},{160,32},{168,40},{176,48},{184,... | collective-permute-start | bytes 49160 | tf_op jit(solution)/shard_map/ppermute | solution.py:511
  143.7 0.0 collective-permute-start.11
  143.7 0.0 collective-permute-done.13
  143.7 1.9 %collective-permute-done.12 = bf16[64,128]{1,0:T(8,128)(2,1)S(1)} collective-permute-done((bf16[64,128]{1,0:T(8,128)(2,1)S(1)}, bf16[64,128]{1,0:T(8,128)(2,1)S(1)}, u32[]{:S(2)}, u32[]{:S(2)}) %collective-permute-start.12) | collective-permute-done | bytes 16416 | tf_op jit(solution)/shard_map/ppermute | solution.py:511
  145.6 3.0 %collective-permute-done.11 = bf16[64,128]{1,0:T(8,128)(2,1)S(1)} collective-permute-done((bf16[64,128]{1,0:T(8,128)(2,1)S(1)}, bf16[64,128]{1,0:T(8,128)(2,1)S(1)}, u32[]{:S(2)}, u32[]{:S(2)}) %collective-permute-start.11) | collective-permute-done | bytes 16416 | tf_op jit(solution)/shard_map/ppermute | solution.py:511
  148.6 0.6 broadcast_in_dim.49
  149.3 8.6 %all-to-all-start.4 = ((bf16[8,32,128]{2,1,0:T(8,128)(2,1)}), bf16[8,32,128]{2,1,0:T(8,128)(2,1)S(1)}, u32[]{:S(2)}, u32[]{:S(2)}) async-start(bf16[8,32,128]{2,1,0:T(8,128)(2,1)} %broadcast_in_dim.49), calls=%async_computation.4 | async-start | bytes 131072 | tf_op jit(solution)/shard_map/all_to_all | solution.py:408
  157.9 0.6 slice.42
  158.5 4.6 %finish.1 = (bf16[512,1024]{1,0:T(8,128)(2,1)}, bf16[512,1024]{1,0:T(8,128)(2,1)}) custom-call(f32[2,512,1024]{2,1,0:T(8,128)} %get-tuple-element.88.refs_0_, bf16[2,256,1024]{2,1,0:T(8,128)(2,1)} %copy-done.7, bf16[2,256,1024]{2,1,0:T(8,128)(2,1)} %collective-permute-done.10.refs_2_, bf16[8,640,128]{2,1,0:T(8,128)(2,1)} %copy-done.1, f32[8,4,128]{2,1,0:T(4,128)} %bitcast.81), custom_call_target="tpu_custom_call" | custom-call | flops 1 | bytes 1 | tf_op jit(solution)/shard_map/finish/pallas_call | solution.py:393
  163.1 0.0 all-to-all-done.4
  163.1 0.7 copy_bitcast_fusion
  (37 shorter events, 0.3 us)
Async XLA Ops:
  4.2 5.5 %copy-start.8 = (bf16[16,1024]{1,0:T(8,128)(2,1)S(1)}, bf16[16,1024]{1,0:T(8,128)(2,1)}, u32[]{:S(2)}) copy-start(bf16[16,1024]{1,0:T(8,128)(2,1)} %get-tuple-element.51) | copy-start | bytes 98308
  4.2 22.5 %all-to-all-start = ((bf16[8,64,1024]{2,1,0:T(8,128)(2,1)}), bf16[8,64,1024]{2,1,0:T(8,128)(2,1)S(1)}, u32[]{:S(2)}, u32[]{:S(2)}) async-start(bf16[8,64,1024]{2,1,0:T(8,128)(2,1)} %get-tuple-element.52), calls=%async_computation | async-start | bytes 2097152 | tf_op jit(solution)/shard_map/all_to_all | solution.py:408
  9.7 14.6 %collective-permute-start.2 = (bf16[16,1024]{1,0:T(8,128)(2,1)S(1)}, bf16[16,1024]{1,0:T(8,128)(2,1)S(1)}, u32[]{:S(2)}, u32[]{:S(2)}) collective-permute-start(bf16[16,1024]{1,0:T(8,128)(2,1)S(1)} %copy-done.8), channel_id=1, source_target_pairs={{0,192},{8,200},{16,208},{24,216},{32,224},{40,232},{48,240},{56,2... | collective-permute-start | bytes 98312 | tf_op jit(solution)/shard_map/ppermute | solution.py:453
  9.8 16.8 %collective-permute-start.1 = (bf16[16,1024]{1,0:T(8,128)(2,1)S(1)}, bf16[16,1024]{1,0:T(8,128)(2,1)S(1)}, u32[]{:S(2)}, u32[]{:S(2)}) collective-permute-start(bf16[16,1024]{1,0:T(8,128)(2,1)S(1)} %copy-done.8), channel_id=1, source_target_pairs={{0,128},{8,136},{16,144},{24,152},{32,160},{40,168},{48,176},{56,1... | collective-permute-start | bytes 98312 | tf_op jit(solution)/shard_map/ppermute | solution.py:453
  15.2 11.4 %collective-permute-start = (bf16[16,1024]{1,0:T(8,128)(2,1)S(1)}, bf16[16,1024]{1,0:T(8,128)(2,1)S(1)}, u32[]{:S(2)}, u32[]{:S(2)}) collective-permute-start(bf16[16,1024]{1,0:T(8,128)(2,1)S(1)} %copy-done.8), channel_id=1, source_target_pairs={{0,64},{8,72},{16,80},{24,88},{32,96},{40,104},{48,112},{56,120},{... | collective-permute-start | bytes 98312 | tf_op jit(solution)/shard_map/ppermute | solution.py:453
  26.7 28.0 %copy-start = (bf16[8,64,1024]{2,1,0:T(8,128)(2,1)}, bf16[8,64,1024]{2,1,0:T(8,128)(2,1)S(1)}, u32[]{:S(2)}) copy-start(bf16[8,64,1024]{2,1,0:T(8,128)(2,1)S(1)} %all-to-all-done.refs_2_.refs_3_) | copy-start | bytes 3145732
  27.5 12.4 %all-to-all-start.1 = ((bf16[8,16,1024]{2,1,0:T(8,128)(2,1)}), bf16[8,16,1024]{2,1,0:T(8,128)(2,1)S(1)}, u32[]{:S(2)}, u32[]{:S(2)}) async-start(bf16[8,16,1024]{2,1,0:T(8,128)(2,1)} %broadcast_in_dim.41), calls=%async_computation.1 | async-start | bytes 524288 | tf_op jit(solution)/shard_map/all_to_all | solution.py:408
  39.9 14.8 %copy-start.4 = (bf16[8,16,1024]{2,1,0:T(8,128)(2,1)}, bf16[8,16,1024]{2,1,0:T(8,128)(2,1)S(1)}, u32[]{:S(2)}) copy-start(bf16[8,16,1024]{2,1,0:T(8,128)(2,1)S(1)} %all-to-all-done.1.refs_3_.refs_4_) | copy-start | bytes 786436
  39.9 25.3 %collective-permute-start.3 = (bf16[2,256,1024]{2,1,0:T(8,128)(2,1)}, bf16[2,256,1024]{2,1,0:T(8,128)(2,1)S(1)}, u32[]{:S(2)}, u32[]{:S(2)}) collective-permute-start(bf16[2,256,1024]{2,1,0:T(8,128)(2,1)} %get-tuple-element.56), channel_id=1, source_target_pairs={{0,8},{8,16},{16,24},{24,32},{32,40},{40,48},{48,56},{56,64},{64,7... | collective-permute-start | bytes 3145736 | tf_op jit(solution)/shard_map/ppermute | solution.py:463
  41.8 24.4 %collective-permute-start.4 = (bf16[2,256,1024]{2,1,0:T(8,128)(2,1)}, bf16[2,256,1024]{2,1,0:T(8,128)(2,1)S(1)}, u32[]{:S(2)}, u32[]{:S(2)}) collective-permute-start(bf16[2,256,1024]{2,1,0:T(8,128)(2,1)} %get-tuple-element.58), channel_id=1, source_target_pairs={{8,0},{16,8},{24,16},{32,24},{40,32},{48,40},{56,48},{64,56},{72,6... | collective-permute-start | bytes 3145736 | tf_op jit(solution)/shard_map/ppermute | solution.py:464
  48.3 2.9 %copy-start.5 = (bf16[1024,1024]{1,0:T(8,128)(2,1)S(1)}, bf16[1024,1024]{1,0:T(8,128)(2,1)}, u32[]{:S(2)}) copy-start(bf16[1024,1024]{1,0:T(8,128)(2,1)} %refs_1_.1) | copy-start | bytes 6291460
  65.2 1.0 copy-start.2
  66.2 1.0 copy-start.3
  81.5 20.8 %all-to-all-start.2 = ((bf16[8,640,128]{2,1,0:T(8,128)(2,1)}), bf16[8,640,128]{2,1,0:T(8,128)(2,1)S(1)}, u32[]{:S(2)}, u32[]{:S(2)}) async-start(bf16[8,640,128]{2,1,0:T(8,128)(2,1)} %bitcast.74), calls=%async_computation.2 | async-start | bytes 2621440 | tf_op jit(solution)/shard_map/all_to_all | solution.py:408
  90.0 12.3 %collective-permute-start.5 = (bf16[4,1024,128]{2,1,0:T(8,128)(2,1)}, bf16[4,1024,128]{2,1,0:T(8,128)(2,1)S(1)}, u32[]{:S(2)}, u32[]{:S(2)}) collective-permute-start(bf16[4,1024,128]{2,1,0:T(8,128)(2,1)} %get-tuple-element.71), channel_id=1, source_target_pairs={{0,1},{1,0},{2,3},{3,2},{4,5},{5,4},{6,7},{7,6},{8,9},{9,8},{10,11... | collective-permute-start | bytes 3145736 | tf_op jit(solution)/shard_map/ppermute | solution.py:478
  95.4 6.9 %copy-start.6 = (bf16[4,1024,128]{2,1,0:T(8,128)(2,1)S(1)}, bf16[4,1024,128]{2,1,0:T(8,128)(2,1)}, u32[]{:S(2)}) copy-start(bf16[4,1024,128]{2,1,0:T(8,128)(2,1)} %get-tuple-element.70) | copy-start | bytes 3145732
  102.3 28.5 %copy-start.1 = (bf16[8,640,128]{2,1,0:T(8,128)(2,1)}, bf16[8,640,128]{2,1,0:T(8,128)(2,1)S(1)}, u32[]{:S(2)}) copy-start(bf16[8,640,128]{2,1,0:T(8,128)(2,1)S(1)} %all-to-all-done.2.refs_3_) | copy-start | bytes 3932164
  102.7 35.5 %collective-permute-start.9 = (bf16[2,256,1024]{2,1,0:T(8,128)(2,1)}, bf16[2,256,1024]{2,1,0:T(8,128)(2,1)S(1)}, u32[]{:S(2)}, u32[]{:S(2)}) collective-permute-start(bf16[2,256,1024]{2,1,0:T(8,128)(2,1)} %get-tuple-element.89), channel_id=1, source_target_pairs={{0,8},{8,16},{16,24},{24,32},{32,40},{40,48},{48,56},{56,64},{64,7... | collective-permute-start | bytes 3145736 | tf_op jit(solution)/shard_map/ppermute | solution.py:494
  106.3 31.9 %collective-permute-start.10 = (bf16[2,256,1024]{2,1,0:T(8,128)(2,1)}, bf16[2,256,1024]{2,1,0:T(8,128)(2,1)}, u32[]{:S(2)}, u32[]{:S(2)}) collective-permute-start(bf16[2,256,1024]{2,1,0:T(8,128)(2,1)} %get-tuple-element.81), channel_id=1, source_target_pairs={{8,0},{16,8},{24,16},{32,24},{40,32},{48,40},{56,48},{64,56},{72,6... | collective-permute-start | bytes 3145736 | tf_op jit(solution)/shard_map/ppermute | solution.py:493
  110.7 12.7 %collective-permute-start.6 = (bf16[1024,128]{1,0:T(8,128)(2,1)S(1)}, bf16[1024,128]{1,0:T(8,128)(2,1)S(1)}, u32[]{:S(2)}, u32[]{:S(2)}) collective-permute-start(bf16[1024,128]{1,0:T(8,128)(2,1)S(1)} %get-tuple-element.95), channel_id=1, source_target_pairs={{0,2},{1,3},{2,4},{3,5},{4,6},{5,7},{6,0},{7,1},{8,10},{9,11},{10,... | collective-permute-start | bytes 786440 | tf_op jit(solution)/shard_map/ppermute | solution.py:488
  112.1 11.3 %collective-permute-start.7 = (bf16[1024,128]{1,0:T(8,128)(2,1)S(1)}, bf16[1024,128]{1,0:T(8,128)(2,1)S(1)}, u32[]{:S(2)}, u32[]{:S(2)}) collective-permute-start(bf16[1024,128]{1,0:T(8,128)(2,1)S(1)} %get-tuple-element.94), channel_id=1, source_target_pairs={{0,4},{1,5},{2,6},{3,7},{4,0},{5,1},{6,2},{7,3},{8,12},{9,13},{10,... | collective-permute-start | bytes 786440 | tf_op jit(solution)/shard_map/ppermute | solution.py:488
  113.1 13.4 %collective-permute-start.8 = (bf16[1024,128]{1,0:T(8,128)(2,1)S(1)}, bf16[1024,128]{1,0:T(8,128)(2,1)S(1)}, u32[]{:S(2)}, u32[]{:S(2)}) collective-permute-start(bf16[1024,128]{1,0:T(8,128)(2,1)S(1)} %get-tuple-element.93), channel_id=1, source_target_pairs={{0,6},{1,7},{2,0},{3,1},{4,2},{5,3},{6,4},{7,5},{8,14},{9,15},{10,... | collective-permute-start | bytes 786440 | tf_op jit(solution)/shard_map/ppermute | solution.py:488
  127.3 10.9 %all-to-all-start.3 = ((bf16[8,128,128]{2,1,0:T(8,128)(2,1)}), bf16[8,128,128]{2,1,0:T(8,128)(2,1)S(1)}, u32[]{:S(2)}, u32[]{:S(2)}) async-start(bf16[8,128,128]{2,1,0:T(8,128)(2,1)} %bitcast.19), calls=%async_computation.3 | async-start | bytes 524288 | tf_op jit(solution)/shard_map/all_to_all | solution.py:408
  138.2 20.3 %copy-start.7 = (bf16[2,256,1024]{2,1,0:T(8,128)(2,1)}, bf16[2,256,1024]{2,1,0:T(8,128)(2,1)S(1)}, u32[]{:S(2)}) copy-start(bf16[2,256,1024]{2,1,0:T(8,128)(2,1)S(1)} %collective-permute-done.9.refs_1_) | copy-start | bytes 3145732
  138.3 5.4 %collective-permute-start.13 = (bf16[64,128]{1,0:T(8,128)(2,1)S(1)}, bf16[64,128]{1,0:T(8,128)(2,1)S(1)}, u32[]{:S(2)}, u32[]{:S(2)}) collective-permute-start(bf16[64,128]{1,0:T(8,128)(2,1)S(1)} %pad_maximum_fusion.5), channel_id=1, source_target_pairs={{192,0},{200,8},{208,16},{216,24},{224,32},{232,40},{240,48},{248,... | collective-permute-start | bytes 49160 | tf_op jit(solution)/shard_map/ppermute | solution.py:511
  139.0 6.6 %collective-permute-start.12 = (bf16[64,128]{1,0:T(8,128)(2,1)S(1)}, bf16[64,128]{1,0:T(8,128)(2,1)S(1)}, u32[]{:S(2)}, u32[]{:S(2)}) collective-permute-start(bf16[64,128]{1,0:T(8,128)(2,1)S(1)} %pad_maximum_fusion.4), channel_id=1, source_target_pairs={{128,0},{136,8},{144,16},{152,24},{160,32},{168,40},{176,48},{184,... | collective-permute-start | bytes 49160 | tf_op jit(solution)/shard_map/ppermute | solution.py:511
  143.7 4.9 %collective-permute-start.11 = (bf16[64,128]{1,0:T(8,128)(2,1)S(1)}, bf16[64,128]{1,0:T(8,128)(2,1)S(1)}, u32[]{:S(2)}, u32[]{:S(2)}) collective-permute-start(bf16[64,128]{1,0:T(8,128)(2,1)S(1)} %pad_maximum_fusion.3), channel_id=1, source_target_pairs={{64,0},{72,8},{80,16},{88,24},{96,32},{104,40},{112,48},{120,56},{... | collective-permute-start | bytes 49160 | tf_op jit(solution)/shard_map/ppermute | solution.py:511
  149.3 13.8 %all-to-all-start.4 = ((bf16[8,32,128]{2,1,0:T(8,128)(2,1)}), bf16[8,32,128]{2,1,0:T(8,128)(2,1)S(1)}, u32[]{:S(2)}, u32[]{:S(2)}) async-start(bf16[8,32,128]{2,1,0:T(8,128)(2,1)} %broadcast_in_dim.49), calls=%async_computation.4 | async-start | bytes 131072 | tf_op jit(solution)/shard_map/all_to_all | solution.py:408

commit v4 on v3

--- a/solution.py
+++ b/solution.py
@@ -219,26 +219,6 @@
     stat_ref[0, 1:2] = jnp.sum(jnp.transpose(g_ref[...].astype(F32)) * across.astype(F32), axis=0, keepdims=True)
 
 
-def forward_near(edge, q, g, before, after, acc, stat):
-    tokens, width = q.shape
-    heads = width // HEAD
-    rows = cols(tokens)
-    near = cols(2, BLOCK)
-    return over_heads(
-        forward_near_kernel,
-        heads,
-        PER[2],
-        [SMEM, rows, rows, near, near, heads_of(HEAD, tokens), heads_of(2, tokens)],
-        [rows, leading(HEAD, tokens), heads_of(2, tokens)],
-        [
-            shape((tokens, width), BF16),
-            shape((width, tokens), BF16),
-            shape((heads, 2, tokens), F32),
-        ],
-        "forward_near",
-    )(edge, q, g, before, after, acc, stat)
-
-
 def weight_kernel(core_ref, across_ref, up_ref, keep_ref, send_ref):
     weight = dot(across_ref[...], up_ref[...], 1, 0).astype(BF16)
     first = core_ref[0] == 0
@@ -264,6 +244,87 @@
 def gradients(s, dprob, stat_ref):
     p = jnp.exp2(s - stat_ref[0, 0:1])
     return p.astype(BF16), (p * (dprob - stat_ref[0, 1:2])).astype(BF16)
+
+
+def backward_near_kernel(
+    edge_ref, q_ref, g_ref, before, after, stat_ref, part_ref, sum_ref, dbefore_ref, dafter_ref
+):
+    q, g = q_ref[...], g_ref[...]
+    s = near_scores(edge_ref, before, after, q)
+    dprob = both(dot(before[1], g[:BLOCK], 1, 1), dot(after[1], g[BLOCK:], 1, 1))
+    p, ds = gradients(s, dprob, stat_ref)
+    for side, ref in enumerate((dbefore_ref, dafter_ref)):
+        rows = slice(side * BLOCK, (side + 1) * BLOCK)
+        ref[0] = (dot(ds[:, rows], q[rows], 1, 0) * FACTOR).astype(BF16)
+        ref[1] = dot(p[:, rows], g[rows], 1, 0).astype(BF16)
+    dq = both(dot(before[0], ds[:, :BLOCK], 0, 0), dot(after[0], ds[:, BLOCK:], 0, 0))
+    sum_ref[0] = part_ref[0] + dq
+
+
+def backward_near(edge, q, g, before, after, stat, part):
+    tokens, width = q.shape
+    heads = width // HEAD
+    rows = cols(tokens)
+    near = cols(2, BLOCK)
+    return over_heads(
+        backward_near_kernel,
+        heads,
+        PER[4],
+        [SMEM, rows, rows, near, near, heads_of(2, tokens), heads_of(HEAD, tokens)],
+        [heads_of(HEAD, tokens), near, near],
+        [shape((heads, HEAD, tokens), F32), shape((2, BLOCK, width), BF16), shape((2, BLOCK, width), BF16)],
+        "backward_near",
+    )(edge, q, g, before, after, stat, part)
+
+
+def backward_coarse_kernel(bias_ref, q_ref, g_ref, one, two, stat_ref, sum_ref, out_ref):
+    q, g = q_ref[...], g_ref[...]
+    keys, values = coarse_rows(one, two)
+    s = dot(keys, q, 1, 1) * LOG2 + bias_ref[...]
+    p, ds = gradients(s, dot(values, g, 1, 1), stat_ref)
+    dk = dot(ds, q, 1, 0) * FACTOR
+    dv = dot(p, g, 1, 0)
+    sum_ref[0] = dot(keys, ds, 0, 0)
+    count = one.shape[0] * (one.shape[1] // 2)
+    pieces = [d.reshape(out_ref.shape[0], -1, HEAD) for d in (dk[:count], dv[:count], dk[count:], dv[count:])]
+    out_ref[:, 0] = jnp.concatenate(pieces, axis=1).astype(BF16)
+
+
+def middle_kernel(
+    edge_ref, bias_ref, q_ref, g_ref, before, after, one, two, acc_ref, own_ref,
+    attn_ref, across_ref, stat_ref, sum_ref, out_ref,
+):
+    forward_near_kernel(edge_ref, q_ref, g_ref, before, after, acc_ref, own_ref, attn_ref, across_ref, stat_ref)
+    backward_coarse_kernel(bias_ref, q_ref, g_ref, one, two, stat_ref, sum_ref, out_ref)
+
+
+def middle(edge, bias, q, g, before, after, one, two, acc, stat):
+    tokens, width = q.shape
+    heads = width // HEAD
+    rows = cols(tokens)
+    near = cols(2, BLOCK)
+    slots, per_slot = one.shape[0], one.shape[1] + two.shape[1]
+    return over_heads(
+        middle_kernel,
+        heads,
+        PER[2],
+        [
+            SMEM, fixed(*bias.shape), rows, rows, near, near, cols(*one.shape[:2]), cols(*two.shape[:2]),
+            heads_of(HEAD, tokens), heads_of(2, tokens),
+        ],
+        [
+            rows, leading(HEAD, tokens), heads_of(2, tokens), heads_of(HEAD, tokens),
+            second(slots, 1, per_slot, HEAD),
+        ],
+        [
+            shape((tokens, width), BF16),
+            shape((width, tokens), BF16),
+            shape((heads, 2, tokens), F32),
+            shape((heads, HEAD, tokens), F32),
+            shape((slots, heads, per_slot, HEAD), BF16),
+        ],
+        "middle",
+    )(edge, bias, q, g, before, after, one, two, acc, stat)
 
 
 def backward_near_kernel(
@@ -464,10 +525,9 @@
     after = lax.ppermute(first, "ctx", down)
     acc, stat = forward_coarse(bias, after_all(q, last, g), one, two, acc, stat)
     before, after = lax.optimization_barrier((before, after, acc))[:2]
-    attn, across, stat = forward_near(edge, q, g, before, after, acc, stat)
-
-    heads = width // HEAD
-    part, packed = backward_coarse(bias, q, g, one, two, stat)
+    attn, across, stat, part, packed = middle(edge, bias, q, g, before, after, one, two, acc, stat)
+
+    heads = width // HEAD
     packed = packed.reshape(GROUP, -1, HEAD)
     g, stat = lax.optimization_barrier((g, stat, packed))[:2]
     across = after_all(across, packed)

time: 165 us -> 162 us (0.982)
  Pallas kernels: 60.4 us -> 56.9 us
    pallas_call x2 -> x1, Pallas kernels: 14.3 us -> 10.9 us  [middle(): over_heads(middle_kernel, heads, PER[2], [SMEM, fixed(*bias.shape), rows,...]
  transfers between devices with their start and end apart: 19 -> 19, of which waited for: 8 -> 8; matrix products, arithmetic and copies ran while one was open for 6% -> 6% of each run, Pallas kernels for 26% -> 27%
where the time goes in v4:
time: 162 us; the launch traced here: 160 us
  starting transfers between devices  66.8 us (41%)
  Pallas kernels  56.9 us (35%)
  waiting for transfers between devices  23 us (14%)
  local copies, waits for them, and re-layouts  7.04 us (4%)
  matrix products  3.49 us (2%)
  other arithmetic  2.08 us (1%)
    all_to_all x5, starting transfers between devices, exchange(): return lax.all_to_all(x, axis, 0, 0, axis_index_groups=groups, tiled=True)  28.6 us
    pallas_call x1, Pallas kernels, middle(): over_heads(middle_kernel, heads, PER[2], [SMEM, fixed(*bias.shape), rows,...  10.9 us
    pallas_call x1, Pallas kernels, backward_own(): over_heads(backward_own_kernel, heads, PER[4], [rows, rows, rows, rows, h...  8.52 us
    all_to_all x5, waiting for transfers between devices, exchange(): return lax.all_to_all(x, axis, 0, 0, axis_index_groups=groups, tiled=True)  8.43 us
    ppermute x3, starting transfers between devices, on_device(): two = [two] + [lax.ppermute(two, 'ctx', moves) for moves in far[1:]]  7.86 us
    pallas_call x1, Pallas kernels, forward_coarse(): over_heads(forward_coarse_kernel, heads, PER[3], [fixed(*bias.shape), col...  7.13 us
    pallas_call x1, Pallas kernels, backward_near(): over_heads(backward_near_kernel, heads, PER[4], [SMEM, rows, rows, near,...  6.91 us
    pallas_call x1, Pallas kernels, forward_own(): over_heads(own_kernel, heads, PER[1], [rows, rows, rows], [heads_of(HEAD,...  6.72 us
  transfers between devices with their start and end apart: 19, of which 8 were waited for; matrix products, arithmetic and copies ran while one was open for 6% of the time, Pallas kernels for 27%

profile of v4, /device:TPU:73, one launch (start us, length us, event | category | flops | bytes accessed | tf_op | source)
XLA Modules:
  0.0 160.3 jit_solution(16679263563988950830)
XLA Ops:
  0.6 3.6 %prepare.1 = (bf16[2,256,1024]{2,1,0:T(8,128)(2,1)}, bf16[2,256,1024]{2,1,0:T(8,128)(2,1)}, bf16[8,64,1024]{2,1,0:T(8,128)(2,1)}, bf16[16,1024]{1,0:T(8,128)(2,1)}) custom-call(bf16[512,1024]{1,0:T(8,128)(2,1)} %bitcast.63, bf16[512,1024]{1,0:T(8,128)(2,1)} %bitcast.66), custom_call_target="tpu_custom_call" | custom-call | flops 1 | bytes 1 | tf_op jit(solution)/shard_map/prepare/pallas_call | solution.py:110
  4.2 5.5 %all-to-all-start = ((bf16[8,64,1024]{2,1,0:T(8,128)(2,1)}), bf16[8,64,1024]{2,1,0:T(8,128)(2,1)S(1)}, u32[]{:S(2)}, u32[]{:S(2)}) async-start(bf16[8,64,1024]{2,1,0:T(8,128)(2,1)} %get-tuple-element.52), calls=%async_computation | async-start | bytes 2097152 | tf_op jit(solution)/shard_map/all_to_all | solution.py:469
  9.7 0.0 copy-done.8
  9.7 0.1 collective-permute-start.2
  9.8 5.4 %collective-permute-start.1 = (bf16[16,1024]{1,0:T(8,128)(2,1)S(1)}, bf16[16,1024]{1,0:T(8,128)(2,1)S(1)}, u32[]{:S(2)}, u32[]{:S(2)}) collective-permute-start(bf16[16,1024]{1,0:T(8,128)(2,1)S(1)} %copy-done.8), channel_id=1, source_target_pairs={{0,128},{8,136},{16,144},{24,152},{32,160},{40,168},{48,176},{56,1... | collective-permute-start | bytes 98312 | tf_op jit(solution)/shard_map/ppermute | solution.py:514
  15.2 2.4 %collective-permute-start = (bf16[16,1024]{1,0:T(8,128)(2,1)S(1)}, bf16[16,1024]{1,0:T(8,128)(2,1)S(1)}, u32[]{:S(2)}, u32[]{:S(2)}) collective-permute-start(bf16[16,1024]{1,0:T(8,128)(2,1)S(1)} %copy-done.8), channel_id=1, source_target_pairs={{0,64},{8,72},{16,80},{24,88},{32,96},{40,104},{48,112},{56,120},{... | collective-permute-start | bytes 98312 | tf_op jit(solution)/shard_map/ppermute | solution.py:514
  17.6 6.7 %forward_own.1 = (f32[8,128,512]{2,1,0:T(8,128)}, f32[8,2,512]{2,1,0:T(2,128)}) custom-call(bf16[512,1024]{1,0:T(8,128)(2,1)} %bitcast.58, bf16[512,1024]{1,0:T(8,128)(2,1)} %bitcast.64, bf16[512,1024]{1,0:T(8,128)(2,1)} %bitcast.67), custom_call_target="tpu_custom_call" | custom-call | flops 1 | bytes 1 | tf_op jit(solution)/shard_map/forward_own/pallas_call | solution.py:157
  24.3 0.0 collective-permute-done.2
  24.3 2.3 %collective-permute-done.1 = bf16[16,1024]{1,0:T(8,128)(2,1)S(1)} collective-permute-done((bf16[16,1024]{1,0:T(8,128)(2,1)S(1)}, bf16[16,1024]{1,0:T(8,128)(2,1)S(1)}, u32[]{:S(2)}, u32[]{:S(2)}) %collective-permute-start.1) | collective-permute-done | bytes 32800 | tf_op jit(solution)/shard_map/ppermute | solution.py:514
  26.6 0.0 collective-permute-done
  26.7 0.0 all-to-all-done.refs_2_.refs_6_
  26.7 0.0 copy-start
  26.7 0.8 broadcast_in_dim.44
  27.5 6.3 %all-to-all-start.1 = ((bf16[8,16,1024]{2,1,0:T(8,128)(2,1)}), bf16[8,16,1024]{2,1,0:T(8,128)(2,1)S(1)}, u32[]{:S(2)}, u32[]{:S(2)}) async-start(bf16[8,16,1024]{2,1,0:T(8,128)(2,1)} %broadcast_in_dim.44), calls=%async_computation.1 | async-start | bytes 524288 | tf_op jit(solution)/shard_map/all_to_all | solution.py:469
  33.9 6.0 %all-to-all-done.1.refs_3_.refs_7_ = bf16[8,16,1024]{2,1,0:T(8,128)(2,1)S(1)} async-done(((bf16[8,16,1024]{2,1,0:T(8,128)(2,1)}), bf16[8,16,1024]{2,1,0:T(8,128)(2,1)S(1)}, u32[]{:S(2)}, u32[]{:S(2)}) %all-to-all-start.1) | async-done | bytes 262176 | tf_op jit(solution)/shard_map/all_to_all | solution.py:469
  39.9 1.9 %collective-permute-start.3 = (bf16[2,256,1024]{2,1,0:T(8,128)(2,1)}, bf16[2,256,1024]{2,1,0:T(8,128)(2,1)S(1)}, u32[]{:S(2)}, u32[]{:S(2)}) collective-permute-start(bf16[2,256,1024]{2,1,0:T(8,128)(2,1)} %get-tuple-element.56), channel_id=1, source_target_pairs={{0,8},{8,16},{16,24},{24,32},{32,40},{40,48},{48,56},{56,64},{64,7... | collective-permute-start | bytes 3145736 | tf_op jit(solution)/shard_map/ppermute | solution.py:524
  41.8 5.5 %collective-permute-start.4 = (bf16[2,256,1024]{2,1,0:T(8,128)(2,1)}, bf16[2,256,1024]{2,1,0:T(8,128)(2,1)S(1)}, u32[]{:S(2)}, u32[]{:S(2)}) collective-permute-start(bf16[2,256,1024]{2,1,0:T(8,128)(2,1)} %get-tuple-element.58), channel_id=1, source_target_pairs={{8,0},{16,8},{24,16},{32,24},{40,32},{48,40},{56,48},{64,56},{72,6... | collective-permute-start | bytes 3145736 | tf_op jit(solution)/shard_map/ppermute | solution.py:525
  47.3 0.1 compare_and_fusion
  47.4 0.1 abs_compare_fusion
  47.5 0.8 copy.23
  48.3 1.5 broadcast_in_dim.42
  49.7 0.9 copy.32
  50.6 0.6 add_select_fusion.1.refs_0_
  51.3 3.5 %convolution_convert_fusion.refs_3_.refs_2_ = bf16[512,1024]{1,0:T(8,128)(2,1)} fusion(bf16[512,1024]{1,0:T(8,128)(2,1)} %bitcast.74, bf16[1024,1024]{1,0:T(8,128)(2,1)S(1)} %copy-done.5), kind=kOutput, calls=%fused_computation | convolution fusion | flops 1074266112 | bytes 4194304 | tf_op jit(solution)/shard_map/dot_general | solution.py:25
  54.8 7.1 %forward_coarse.1 = (f32[8,128,512]{2,1,0:T(8,128)}, f32[8,2,512]{2,1,0:T(2,128)}) custom-call(f32[320,512]{1,0:T(8,128)} %bitcast.70, bf16[512,1024]{1,0:T(8,128)(2,1)} %bitcast.59, bf16[8,64,1024]{2,1,0:T(8,128)(2,1)} %copy-done, bf16[8,16,1024]{2,1,0:T(8,128)(2,1)} %copy-done.4, f32[8,128,512]{2,1,0:T(8,128)} %get-tuple-element.53.refs_4_, ...), custom_call_target="tpu_custom_call" | custom-call | flops 1 | bytes 1 | tf_op jit(solution)/shard_map/forward_coarse/pallas_call | solution.py:198
  61.9 3.3 %collective-permute-done.3.refs_4_.refs_3_ = bf16[2,256,1024]{2,1,0:T(8,128)(2,1)S(1)} collective-permute-done((bf16[2,256,1024]{2,1,0:T(8,128)(2,1)}, bf16[2,256,1024]{2,1,0:T(8,128)(2,1)S(1)}, u32[]{:S(2)}, u32[]{:S(2)}) %collective-permute-start.3) | collective-permute-done | bytes 1048608 | tf_op jit(solution)/shard_map/ppermute | solution.py:524
  65.2 1.0 collective-permute-done.4.refs_5_.refs_4_
  66.2 1.0 copy-done.3
  67.2 10.9 %middle.1 = (bf16[512,1024]{1,0:T(8,128)(2,1)}, bf16[1024,512]{1,0:T(8,128)(2,1)}, f32[8,2,512]{2,1,0:T(2,128)}, f32[8,128,512]{2,1,0:T(8,128)}, bf16[8,8,80,128]{3,2,1,0:T(8,128)(2,1)}) custom-call(f32[2]{0:T(128)} %add_select_fusion.1.refs_0_, f32[320,512]{1,0:T(8,128)} %bitcast.71, bf16[512,1024]{1,0:T(8,128)(2,1)} %bitcast.60, ...), custom_call_target="tpu_custom_call" | custom-call | flops 1 | bytes 1 | tf_op jit(solution)/shard_map/middle/pallas_call | solution.py:307
  78.0 4.8 %all-to-all-start.2 = ((bf16[8,640,128]{2,1,0:T(8,128)(2,1)}), bf16[8,640,128]{2,1,0:T(8,128)(2,1)S(1)}, u32[]{:S(2)}, u32[]{:S(2)}) async-start(bf16[8,640,128]{2,1,0:T(8,128)(2,1)} %bitcast.73), calls=%async_computation.2 | async-start | bytes 2621440 | tf_op jit(solution)/shard_map/all_to_all | solution.py:469
  82.8 3.8 %weight_terms.1 = (bf16[4,1024,128]{2,1,0:T(8,128)(2,1)}, bf16[4,1024,128]{2,1,0:T(8,128)(2,1)}) custom-call(s32[1]{0:T(128)} %bitcast.11.refs_0_, bf16[1024,512]{1,0:T(8,128)(2,1)} %get-tuple-element.68.refs_1_, bf16[512,1024]{1,0:T(8,128)(2,1)} %bitcast.75), custom_call_target="tpu_custom_call" | custom-call | flops 1 | bytes 1 | tf_op jit(solution)/shard_map/weight_terms/pallas_call | solution.py:233
  86.6 5.4 %collective-permute-start.5 = (bf16[4,1024,128]{2,1,0:T(8,128)(2,1)}, bf16[4,1024,128]{2,1,0:T(8,128)(2,1)S(1)}, u32[]{:S(2)}, u32[]{:S(2)}) collective-permute-start(bf16[4,1024,128]{2,1,0:T(8,128)(2,1)} %get-tuple-element.70), channel_id=1, source_target_pairs={{0,1},{1,0},{2,3},{3,2},{4,5},{5,4},{6,7},{7,6},{8,9},{9,8},{10,11... | collective-permute-start | bytes 3145736 | tf_op jit(solution)/shard_map/ppermute | solution.py:538
  92.0 6.9 %backward_near.1 = (f32[8,128,512]{2,1,0:T(8,128)}, bf16[2,256,1024]{2,1,0:T(8,128)(2,1)}, bf16[2,256,1024]{2,1,0:T(8,128)(2,1)}) custom-call(f32[2]{0:T(128)} %add_select_fusion.1.refs_0_, bf16[512,1024]{1,0:T(8,128)(2,1)} %bitcast.61, bf16[512,1024]{1,0:T(8,128)(2,1)} %convolution_convert_fusion.refs_3_.refs_2_, bf16[2,256,1024]{2,1,0:T(8,128)(2,1)} %copy-done.2, ...), custom_call_target="tpu_custom_call" | custom-call | flops 1 | bytes 1 | tf_op jit(solution)/shard_map/backward_near/pallas_call | solution.py:350
  98.9 0.0 collective-permute-done.5
  98.9 0.0 all-to-all-done.2.refs_3_
  98.9 0.3 fusion.3
  99.2 3.6 %collective-permute-start.9 = (bf16[2,256,1024]{2,1,0:T(8,128)(2,1)}, bf16[2,256,1024]{2,1,0:T(8,128)(2,1)S(1)}, u32[]{:S(2)}, u32[]{:S(2)}) collective-permute-start(bf16[2,256,1024]{2,1,0:T(8,128)(2,1)} %get-tuple-element.89), channel_id=1, source_target_pairs={{0,8},{8,16},{16,24},{24,32},{32,40},{40,48},{48,56},{56,64},{64,7... | collective-permute-start | bytes 3145736 | tf_op jit(solution)/shard_map/ppermute | solution.py:554
  102.9 4.4 %collective-permute-start.10 = (bf16[2,256,1024]{2,1,0:T(8,128)(2,1)}, bf16[2,256,1024]{2,1,0:T(8,128)(2,1)}, u32[]{:S(2)}, u32[]{:S(2)}) collective-permute-start(bf16[2,256,1024]{2,1,0:T(8,128)(2,1)} %get-tuple-element.81), channel_id=1, source_target_pairs={{8,0},{16,8},{24,16},{32,24},{40,32},{48,40},{56,48},{64,56},{72,6... | collective-permute-start | bytes 3145736 | tf_op jit(solution)/shard_map/ppermute | solution.py:553
  107.3 1.4 collective-permute-start.6
  108.7 1.0 collective-permute-start.7
  109.7 1.8 %collective-permute-start.8 = (bf16[1024,128]{1,0:T(8,128)(2,1)S(1)}, bf16[1024,128]{1,0:T(8,128)(2,1)S(1)}, u32[]{:S(2)}, u32[]{:S(2)}) collective-permute-start(bf16[1024,128]{1,0:T(8,128)(2,1)S(1)} %get-tuple-element.93), channel_id=1, source_target_pairs={{0,6},{1,7},{2,0},{3,1},{4,2},{5,3},{6,4},{7,5},{8,14},{9,15},{10,... | collective-permute-start | bytes 786440 | tf_op jit(solution)/shard_map/ppermute | solution.py:548
  111.5 8.5 %backward_own.1 = (bf16[512,1024]{1,0:T(8,128)(2,1)}, f32[2,512,1024]{2,1,0:T(8,128)}) custom-call(bf16[512,1024]{1,0:T(8,128)(2,1)} %bitcast.62, bf16[512,1024]{1,0:T(8,128)(2,1)} %bitcast.65, bf16[512,1024]{1,0:T(8,128)(2,1)} %bitcast.68, bf16[512,1024]{1,0:T(8,128)(2,1)} %convolution_convert_fusion.refs_3_.refs_2_, ...), custom_call_target="tpu_custom_call" | custom-call | flops 1 | bytes 1 | tf_op jit(solution)/shard_map/backward_own/pallas_call | solution.py:407
  120.0 0.0 collective-permute-done.6
  120.0 0.0 collective-permute-done.7
  120.0 3.0 %collective-permute-done.8 = bf16[1024,128]{1,0:T(8,128)(2,1)S(1)} collective-permute-done((bf16[1024,128]{1,0:T(8,128)(2,1)S(1)}, bf16[1024,128]{1,0:T(8,128)(2,1)S(1)}, u32[]{:S(2)}, u32[]{:S(2)}) %collective-permute-start.8) | collective-permute-done | bytes 262176 | tf_op jit(solution)/shard_map/ppermute | solution.py:548
  123.0 0.1 add_convert_fusion
  123.2 0.7 copy.24
  123.9 3.4 %all-to-all-start.3 = ((bf16[8,128,128]{2,1,0:T(8,128)(2,1)}), bf16[8,128,128]{2,1,0:T(8,128)(2,1)S(1)}, u32[]{:S(2)}, u32[]{:S(2)}) async-start(bf16[8,128,128]{2,1,0:T(8,128)(2,1)} %bitcast.19), calls=%async_computation.3 | async-start | bytes 524288 | tf_op jit(solution)/shard_map/all_to_all | solution.py:469
  127.5 4.8 %project.1 = bf16[512,1024]{1,0:T(8,128)(2,1)} custom-call(bf16[512,1024]{1,0:T(8,128)(2,1)} %get-tuple-element.87.refs_0_, bf16[1024,1024]{1,0:T(8,128)(2,1)} %refs_1_.1), custom_call_target="tpu_custom_call" | custom-call | flops 1 | bytes 1 | tf_op jit(solution)/shard_map/project/pallas_call | solution.py:426
  132.3 2.4 %all-to-all-done.3 = bf16[8,128,128]{2,1,0:T(8,128)(2,1)S(1)} async-done(((bf16[8,128,128]{2,1,0:T(8,128)(2,1)}), bf16[8,128,128]{2,1,0:T(8,128)(2,1)S(1)}, u32[]{:S(2)}, u32[]{:S(2)}) %all-to-all-start.3) | async-done | bytes 262176 | tf_op jit(solution)/shard_map/all_to_all | solution.py:469
  134.7 0.0 collective-permute-done.9.refs_1_
  134.7 0.0 collective-permute-done.10.refs_2_
  134.8 0.7 collective-permute-start.13
  135.6 4.7 %collective-permute-start.12 = (bf16[64,128]{1,0:T(8,128)(2,1)S(1)}, bf16[64,128]{1,0:T(8,128)(2,1)S(1)}, u32[]{:S(2)}, u32[]{:S(2)}) collective-permute-start(bf16[64,128]{1,0:T(8,128)(2,1)S(1)} %pad_maximum_fusion.4), channel_id=1, source_target_pairs={{128,0},{136,8},{144,16},{152,24},{160,32},{168,40},{176,48},{184,... | collective-permute-start | bytes 49160 | tf_op jit(solution)/shard_map/ppermute | solution.py:571
  140.2 0.0 collective-permute-start.11
  140.2 0.0 collective-permute-done.13
  140.3 1.9 %collective-permute-done.12 = bf16[64,128]{1,0:T(8,128)(2,1)S(1)} collective-permute-done((bf16[64,128]{1,0:T(8,128)(2,1)S(1)}, bf16[64,128]{1,0:T(8,128)(2,1)S(1)}, u32[]{:S(2)}, u32[]{:S(2)}) %collective-permute-start.12) | collective-permute-done | bytes 16416 | tf_op jit(solution)/shard_map/ppermute | solution.py:571
  142.2 3.0 %collective-permute-done.11 = bf16[64,128]{1,0:T(8,128)(2,1)S(1)} collective-permute-done((bf16[64,128]{1,0:T(8,128)(2,1)S(1)}, bf16[64,128]{1,0:T(8,128)(2,1)S(1)}, u32[]{:S(2)}, u32[]{:S(2)}) %collective-permute-start.11) | collective-permute-done | bytes 16416 | tf_op jit(solution)/shard_map/ppermute | solution.py:571
  145.2 0.6 broadcast_in_dim.49
  145.8 8.6 %all-to-all-start.4 = ((bf16[8,32,128]{2,1,0:T(8,128)(2,1)}), bf16[8,32,128]{2,1,0:T(8,128)(2,1)S(1)}, u32[]{:S(2)}, u32[]{:S(2)}) async-start(bf16[8,32,128]{2,1,0:T(8,128)(2,1)} %broadcast_in_dim.49), calls=%async_computation.4 | async-start | bytes 131072 | tf_op jit(solution)/shard_map/all_to_all | solution.py:469
  154.4 0.6 slice.42
  155.0 4.6 %finish.1 = (bf16[512,1024]{1,0:T(8,128)(2,1)}, bf16[512,1024]{1,0:T(8,128)(2,1)}) custom-call(f32[2,512,1024]{2,1,0:T(8,128)} %get-tuple-element.88.refs_0_, bf16[2,256,1024]{2,1,0:T(8,128)(2,1)} %copy-done.7, bf16[2,256,1024]{2,1,0:T(8,128)(2,1)} %collective-permute-done.10.refs_2_, bf16[8,640,128]{2,1,0:T(8,128)(2,1)} %copy-done.1, f32[8,4,128]{2,1,0:T(4,128)} %bitcast.80), custom_call_target="tpu_custom_call" | custom-call | flops 1 | bytes 1 | tf_op jit(solution)/shard_map/finish/pallas_call | solution.py:454
  159.6 0.0 all-to-all-done.4
  159.7 0.7 copy_bitcast_fusion
  (36 shorter events, 0.3 us)
Async XLA Ops:
  4.2 5.5 %copy-start.8 = (bf16[16,1024]{1,0:T(8,128)(2,1)S(1)}, bf16[16,1024]{1,0:T(8,128)(2,1)}, u32[]{:S(2)}) copy-start(bf16[16,1024]{1,0:T(8,128)(2,1)} %get-tuple-element.51) | copy-start | bytes 98308
  4.2 22.5 %all-to-all-start = ((bf16[8,64,1024]{2,1,0:T(8,128)(2,1)}), bf16[8,64,1024]{2,1,0:T(8,128)(2,1)S(1)}, u32[]{:S(2)}, u32[]{:S(2)}) async-start(bf16[8,64,1024]{2,1,0:T(8,128)(2,1)} %get-tuple-element.52), calls=%async_computation | async-start | bytes 2097152 | tf_op jit(solution)/shard_map/all_to_all | solution.py:469
  9.7 14.6 %collective-permute-start.2 = (bf16[16,1024]{1,0:T(8,128)(2,1)S(1)}, bf16[16,1024]{1,0:T(8,128)(2,1)S(1)}, u32[]{:S(2)}, u32[]{:S(2)}) collective-permute-start(bf16[16,1024]{1,0:T(8,128)(2,1)S(1)} %copy-done.8), channel_id=1, source_target_pairs={{0,192},{8,200},{16,208},{24,216},{32,224},{40,232},{48,240},{56,2... | collective-permute-start | bytes 98312 | tf_op jit(solution)/shard_map/ppermute | solution.py:514
  9.8 16.8 %collective-permute-start.1 = (bf16[16,1024]{1,0:T(8,128)(2,1)S(1)}, bf16[16,1024]{1,0:T(8,128)(2,1)S(1)}, u32[]{:S(2)}, u32[]{:S(2)}) collective-permute-start(bf16[16,1024]{1,0:T(8,128)(2,1)S(1)} %copy-done.8), channel_id=1, source_target_pairs={{0,128},{8,136},{16,144},{24,152},{32,160},{40,168},{48,176},{56,1... | collective-permute-start | bytes 98312 | tf_op jit(solution)/shard_map/ppermute | solution.py:514
  15.2 11.4 %collective-permute-start = (bf16[16,1024]{1,0:T(8,128)(2,1)S(1)}, bf16[16,1024]{1,0:T(8,128)(2,1)S(1)}, u32[]{:S(2)}, u32[]{:S(2)}) collective-permute-start(bf16[16,1024]{1,0:T(8,128)(2,1)S(1)} %copy-done.8), channel_id=1, source_target_pairs={{0,64},{8,72},{16,80},{24,88},{32,96},{40,104},{48,112},{56,120},{... | collective-permute-start | bytes 98312 | tf_op jit(solution)/shard_map/ppermute | solution.py:514
  26.7 28.1 %copy-start = (bf16[8,64,1024]{2,1,0:T(8,128)(2,1)}, bf16[8,64,1024]{2,1,0:T(8,128)(2,1)S(1)}, u32[]{:S(2)}) copy-start(bf16[8,64,1024]{2,1,0:T(8,128)(2,1)S(1)} %all-to-all-done.refs_2_.refs_6_) | copy-start | bytes 3145732
  27.5 12.4 %all-to-all-start.1 = ((bf16[8,16,1024]{2,1,0:T(8,128)(2,1)}), bf16[8,16,1024]{2,1,0:T(8,128)(2,1)S(1)}, u32[]{:S(2)}, u32[]{:S(2)}) async-start(bf16[8,16,1024]{2,1,0:T(8,128)(2,1)} %broadcast_in_dim.44), calls=%async_computation.1 | async-start | bytes 524288 | tf_op jit(solution)/shard_map/all_to_all | solution.py:469
  39.9 14.9 %copy-start.4 = (bf16[8,16,1024]{2,1,0:T(8,128)(2,1)}, bf16[8,16,1024]{2,1,0:T(8,128)(2,1)S(1)}, u32[]{:S(2)}) copy-start(bf16[8,16,1024]{2,1,0:T(8,128)(2,1)S(1)} %all-to-all-done.1.refs_3_.refs_7_) | copy-start | bytes 786436
  39.9 25.3 %collective-permute-start.3 = (bf16[2,256,1024]{2,1,0:T(8,128)(2,1)}, bf16[2,256,1024]{2,1,0:T(8,128)(2,1)S(1)}, u32[]{:S(2)}, u32[]{:S(2)}) collective-permute-start(bf16[2,256,1024]{2,1,0:T(8,128)(2,1)} %get-tuple-element.56), channel_id=1, source_target_pairs={{0,8},{8,16},{16,24},{24,32},{32,40},{40,48},{48,56},{56,64},{64,7... | collective-permute-start | bytes 3145736 | tf_op jit(solution)/shard_map/ppermute | solution.py:524
  41.8 24.4 %collective-permute-start.4 = (bf16[2,256,1024]{2,1,0:T(8,128)(2,1)}, bf16[2,256,1024]{2,1,0:T(8,128)(2,1)S(1)}, u32[]{:S(2)}, u32[]{:S(2)}) collective-permute-start(bf16[2,256,1024]{2,1,0:T(8,128)(2,1)} %get-tuple-element.58), channel_id=1, source_target_pairs={{8,0},{16,8},{24,16},{32,24},{40,32},{48,40},{56,48},{64,56},{72,6... | collective-permute-start | bytes 3145736 | tf_op jit(solution)/shard_map/ppermute | solution.py:525
  48.3 3.0 %copy-start.5 = (bf16[1024,1024]{1,0:T(8,128)(2,1)S(1)}, bf16[1024,1024]{1,0:T(8,128)(2,1)}, u32[]{:S(2)}) copy-start(bf16[1024,1024]{1,0:T(8,128)(2,1)} %refs_1_.1) | copy-start | bytes 6291460
  65.2 1.0 copy-start.2
  66.2 1.0 copy-start.3
  78.0 20.9 %all-to-all-start.2 = ((bf16[8,640,128]{2,1,0:T(8,128)(2,1)}), bf16[8,640,128]{2,1,0:T(8,128)(2,1)S(1)}, u32[]{:S(2)}, u32[]{:S(2)}) async-start(bf16[8,640,128]{2,1,0:T(8,128)(2,1)} %bitcast.73), calls=%async_computation.2 | async-start | bytes 2621440 | tf_op jit(solution)/shard_map/all_to_all | solution.py:469
  86.6 12.3 %collective-permute-start.5 = (bf16[4,1024,128]{2,1,0:T(8,128)(2,1)}, bf16[4,1024,128]{2,1,0:T(8,128)(2,1)S(1)}, u32[]{:S(2)}, u32[]{:S(2)}) collective-permute-start(bf16[4,1024,128]{2,1,0:T(8,128)(2,1)} %get-tuple-element.70), channel_id=1, source_target_pairs={{0,1},{1,0},{2,3},{3,2},{4,5},{5,4},{6,7},{7,6},{8,9},{9,8},{10,11... | collective-permute-start | bytes 3145736 | tf_op jit(solution)/shard_map/ppermute | solution.py:538
  92.0 7.0 %copy-start.6 = (bf16[4,1024,128]{2,1,0:T(8,128)(2,1)S(1)}, bf16[4,1024,128]{2,1,0:T(8,128)(2,1)}, u32[]{:S(2)}) copy-start(bf16[4,1024,128]{2,1,0:T(8,128)(2,1)} %get-tuple-element.69) | copy-start | bytes 3145732
  98.9 28.5 %copy-start.1 = (bf16[8,640,128]{2,1,0:T(8,128)(2,1)}, bf16[8,640,128]{2,1,0:T(8,128)(2,1)S(1)}, u32[]{:S(2)}) copy-start(bf16[8,640,128]{2,1,0:T(8,128)(2,1)S(1)} %all-to-all-done.2.refs_3_) | copy-start | bytes 3932164
  99.2 35.5 %collective-permute-start.9 = (bf16[2,256,1024]{2,1,0:T(8,128)(2,1)}, bf16[2,256,1024]{2,1,0:T(8,128)(2,1)S(1)}, u32[]{:S(2)}, u32[]{:S(2)}) collective-permute-start(bf16[2,256,1024]{2,1,0:T(8,128)(2,1)} %get-tuple-element.89), channel_id=1, source_target_pairs={{0,8},{8,16},{16,24},{24,32},{32,40},{40,48},{48,56},{56,64},{64,7... | collective-permute-start | bytes 3145736 | tf_op jit(solution)/shard_map/ppermute | solution.py:554
  102.9 31.9 %collective-permute-start.10 = (bf16[2,256,1024]{2,1,0:T(8,128)(2,1)}, bf16[2,256,1024]{2,1,0:T(8,128)(2,1)}, u32[]{:S(2)}, u32[]{:S(2)}) collective-permute-start(bf16[2,256,1024]{2,1,0:T(8,128)(2,1)} %get-tuple-element.81), channel_id=1, source_target_pairs={{8,0},{16,8},{24,16},{32,24},{40,32},{48,40},{56,48},{64,56},{72,6... | collective-permute-start | bytes 3145736 | tf_op jit(solution)/shard_map/ppermute | solution.py:553
  107.3 12.7 %collective-permute-start.6 = (bf16[1024,128]{1,0:T(8,128)(2,1)S(1)}, bf16[1024,128]{1,0:T(8,128)(2,1)S(1)}, u32[]{:S(2)}, u32[]{:S(2)}) collective-permute-start(bf16[1024,128]{1,0:T(8,128)(2,1)S(1)} %get-tuple-element.95), channel_id=1, source_target_pairs={{0,2},{1,3},{2,4},{3,5},{4,6},{5,7},{6,0},{7,1},{8,10},{9,11},{10,... | collective-permute-start | bytes 786440 | tf_op jit(solution)/shard_map/ppermute | solution.py:548
  108.7 11.3 %collective-permute-start.7 = (bf16[1024,128]{1,0:T(8,128)(2,1)S(1)}, bf16[1024,128]{1,0:T(8,128)(2,1)S(1)}, u32[]{:S(2)}, u32[]{:S(2)}) collective-permute-start(bf16[1024,128]{1,0:T(8,128)(2,1)S(1)} %get-tuple-element.94), channel_id=1, source_target_pairs={{0,4},{1,5},{2,6},{3,7},{4,0},{5,1},{6,2},{7,3},{8,12},{9,13},{10,... | collective-permute-start | bytes 786440 | tf_op jit(solution)/shard_map/ppermute | solution.py:548
  109.7 13.4 %collective-permute-start.8 = (bf16[1024,128]{1,0:T(8,128)(2,1)S(1)}, bf16[1024,128]{1,0:T(8,128)(2,1)S(1)}, u32[]{:S(2)}, u32[]{:S(2)}) collective-permute-start(bf16[1024,128]{1,0:T(8,128)(2,1)S(1)} %get-tuple-element.93), channel_id=1, source_target_pairs={{0,6},{1,7},{2,0},{3,1},{4,2},{5,3},{6,4},{7,5},{8,14},{9,15},{10,... | collective-permute-start | bytes 786440 | tf_op jit(solution)/shard_map/ppermute | solution.py:548
  123.9 10.8 %all-to-all-start.3 = ((bf16[8,128,128]{2,1,0:T(8,128)(2,1)}), bf16[8,128,128]{2,1,0:T(8,128)(2,1)S(1)}, u32[]{:S(2)}, u32[]{:S(2)}) async-start(bf16[8,128,128]{2,1,0:T(8,128)(2,1)} %bitcast.19), calls=%async_computation.3 | async-start | bytes 524288 | tf_op jit(solution)/shard_map/all_to_all | solution.py:469
  134.7 20.3 %copy-start.7 = (bf16[2,256,1024]{2,1,0:T(8,128)(2,1)}, bf16[2,256,1024]{2,1,0:T(8,128)(2,1)S(1)}, u32[]{:S(2)}) copy-start(bf16[2,256,1024]{2,1,0:T(8,128)(2,1)S(1)} %collective-permute-done.9.refs_1_) | copy-start | bytes 3145732
  134.8 5.4 %collective-permute-start.13 = (bf16[64,128]{1,0:T(8,128)(2,1)S(1)}, bf16[64,128]{1,0:T(8,128)(2,1)S(1)}, u32[]{:S(2)}, u32[]{:S(2)}) collective-permute-start(bf16[64,128]{1,0:T(8,128)(2,1)S(1)} %pad_maximum_fusion.5), channel_id=1, source_target_pairs={{192,0},{200,8},{208,16},{216,24},{224,32},{232,40},{240,48},{248,... | collective-permute-start | bytes 49160 | tf_op jit(solution)/shard_map/ppermute | solution.py:571
  135.6 6.6 %collective-permute-start.12 = (bf16[64,128]{1,0:T(8,128)(2,1)S(1)}, bf16[64,128]{1,0:T(8,128)(2,1)S(1)}, u32[]{:S(2)}, u32[]{:S(2)}) collective-permute-start(bf16[64,128]{1,0:T(8,128)(2,1)S(1)} %pad_maximum_fusion.4), channel_id=1, source_target_pairs={{128,0},{136,8},{144,16},{152,24},{160,32},{168,40},{176,48},{184,... | collective-permute-start | bytes 49160 | tf_op jit(solution)/shard_map/ppermute | solution.py:571
  140.2 4.9 %collective-permute-start.11 = (bf16[64,128]{1,0:T(8,128)(2,1)S(1)}, bf16[64,128]{1,0:T(8,128)(2,1)S(1)}, u32[]{:S(2)}, u32[]{:S(2)}) collective-permute-start(bf16[64,128]{1,0:T(8,128)(2,1)S(1)} %pad_maximum_fusion.3), channel_id=1, source_target_pairs={{64,0},{72,8},{80,16},{88,24},{96,32},{104,40},{112,48},{120,56},{... | collective-permute-start | bytes 49160 | tf_op jit(solution)/shard_map/ppermute | solution.py:571
  145.8 13.8 %all-to-all-start.4 = ((bf16[8,32,128]{2,1,0:T(8,128)(2,1)}), bf16[8,32,128]{2,1,0:T(8,128)(2,1)S(1)}, u32[]{:S(2)}, u32[]{:S(2)}) async-start(bf16[8,32,128]{2,1,0:T(8,128)(2,1)} %broadcast_in_dim.49), calls=%async_computation.4 | async-start | bytes 131072 | tf_op jit(solution)/shard_map/all_to_all | solution.py:469
